TPU v7x, 128 devices: a whole 4x4x4 slice. The times are simulated.
128 devices in a mesh: sweep: 8 (over z, core), layer: 16 (over x, y).
Axes of the slice: x: 4, y: 4, z: 4, core: 2. Of those that a mesh axis runs over, the one named last changes fastest.
Arguments:
- green: bfloat16 [8, 2, 8192, 8192], P('sweep', None, 'layer'), may hold values from -1 to 1
- down_source: float32 [8, 2, 16, 8192], P('sweep', None, None, 'layer'), may hold values from -6 to 6
- up_source: float32 [8, 2, 16, 8192], P('sweep', None, None, 'layer'), may hold values from -6 to 6
Outputs:
- total: float32 [8, 2, 16, 8192], P('sweep', None, None, 'layer')
All inputs are finite; a program needn't handle non-finite values.
Results may differ from a plain program's by a relative error of at most 0.02.
Values may be sent and summed in bfloat16 or wider, within the bound.
No kernel may reach another device: no remote copies, remote signals or barrier semaphores. Data moves between devices by JAX's collectives and lax.ppermute only.
A program may use at most 64 MiB of HBM per device.

v0:
```python
import jax
import jax.numpy as jnp
from jax import lax
from jax.sharding import PartitionSpec as P


def in_order(blocks, dim):
    blocks = jnp.moveaxis(blocks, 0, dim)
    shape = blocks.shape
    return blocks.reshape(*shape[:dim], shape[dim] * shape[dim + 1], *shape[dim + 2 :])


def sent_to_all(shard, axis):
    copies = jnp.broadcast_to(shard, (lax.axis_size(axis), *shard.shape))
    return lax.all_to_all(copies, axis, split_axis=0, concat_axis=0, tiled=True)


def gather_directly(shard, axis, dim):
    return in_order(sent_to_all(shard, axis), dim)


def from_behind(shard, axis, by):
    size = lax.axis_size(axis)
    pairs = [(i, i + by) for i in range(size) if 0 <= i + by < size]
    return lax.ppermute(shard, axis, pairs)


def split_up(shard, dim, size):
    shape = shard.shape
    blocks = shard.reshape(*shape[:dim], size, shape[dim] // size, *shape[dim + 1 :])
    return jnp.moveaxis(blocks, dim, 0)


def summed_on_arrival(shard, axis, dim):
    size = lax.axis_size(axis)
    blocks = lax.all_to_all(split_up(shard, dim, size), axis, 0, 0, tiled=True)
    return jnp.sum(blocks.astype(jnp.float32), axis=0)


def rows_product(trace_in, matrix):
    contract = (((1,), (1,)), ((), ()))
    real_real = lax.dot_general(
        trace_in[0], matrix[0], contract, preferred_element_type=jnp.float32
    )
    imag_imag = lax.dot_general(
        trace_in[1], matrix[1], contract, preferred_element_type=jnp.float32
    )
    real_imag = lax.dot_general(
        trace_in[0], matrix[1], contract, preferred_element_type=jnp.float32
    )
    imag_real = lax.dot_general(
        trace_in[1], matrix[0], contract, preferred_element_type=jnp.float32
    )
    return jnp.stack([real_real - imag_imag, real_imag + imag_real])


def cols_product(trace_in, matrix):
    real_real = jnp.dot(trace_in[0], matrix[0], preferred_element_type=jnp.float32)
    imag_imag = jnp.dot(trace_in[1], matrix[1], preferred_element_type=jnp.float32)
    real_imag = jnp.dot(trace_in[0], matrix[1], preferred_element_type=jnp.float32)
    imag_real = jnp.dot(trace_in[1], matrix[0], preferred_element_type=jnp.float32)
    return jnp.stack([real_real - imag_imag, real_imag + imag_real])


def run_chain(own_term, product, passing, forward, blocks):
    count = lax.axis_size("sweep")
    my_index = lax.axis_index("sweep")
    position = my_index if forward else count - 1 - my_index
    width = own_term.shape[1] // blocks

    def turn(counter, state):
        result, incoming = state
        block_index = counter - position
        active = (block_index >= 0) & (block_index < blocks)
        update = own_term + product(incoming)
        previous = result
        result = jnp.where(active, update, previous)
        return (result, passing(update.astype(jnp.bfloat16)))

    start_state = (jnp.zeros_like(own_term), jnp.zeros((2, width, own_term.shape[2]), jnp.bfloat16))
    result, _unused = lax.fori_loop(0, count + blocks - 1, turn, start_state)
    return result


def local(green, down_source, up_source):
    matrix = green[0]
    blocks = 1

    def down_product(incoming):
        return rows_product(gather_directly(incoming, "layer", 2), matrix)

    def pass_down(outgoing):
        return from_behind(outgoing, "sweep", 1)

    downward = run_chain(down_source[0], down_product, pass_down, True, blocks)

    def up_product(incoming):
        return summed_on_arrival(cols_product(incoming, matrix).astype(jnp.bfloat16), "layer", 2)

    def pass_up(outgoing):
        return from_behind(outgoing, "sweep", -1)

    total = run_chain(up_source[0] + downward, up_product, pass_up, False, blocks)
    return total[None]


def solution(mesh):
    in_specs = (
        P("sweep", None, "layer", None),
        P("sweep", None, None, "layer"),
        P("sweep", None, None, "layer"),
    )
    out_specs = P("sweep", None, None, "layer")
    return jax.shard_map(local, mesh=mesh, in_specs=in_specs, out_specs=out_specs, check_vma=False)
```

profile of v0, /device:TPU:1, one launch (start us, length us, event | category | flops | bytes accessed | tf_op | source)
XLA Modules:
  0.0 571.4 jit_solution(1278927016619222354)
XLA Ops:
  0.0 302.1 %while.32 = (s32[]{:T(128)}, f32[2,16,512]{2,1,0:T(8,128)S(1)}, bf16[2,16,512]{2,1,0:T(8,128)(2,1)S(1)}, s32[]{:T(128)}, bf16[2,512,8192]{2,1,0:T(8,128)(2,1)}, /*index=5*/f32[2,16,512]{2,1,0:T(8,128)}, s32[]{:T(128)}, s32[]{:T(128)}) while((s32[]{:T(128)}, f32[2,16,512]{2,1,0:T(8,128)S(1)}, bf16[2,16,512]{2,1,0:T(8,128)(2,1)S(1)}, ...), condition=%wide.region_1.2_spmd.clone, body=%wide.region_0.1_spmd.clone.sunk | while | flops 536969216 | bytes 106823920 | solution.py:81
  0.9 7.6 %all-to-all-start = ((bf16[16,2,16,512]{3,2,1,0:T(8,128)(2,1)}), bf16[16,2,16,512]{3,2,1,0:T(8,128)(2,1)S(1)}, u32[]{:S(2)}, u32[]{:S(2)}) async-start(bf16[16,2,16,512]{3,2,1,0:T(8,128)(2,1)} %broadcast_in_dim.13), calls=%async_computation | async-start | bytes 1048576 | tf_op jit(solution)/shard_map/while/body/eval_jaxpr/all_to_all | solution.py:15
  8.5 10.3 %all-to-all-done = bf16[16,2,16,512]{3,2,1,0:T(8,128)(2,1)S(1)} async-done(((bf16[16,2,16,512]{3,2,1,0:T(8,128)(2,1)}), bf16[16,2,16,512]{3,2,1,0:T(8,128)(2,1)S(1)}, u32[]{:S(2)}, u32[]{:S(2)}) %all-to-all-start) | async-done | bytes 524320 | tf_op jit(solution)/shard_map/while/body/eval_jaxpr/all_to_all | solution.py:15
  24.7 6.5 %fusion.85 = f32[16,512]{1,0:T(8,128)S(1)} fusion(bf16[16,8192]{1,0:T(8,128)(2,1)S(1)} %bitcast.127, bf16[2,512,8192]{2,1,0:T(8,128)(2,1)} %get-tuple-element.403), kind=kOutput, calls=%fused_computation.clone.1 | convolution fusion | flops 134217728 | bytes 8683520 | tf_op jit(solution)/shard_map/while/body/eval_jaxpr/dot_general | solution.py:48
  46.8 9.9 %all-to-all-done = bf16[16,2,16,512]{3,2,1,0:T(8,128)(2,1)S(1)} async-done(((bf16[16,2,16,512]{3,2,1,0:T(8,128)(2,1)}), bf16[16,2,16,512]{3,2,1,0:T(8,128)(2,1)S(1)}, u32[]{:S(2)}, u32[]{:S(2)}) %all-to-all-start) | async-done | bytes 524320 | tf_op jit(solution)/shard_map/while/body/eval_jaxpr/all_to_all | solution.py:15
  62.6 6.5 %fusion.85 = f32[16,512]{1,0:T(8,128)S(1)} fusion(bf16[16,8192]{1,0:T(8,128)(2,1)S(1)} %bitcast.127, bf16[2,512,8192]{2,1,0:T(8,128)(2,1)} %get-tuple-element.403), kind=kOutput, calls=%fused_computation.clone.1 | convolution fusion | flops 134217728 | bytes 8683520 | tf_op jit(solution)/shard_map/while/body/eval_jaxpr/dot_general | solution.py:48
  85.1 8.9 %all-to-all-done = bf16[16,2,16,512]{3,2,1,0:T(8,128)(2,1)S(1)} async-done(((bf16[16,2,16,512]{3,2,1,0:T(8,128)(2,1)}), bf16[16,2,16,512]{3,2,1,0:T(8,128)(2,1)S(1)}, u32[]{:S(2)}, u32[]{:S(2)}) %all-to-all-start) | async-done | bytes 524320 | tf_op jit(solution)/shard_map/while/body/eval_jaxpr/all_to_all | solution.py:15
  99.9 6.5 %fusion.85 = f32[16,512]{1,0:T(8,128)S(1)} fusion(bf16[16,8192]{1,0:T(8,128)(2,1)S(1)} %bitcast.127, bf16[2,512,8192]{2,1,0:T(8,128)(2,1)} %get-tuple-element.403), kind=kOutput, calls=%fused_computation.clone.1 | convolution fusion | flops 134217728 | bytes 8683520 | tf_op jit(solution)/shard_map/while/body/eval_jaxpr/dot_general | solution.py:48
  110.9 6.6 %collective-permute-start = (bf16[2,16,512]{2,1,0:T(8,128)(2,1)S(1)}, bf16[2,16,512]{2,1,0:T(8,128)(2,1)S(1)}, u32[]{:S(2)}, u32[]{:S(2)}) collective-permute-start(bf16[2,16,512]{2,1,0:T(8,128)(2,1)S(1)} %get-tuple-element.374), channel_id=1, source_target_pairs={{0,16},{16,32},{32,48},{48,64},{64,80},{80,96},{96,112},{1,17},{17... | collective-permute-start | bytes 98312 | tf_op jit(solution)/shard_map/while/body/eval_jaxpr/ppermute | solution.py:25
  123.0 8.9 %all-to-all-done = bf16[16,2,16,512]{3,2,1,0:T(8,128)(2,1)S(1)} async-done(((bf16[16,2,16,512]{3,2,1,0:T(8,128)(2,1)}), bf16[16,2,16,512]{3,2,1,0:T(8,128)(2,1)S(1)}, u32[]{:S(2)}, u32[]{:S(2)}) %all-to-all-start) | async-done | bytes 524320 | tf_op jit(solution)/shard_map/while/body/eval_jaxpr/all_to_all | solution.py:15
  137.8 6.5 %fusion.85 = f32[16,512]{1,0:T(8,128)S(1)} fusion(bf16[16,8192]{1,0:T(8,128)(2,1)S(1)} %bitcast.127, bf16[2,512,8192]{2,1,0:T(8,128)(2,1)} %get-tuple-element.403), kind=kOutput, calls=%fused_computation.clone.1 | convolution fusion | flops 134217728 | bytes 8683520 | tf_op jit(solution)/shard_map/while/body/eval_jaxpr/dot_general | solution.py:48
  159.7 9.0 %all-to-all-done = bf16[16,2,16,512]{3,2,1,0:T(8,128)(2,1)S(1)} async-done(((bf16[16,2,16,512]{3,2,1,0:T(8,128)(2,1)}), bf16[16,2,16,512]{3,2,1,0:T(8,128)(2,1)S(1)}, u32[]{:S(2)}, u32[]{:S(2)}) %all-to-all-start) | async-done | bytes 524320 | tf_op jit(solution)/shard_map/while/body/eval_jaxpr/all_to_all | solution.py:15
  196.4 9.2 %all-to-all-done = bf16[16,2,16,512]{3,2,1,0:T(8,128)(2,1)S(1)} async-done(((bf16[16,2,16,512]{3,2,1,0:T(8,128)(2,1)}), bf16[16,2,16,512]{3,2,1,0:T(8,128)(2,1)S(1)}, u32[]{:S(2)}, u32[]{:S(2)}) %all-to-all-start) | async-done | bytes 524320 | tf_op jit(solution)/shard_map/while/body/eval_jaxpr/all_to_all | solution.py:15
  233.1 9.3 %all-to-all-done = bf16[16,2,16,512]{3,2,1,0:T(8,128)(2,1)S(1)} async-done(((bf16[16,2,16,512]{3,2,1,0:T(8,128)(2,1)}), bf16[16,2,16,512]{3,2,1,0:T(8,128)(2,1)S(1)}, u32[]{:S(2)}, u32[]{:S(2)}) %all-to-all-start) | async-done | bytes 524320 | tf_op jit(solution)/shard_map/while/body/eval_jaxpr/all_to_all | solution.py:15
  269.8 9.5 %all-to-all-done = bf16[16,2,16,512]{3,2,1,0:T(8,128)(2,1)S(1)} async-done(((bf16[16,2,16,512]{3,2,1,0:T(8,128)(2,1)}), bf16[16,2,16,512]{3,2,1,0:T(8,128)(2,1)S(1)}, u32[]{:S(2)}, u32[]{:S(2)}) %all-to-all-start) | async-done | bytes 524320 | tf_op jit(solution)/shard_map/while/body/eval_jaxpr/all_to_all | solution.py:15
  302.2 268.6 %while.33 = (s32[]{:T(128)}, f32[2,16,512]{2,1,0:T(8,128)S(1)}, bf16[2,16,512]{2,1,0:T(8,128)(2,1)S(1)}, s32[]{:T(128)}, bf16[2,512,8192]{2,1,0:T(8,128)(2,1)}, ...) while((s32[]{:T(128)}, f32[2,16,512]{2,1,0:T(8,128)S(1)}, bf16[2,16,512]{2,1,0:T(8,128)(2,1)S(1)}, ...), condition=%wide.region_4.5_spmd.clone, body=%wide.region_2.4_spmd.clone.sunk | while | flops 538230784 | bytes 109084896 | solution.py:81
  320.2 9.6 %all-to-all-done.1 = bf16[16,2,16,512]{3,2,1,0:T(8,128)(2,1)S(1)} async-done(((bf16[16,2,16,512]{3,2,1,0:T(8,128)(2,1)}), bf16[16,2,16,512]{3,2,1,0:T(8,128)(2,1)S(1)}, u32[]{:S(2)}, u32[]{:S(2)}) %all-to-all-start.1) | async-done | bytes 524320 | tf_op jit(solution)/shard_map/while/body/eval_jaxpr/all_to_all | solution.py:36
  354.1 9.1 %all-to-all-done.1 = bf16[16,2,16,512]{3,2,1,0:T(8,128)(2,1)S(1)} async-done(((bf16[16,2,16,512]{3,2,1,0:T(8,128)(2,1)}), bf16[16,2,16,512]{3,2,1,0:T(8,128)(2,1)S(1)}, u32[]{:S(2)}, u32[]{:S(2)}) %all-to-all-start.1) | async-done | bytes 524320 | tf_op jit(solution)/shard_map/while/body/eval_jaxpr/all_to_all | solution.py:36
  388.0 8.9 %all-to-all-done.1 = bf16[16,2,16,512]{3,2,1,0:T(8,128)(2,1)S(1)} async-done(((bf16[16,2,16,512]{3,2,1,0:T(8,128)(2,1)}), bf16[16,2,16,512]{3,2,1,0:T(8,128)(2,1)S(1)}, u32[]{:S(2)}, u32[]{:S(2)}) %all-to-all-start.1) | async-done | bytes 524320 | tf_op jit(solution)/shard_map/while/body/eval_jaxpr/all_to_all | solution.py:36
  422.3 8.9 %all-to-all-done.1 = bf16[16,2,16,512]{3,2,1,0:T(8,128)(2,1)S(1)} async-done(((bf16[16,2,16,512]{3,2,1,0:T(8,128)(2,1)}), bf16[16,2,16,512]{3,2,1,0:T(8,128)(2,1)S(1)}, u32[]{:S(2)}, u32[]{:S(2)}) %all-to-all-start.1) | async-done | bytes 524320 | tf_op jit(solution)/shard_map/while/body/eval_jaxpr/all_to_all | solution.py:36
  455.8 8.9 %all-to-all-done.1 = bf16[16,2,16,512]{3,2,1,0:T(8,128)(2,1)S(1)} async-done(((bf16[16,2,16,512]{3,2,1,0:T(8,128)(2,1)}), bf16[16,2,16,512]{3,2,1,0:T(8,128)(2,1)S(1)}, u32[]{:S(2)}, u32[]{:S(2)}) %all-to-all-start.1) | async-done | bytes 524320 | tf_op jit(solution)/shard_map/while/body/eval_jaxpr/all_to_all | solution.py:36
  489.0 9.0 %all-to-all-done.1 = bf16[16,2,16,512]{3,2,1,0:T(8,128)(2,1)S(1)} async-done(((bf16[16,2,16,512]{3,2,1,0:T(8,128)(2,1)}), bf16[16,2,16,512]{3,2,1,0:T(8,128)(2,1)S(1)}, u32[]{:S(2)}, u32[]{:S(2)}) %all-to-all-start.1) | async-done | bytes 524320 | tf_op jit(solution)/shard_map/while/body/eval_jaxpr/all_to_all | solution.py:36
  522.1 9.2 %all-to-all-done.1 = bf16[16,2,16,512]{3,2,1,0:T(8,128)(2,1)S(1)} async-done(((bf16[16,2,16,512]{3,2,1,0:T(8,128)(2,1)}), bf16[16,2,16,512]{3,2,1,0:T(8,128)(2,1)S(1)}, u32[]{:S(2)}, u32[]{:S(2)}) %all-to-all-start.1) | async-done | bytes 524320 | tf_op jit(solution)/shard_map/while/body/eval_jaxpr/all_to_all | solution.py:36
  555.4 9.2 %all-to-all-done.1 = bf16[16,2,16,512]{3,2,1,0:T(8,128)(2,1)S(1)} async-done(((bf16[16,2,16,512]{3,2,1,0:T(8,128)(2,1)}), bf16[16,2,16,512]{3,2,1,0:T(8,128)(2,1)S(1)}, u32[]{:S(2)}, u32[]{:S(2)}) %all-to-all-start.1) | async-done | bytes 524320 | tf_op jit(solution)/shard_map/while/body/eval_jaxpr/all_to_all | solution.py:36
  (259 shorter events, 382.1 us)
Async XLA Ops:
  0.9 17.9 %all-to-all-start = ((bf16[16,2,16,512]{3,2,1,0:T(8,128)(2,1)}), bf16[16,2,16,512]{3,2,1,0:T(8,128)(2,1)S(1)}, u32[]{:S(2)}, u32[]{:S(2)}) async-start(bf16[16,2,16,512]{3,2,1,0:T(8,128)(2,1)} %broadcast_in_dim.13), calls=%async_computation | async-start | bytes 1048576 | tf_op jit(solution)/shard_map/while/body/eval_jaxpr/all_to_all | solution.py:15
  35.8 6.6 %collective-permute-start = (bf16[2,16,512]{2,1,0:T(8,128)(2,1)S(1)}, bf16[2,16,512]{2,1,0:T(8,128)(2,1)S(1)}, u32[]{:S(2)}, u32[]{:S(2)}) collective-permute-start(bf16[2,16,512]{2,1,0:T(8,128)(2,1)S(1)} %get-tuple-element.374), channel_id=1, source_target_pairs={{0,16},{16,32},{32,48},{48,64},{64,80},{80,96},{96,112},{1,17},{17... | collective-permute-start | bytes 98312 | tf_op jit(solution)/shard_map/while/body/eval_jaxpr/ppermute | solution.py:25
  43.2 13.5 %all-to-all-start = ((bf16[16,2,16,512]{3,2,1,0:T(8,128)(2,1)}), bf16[16,2,16,512]{3,2,1,0:T(8,128)(2,1)S(1)}, u32[]{:S(2)}, u32[]{:S(2)}) async-start(bf16[16,2,16,512]{3,2,1,0:T(8,128)(2,1)} %broadcast_in_dim.13), calls=%async_computation | async-start | bytes 1048576 | tf_op jit(solution)/shard_map/while/body/eval_jaxpr/all_to_all | solution.py:15
  73.6 7.0 %collective-permute-start = (bf16[2,16,512]{2,1,0:T(8,128)(2,1)S(1)}, bf16[2,16,512]{2,1,0:T(8,128)(2,1)S(1)}, u32[]{:S(2)}, u32[]{:S(2)}) collective-permute-start(bf16[2,16,512]{2,1,0:T(8,128)(2,1)S(1)} %get-tuple-element.374), channel_id=1, source_target_pairs={{0,16},{16,32},{32,48},{48,64},{64,80},{80,96},{96,112},{1,17},{17... | collective-permute-start | bytes 98312 | tf_op jit(solution)/shard_map/while/body/eval_jaxpr/ppermute | solution.py:25
  81.5 12.5 %all-to-all-start = ((bf16[16,2,16,512]{3,2,1,0:T(8,128)(2,1)}), bf16[16,2,16,512]{3,2,1,0:T(8,128)(2,1)S(1)}, u32[]{:S(2)}, u32[]{:S(2)}) async-start(bf16[16,2,16,512]{3,2,1,0:T(8,128)(2,1)} %broadcast_in_dim.13), calls=%async_computation | async-start | bytes 1048576 | tf_op jit(solution)/shard_map/while/body/eval_jaxpr/all_to_all | solution.py:15
  110.9 7.6 %collective-permute-start = (bf16[2,16,512]{2,1,0:T(8,128)(2,1)S(1)}, bf16[2,16,512]{2,1,0:T(8,128)(2,1)S(1)}, u32[]{:S(2)}, u32[]{:S(2)}) collective-permute-start(bf16[2,16,512]{2,1,0:T(8,128)(2,1)S(1)} %get-tuple-element.374), channel_id=1, source_target_pairs={{0,16},{16,32},{32,48},{48,64},{64,80},{80,96},{96,112},{1,17},{17... | collective-permute-start | bytes 98312 | tf_op jit(solution)/shard_map/while/body/eval_jaxpr/ppermute | solution.py:25
  119.4 12.5 %all-to-all-start = ((bf16[16,2,16,512]{3,2,1,0:T(8,128)(2,1)}), bf16[16,2,16,512]{3,2,1,0:T(8,128)(2,1)S(1)}, u32[]{:S(2)}, u32[]{:S(2)}) async-start(bf16[16,2,16,512]{3,2,1,0:T(8,128)(2,1)} %broadcast_in_dim.13), calls=%async_computation | async-start | bytes 1048576 | tf_op jit(solution)/shard_map/while/body/eval_jaxpr/all_to_all | solution.py:15
  148.9 6.4 %collective-permute-start = (bf16[2,16,512]{2,1,0:T(8,128)(2,1)S(1)}, bf16[2,16,512]{2,1,0:T(8,128)(2,1)S(1)}, u32[]{:S(2)}, u32[]{:S(2)}) collective-permute-start(bf16[2,16,512]{2,1,0:T(8,128)(2,1)S(1)} %get-tuple-element.374), channel_id=1, source_target_pairs={{0,16},{16,32},{32,48},{48,64},{64,80},{80,96},{96,112},{1,17},{17... | collective-permute-start | bytes 98312 | tf_op jit(solution)/shard_map/while/body/eval_jaxpr/ppermute | solution.py:25
  156.1 12.6 %all-to-all-start = ((bf16[16,2,16,512]{3,2,1,0:T(8,128)(2,1)}), bf16[16,2,16,512]{3,2,1,0:T(8,128)(2,1)S(1)}, u32[]{:S(2)}, u32[]{:S(2)}) async-start(bf16[16,2,16,512]{3,2,1,0:T(8,128)(2,1)} %broadcast_in_dim.13), calls=%async_computation | async-start | bytes 1048576 | tf_op jit(solution)/shard_map/while/body/eval_jaxpr/all_to_all | solution.py:15
  185.8 6.2 %collective-permute-start = (bf16[2,16,512]{2,1,0:T(8,128)(2,1)S(1)}, bf16[2,16,512]{2,1,0:T(8,128)(2,1)S(1)}, u32[]{:S(2)}, u32[]{:S(2)}) collective-permute-start(bf16[2,16,512]{2,1,0:T(8,128)(2,1)S(1)} %get-tuple-element.374), channel_id=1, source_target_pairs={{0,16},{16,32},{32,48},{48,64},{64,80},{80,96},{96,112},{1,17},{17... | collective-permute-start | bytes 98312 | tf_op jit(solution)/shard_map/while/body/eval_jaxpr/ppermute | solution.py:25
  192.8 12.8 %all-to-all-start = ((bf16[16,2,16,512]{3,2,1,0:T(8,128)(2,1)}), bf16[16,2,16,512]{3,2,1,0:T(8,128)(2,1)S(1)}, u32[]{:S(2)}, u32[]{:S(2)}) async-start(bf16[16,2,16,512]{3,2,1,0:T(8,128)(2,1)} %broadcast_in_dim.13), calls=%async_computation | async-start | bytes 1048576 | tf_op jit(solution)/shard_map/while/body/eval_jaxpr/all_to_all | solution.py:15
  229.6 12.9 %all-to-all-start = ((bf16[16,2,16,512]{3,2,1,0:T(8,128)(2,1)}), bf16[16,2,16,512]{3,2,1,0:T(8,128)(2,1)S(1)}, u32[]{:S(2)}, u32[]{:S(2)}) async-start(bf16[16,2,16,512]{3,2,1,0:T(8,128)(2,1)} %broadcast_in_dim.13), calls=%async_computation | async-start | bytes 1048576 | tf_op jit(solution)/shard_map/while/body/eval_jaxpr/all_to_all | solution.py:15
  266.3 13.1 %all-to-all-start = ((bf16[16,2,16,512]{3,2,1,0:T(8,128)(2,1)}), bf16[16,2,16,512]{3,2,1,0:T(8,128)(2,1)S(1)}, u32[]{:S(2)}, u32[]{:S(2)}) async-start(bf16[16,2,16,512]{3,2,1,0:T(8,128)(2,1)} %broadcast_in_dim.13), calls=%async_computation | async-start | bytes 1048576 | tf_op jit(solution)/shard_map/while/body/eval_jaxpr/all_to_all | solution.py:15
  316.7 13.2 %all-to-all-start.1 = ((bf16[16,2,16,512]{3,2,1,0:T(8,128)(2,1)}), bf16[16,2,16,512]{3,2,1,0:T(8,128)(2,1)S(1)}, u32[]{:S(2)}, u32[]{:S(2)}) async-start(bf16[16,2,16,512]{3,2,1,0:T(8,128)(2,1)} %maximum_bitcast_fusion.2), calls=%async_computation.1 | async-start | bytes 1048576 | tf_op jit(solution)/shard_map/while/body/eval_jaxpr/all_to_all | solution.py:36
  350.5 12.7 %all-to-all-start.1 = ((bf16[16,2,16,512]{3,2,1,0:T(8,128)(2,1)}), bf16[16,2,16,512]{3,2,1,0:T(8,128)(2,1)S(1)}, u32[]{:S(2)}, u32[]{:S(2)}) async-start(bf16[16,2,16,512]{3,2,1,0:T(8,128)(2,1)} %maximum_bitcast_fusion.2), calls=%async_computation.1 | async-start | bytes 1048576 | tf_op jit(solution)/shard_map/while/body/eval_jaxpr/all_to_all | solution.py:36
  363.3 6.8 %collective-permute-start.1 = (bf16[2,16,512]{2,1,0:T(8,128)(2,1)S(1)}, bf16[2,16,512]{2,1,0:T(8,128)(2,1)S(1)}, u32[]{:S(2)}, u32[]{:S(2)}) collective-permute-start(bf16[2,16,512]{2,1,0:T(8,128)(2,1)S(1)} %get-tuple-element.382), channel_id=1, source_target_pairs={{16,0},{32,16},{48,32},{64,48},{80,64},{96,80},{112,96},{17,1},{33... | collective-permute-start | bytes 98312 | tf_op jit(solution)/shard_map/while/body/eval_jaxpr/ppermute | solution.py:25
  384.4 12.5 %all-to-all-start.1 = ((bf16[16,2,16,512]{3,2,1,0:T(8,128)(2,1)}), bf16[16,2,16,512]{3,2,1,0:T(8,128)(2,1)S(1)}, u32[]{:S(2)}, u32[]{:S(2)}) async-start(bf16[16,2,16,512]{3,2,1,0:T(8,128)(2,1)} %maximum_bitcast_fusion.2), calls=%async_computation.1 | async-start | bytes 1048576 | tf_op jit(solution)/shard_map/while/body/eval_jaxpr/all_to_all | solution.py:36
  397.0 7.4 %collective-permute-start.1 = (bf16[2,16,512]{2,1,0:T(8,128)(2,1)S(1)}, bf16[2,16,512]{2,1,0:T(8,128)(2,1)S(1)}, u32[]{:S(2)}, u32[]{:S(2)}) collective-permute-start(bf16[2,16,512]{2,1,0:T(8,128)(2,1)S(1)} %get-tuple-element.382), channel_id=1, source_target_pairs={{16,0},{32,16},{48,32},{64,48},{80,64},{96,80},{112,96},{17,1},{33... | collective-permute-start | bytes 98312 | tf_op jit(solution)/shard_map/while/body/eval_jaxpr/ppermute | solution.py:25
  418.7 12.5 %all-to-all-start.1 = ((bf16[16,2,16,512]{3,2,1,0:T(8,128)(2,1)}), bf16[16,2,16,512]{3,2,1,0:T(8,128)(2,1)S(1)}, u32[]{:S(2)}, u32[]{:S(2)}) async-start(bf16[16,2,16,512]{3,2,1,0:T(8,128)(2,1)} %maximum_bitcast_fusion.2), calls=%async_computation.1 | async-start | bytes 1048576 | tf_op jit(solution)/shard_map/while/body/eval_jaxpr/all_to_all | solution.py:36
  451.5 13.2 %all-to-all-start.1 = ((bf16[16,2,16,512]{3,2,1,0:T(8,128)(2,1)}), bf16[16,2,16,512]{3,2,1,0:T(8,128)(2,1)S(1)}, u32[]{:S(2)}, u32[]{:S(2)}) async-start(bf16[16,2,16,512]{3,2,1,0:T(8,128)(2,1)} %maximum_bitcast_fusion.2), calls=%async_computation.1 | async-start | bytes 1048576 | tf_op jit(solution)/shard_map/while/body/eval_jaxpr/all_to_all | solution.py:36
  464.8 6.3 %collective-permute-start.1 = (bf16[2,16,512]{2,1,0:T(8,128)(2,1)S(1)}, bf16[2,16,512]{2,1,0:T(8,128)(2,1)S(1)}, u32[]{:S(2)}, u32[]{:S(2)}) collective-permute-start(bf16[2,16,512]{2,1,0:T(8,128)(2,1)S(1)} %get-tuple-element.382), channel_id=1, source_target_pairs={{16,0},{32,16},{48,32},{64,48},{80,64},{96,80},{112,96},{17,1},{33... | collective-permute-start | bytes 98312 | tf_op jit(solution)/shard_map/while/body/eval_jaxpr/ppermute | solution.py:25
  485.4 12.6 %all-to-all-start.1 = ((bf16[16,2,16,512]{3,2,1,0:T(8,128)(2,1)}), bf16[16,2,16,512]{3,2,1,0:T(8,128)(2,1)S(1)}, u32[]{:S(2)}, u32[]{:S(2)}) async-start(bf16[16,2,16,512]{3,2,1,0:T(8,128)(2,1)} %maximum_bitcast_fusion.2), calls=%async_computation.1 | async-start | bytes 1048576 | tf_op jit(solution)/shard_map/while/body/eval_jaxpr/all_to_all | solution.py:36
  518.5 12.8 %all-to-all-start.1 = ((bf16[16,2,16,512]{3,2,1,0:T(8,128)(2,1)}), bf16[16,2,16,512]{3,2,1,0:T(8,128)(2,1)S(1)}, u32[]{:S(2)}, u32[]{:S(2)}) async-start(bf16[16,2,16,512]{3,2,1,0:T(8,128)(2,1)} %maximum_bitcast_fusion.2), calls=%async_computation.1 | async-start | bytes 1048576 | tf_op jit(solution)/shard_map/while/body/eval_jaxpr/all_to_all | solution.py:36
  551.8 12.8 %all-to-all-start.1 = ((bf16[16,2,16,512]{3,2,1,0:T(8,128)(2,1)}), bf16[16,2,16,512]{3,2,1,0:T(8,128)(2,1)S(1)}, u32[]{:S(2)}, u32[]{:S(2)}) async-start(bf16[16,2,16,512]{3,2,1,0:T(8,128)(2,1)} %maximum_bitcast_fusion.2), calls=%async_computation.1 | async-start | bytes 1048576 | tf_op jit(solution)/shard_map/while/body/eval_jaxpr/all_to_all | solution.py:36
  (34 other events, 668.8 us)
where the time goes:
time: 574 us; the launch traced here: 571 us
  matrix products  234 us (41%)
  waiting for transfers between devices  191 us (33%)
  starting transfers between devices  121 us (21%)
  local copies, waits for them, and re-layouts  15.7 us (3%)
  other arithmetic  8.1 us (1%)
    all_to_all x8, waiting for transfers between devices, sent_to_all(): return lax.all_to_all(copies, axis, split_axis=0, concat_axis=0, tiled=True)  75 us
    all_to_all x8, waiting for transfers between devices, summed_on_arrival(): blocks = lax.all_to_all(split_up(shard, dim, size), axis, 0, 0, tiled=True)  72.8 us
    ppermute x16, starting transfers between devices, from_behind(): return lax.ppermute(shard, axis, pairs)  58.9 us
    dot_general x8, matrix products, rows_product(): lax.dot_general(trace_in[0], matrix[1], contract, preferred_element_type=...  51.8 us
    dot_general x8, matrix products, rows_product(): lax.dot_general(trace_in[1], matrix[1], contract, preferred_element_type=...  46.4 us
    ppermute x16, waiting for transfers between devices, from_behind(): return lax.ppermute(shard, axis, pairs)  43.3 us
    dot_general x8, matrix products, cols_product(): jnp.dot(trace_in[0], matrix[0], preferred_element_type=jnp.float32)  42.7 us
    dot_general x8, matrix products, cols_product(): jnp.dot(trace_in[0], matrix[1], preferred_element_type=jnp.float32)  37.8 us
  transfers between devices with their start and end apart: 32, of which 32 were waited for; matrix products, arithmetic and copies ran while one was open for 0% of the time, Pallas kernels for 0%

commit v1 on v0

v1 whole, which is shorter than its diff:
```python
import functools

import jax
import jax.numpy as jnp
from jax import lax
from jax.experimental import pallas as pl
from jax.experimental.pallas import tpu as pltpu
from jax.sharding import PartitionSpec as P

F32, BF16 = jnp.float32, jnp.bfloat16
MIB = 1 << 20


def pick_halves(matrix, half, chips):
    parts, rows, cols = matrix.shape
    wide = cols // (2 * chips)

    def body(half_ref, in_ref, out_ref):
        out_ref[...] = in_ref[...]

    return pl.pallas_call(
        body,
        grid_spec=pltpu.PrefetchScalarGridSpec(
            num_scalar_prefetch=1,
            grid=(chips,),
            in_specs=[pl.BlockSpec((parts, rows, wide), lambda i, h: (0, 0, 2 * i + h[0]))],
            out_specs=pl.BlockSpec((parts, rows, wide), lambda i, h: (0, 0, i)),
        ),
        out_shape=jax.ShapeDtypeStruct((parts, rows, cols // 2), BF16),
        compiler_params=pltpu.CompilerParams(vmem_limit_bytes=8 * MIB),
        name="pick_halves",
    )(half, matrix)


def load_half(use_own, half, matrix, received, chips):
    parts, rows, cols = matrix.shape
    wide = cols // (2 * chips)

    def body(own_ref, half_ref, matrix_ref, received_ref, out_ref, sems):
        @pl.when(own_ref[0] == 1)
        def _():
            start = half_ref[0] * wide

            def copy(i):
                at = pl.multiple_of(2 * i * wide + start, wide)
                return pltpu.make_async_copy(
                    matrix_ref.at[:, :, pl.ds(at, wide)],
                    out_ref.at[:, :, pl.ds(i * wide, wide)],
                    sems.at[i],
                )

            for i in range(chips):
                copy(i).start()
            for i in range(chips):
                copy(i).wait()

        @pl.when(own_ref[0] != 1)
        def _():
            def copy(i):
                return pltpu.make_async_copy(
                    received_ref.at[:, :, pl.ds(i * wide, wide)],
                    out_ref.at[:, :, pl.ds(i * wide, wide)],
                    sems.at[i],
                )

            for i in range(chips):
                copy(i).start()
            for i in range(chips):
                copy(i).wait()

    return pl.pallas_call(
        body,
        in_specs=[
            pl.BlockSpec(memory_space=pltpu.SMEM),
            pl.BlockSpec(memory_space=pltpu.SMEM),
            pl.BlockSpec(memory_space=pl.ANY),
            pl.BlockSpec(memory_space=pl.ANY),
        ],
        out_specs=pl.BlockSpec(memory_space=pltpu.VMEM),
        out_shape=pltpu.VMEM((parts, rows, cols // 2), BF16),
        scratch_shapes=[pltpu.SemaphoreType.DMA((chips,))],
        compiler_params=pltpu.CompilerParams(vmem_limit_bytes=20 * MIB),
        name="load_half",
    )(use_own, half, matrix, received)


def vmem_call(body, out_shape, name, flops):
    def call(*args):
        return pl.pallas_call(
            body,
            in_specs=[pl.BlockSpec(memory_space=pltpu.VMEM)] * len(args),
            out_specs=jax.tree.map(lambda _: pl.BlockSpec(memory_space=pltpu.VMEM), out_shape),
            out_shape=out_shape,
            compiler_params=pltpu.CompilerParams(vmem_limit_bytes=24 * MIB),
            cost_estimate=pl.CostEstimate(flops=flops, bytes_accessed=1 << 16, transcendentals=0),
            name=name,
        )(*args)

    return call


def down_body(x_ref, g_ref, core_ref, base_ref, mine_ref, theirs_ref):
    chips, rhs, wide = x_ref.shape
    contract = (((1,), (1,)), ((), ()))
    with_real = with_imag = None
    for i in range(chips):
        at = slice(i * wide, (i + 1) * wide)
        r = lax.dot_general(x_ref[i], g_ref[0, :, at], contract, preferred_element_type=F32)
        m = lax.dot_general(x_ref[i], g_ref[1, :, at], contract, preferred_element_type=F32)
        with_real = r if i == 0 else with_real + r
        with_imag = m if i == 0 else with_imag + m
    n = rhs // 2
    real = with_real[:n] - with_imag[n:]
    imag = with_imag[:n] + with_real[n:]
    first = jnp.concatenate([real[:, :wide], imag[:, :wide]], axis=0)
    second = jnp.concatenate([real[:, wide:], imag[:, wide:]], axis=0)
    on_first = core_ref[0:1, 0:1] == 0
    mine_ref[...] = jnp.where(on_first, first, second) + base_ref[...]
    theirs_ref[...] = jnp.where(on_first, second, first)


def up_body(x_ref, g_ref, out_ref):
    chips, rhs, wide = out_ref.shape
    n = rhs // 2
    x = x_ref[...]
    for i in range(chips):
        at = slice(i * wide, (i + 1) * wide)
        r = jnp.dot(x, g_ref[0, :, at], preferred_element_type=F32)
        m = jnp.dot(x, g_ref[1, :, at], preferred_element_type=F32)
        out_ref[i, :n] = (r[:n] - m[n:]).astype(BF16)
        out_ref[i, n:] = (m[:n] + r[n:]).astype(BF16)


def local(green, down_source, up_source):
    planes = lax.axis_size("sweep") // 2
    chips = lax.axis_size("layer")
    matrix = green[0]
    rows, cols = matrix.shape[1:]
    wide = rows // 2
    rhs = 2 * down_source.shape[2]
    me = lax.axis_index("sweep")
    core, plane = me % 2, me // 2

    swap_pairs = [(i, i ^ 1) for i in range(2 * planes)]

    def swap(x):
        return lax.ppermute(x, "sweep", swap_pairs)

    def hop(x, a, b):
        pairs = [p for c in range(2) for p in ((2 * a + c, 2 * b + c), (2 * b + c, 2 * a + c))]
        return lax.ppermute(x, "sweep", pairs)

    def exchange(blocks):
        return lax.all_to_all(blocks, "layer", 0, 0, tiled=True)

    one = lambda v: v.astype(jnp.int32).reshape(1)
    received = swap(pick_halves(matrix, one(1 - core), chips))

    def halves(source):
        full = source.reshape(rhs, rows)
        own = lax.dynamic_slice(full, (0, core * wide), (rhs, wide))
        other = swap(lax.dynamic_slice(full, (0, (1 - core) * wide), (rhs, wide)))
        first = core == 0
        return jnp.where(first, own, other), jnp.where(first, other, own)

    down_a, down_b = halves(down_source)
    base_a, base_b = down_a, down_b
    up_a, up_b = halves(up_source)

    matrix_b = load_half(one(core == 1), one(core), matrix, received, chips)
    matrix_a = load_half(one(core == 0), one(core), matrix, received, chips)
    core_tile = jnp.broadcast_to(core.astype(jnp.int32), (8, 128))

    flops = 8 * rhs * rows * cols // 2
    part = jax.ShapeDtypeStruct((rhs, wide), F32)
    down_call = vmem_call(down_body, (part, part), "down_product", flops)
    up_call = vmem_call(up_body, jax.ShapeDtypeStruct((chips, rhs, wide), BF16), "up_product", flops)

    def down_product(x, mat, base):
        blocks = exchange(jnp.broadcast_to(x.astype(BF16), (chips, rhs, wide)))
        mine, theirs = down_call(blocks, mat, core_tile, base)
        return mine + swap(theirs)

    def up_product(x, mat, base):
        x = x.astype(BF16)
        other = swap(x)
        first = core == 0
        full = jnp.concatenate([jnp.where(first, x, other), jnp.where(first, other, x)], axis=1)
        blocks = exchange(up_call(full, mat))
        return base + jnp.sum(blocks.astype(F32), axis=0)

    here = lambda p: plane == p
    x = base_a
    for p in range(planes):
        if p > 0:
            x = hop(x.astype(BF16), p - 1, p)
            x = down_product(x, matrix_a, base_a)
            down_a = jnp.where(here(p), x, down_a)
        x = down_product(x, matrix_b, base_b)
        down_b = jnp.where(here(p), x, down_b)

    base_a, base_b = up_a + down_a, up_b + down_b
    total_a, total_b = base_a, base_b
    x = base_b
    for p in reversed(range(planes)):
        if p < planes - 1:
            x = hop(x.astype(BF16), p + 1, p)
            x = up_product(x, matrix_b, base_b)
            total_b = jnp.where(here(p), x, total_b)
        x = up_product(x, matrix_a, base_a)
        total_a = jnp.where(here(p), x, total_a)

    first = core == 0
    keep = jnp.where(first, total_a, total_b)
    other = swap(jnp.where(first, total_b, total_a))
    out = jnp.concatenate([jnp.where(first, keep, other), jnp.where(first, other, keep)], axis=1)
    return out.reshape(1, 2, rhs // 2, rows)


def solution(mesh):
    in_specs = (
        P("sweep", None, "layer", None),
        P("sweep", None, None, "layer"),
        P("sweep", None, None, "layer"),
    )
    out_specs = P("sweep", None, None, "layer")
    return jax.shard_map(local, mesh=mesh, in_specs=in_specs, out_specs=out_specs, check_vma=False)
```

time: 574 us -> 317 us (0.55)
  matrix products: 234 us -> 0 us
  waiting for transfers between devices: 191 us -> 28.3 us
  blocking collectives: 0 us -> 122 us
  starting transfers between devices: 121 us -> 73 us
  Pallas kernels: 0 us -> 41.5 us
  local copies, waits for them, and re-layouts: 15.7 us -> 49.8 us
  other arithmetic: 8.1 us -> 1.21 us
    dot_general x64 -> x0, matrix products: 234 us -> none  [the longest x8 51.8 us: rows_product(): lax.dot_general(trace_in[0], matrix[1], contract, preferred_element_type=...]
    all_to_all x16 -> x3, waiting for transfers between devices: 148 us -> 7.15 us  [exchange(): return lax.all_to_all(blocks, 'layer', 0, 0, tiled=True)]
    all_to_all x0 -> x11, blocking collectives: none -> 122 us  [exchange(): return lax.all_to_all(blocks, 'layer', 0, 0, tiled=True)]
    unnamed x4 -> x38, local copies, waits for them, and re-layouts: 0.64 us -> 47.5 us
    all_to_all x16 -> x3, starting transfers between devices: 61.8 us -> 17.3 us  [exchange(): return lax.all_to_all(blocks, 'layer', 0, 0, tiled=True)]
    pallas_call x0 -> x17, Pallas kernels: none -> 41.5 us  [the longest x14 28.5 us: call(): pl.pallas_call(body, in_specs=[pl.BlockSpec(memory_space=pltpu.VMEM)] * l...]
    ppermute x16 -> x24, waiting for transfers between devices: 43.3 us -> 21.1 us  [the longest x18 18.9 us: swap(): return lax.ppermute(x, 'sweep', swap_pairs)]
    transpose x8 -> x0, other arithmetic: 6.82 us -> none  [split_up(): return jnp.moveaxis(blocks, dim, 0)]
  transfers between devices with their start and end apart: 32 -> 27, of which waited for: 32 -> 19; matrix products, arithmetic and copies ran while one was open for 0% -> 0% of each run, Pallas kernels for 0% -> 2%
where the time goes in v1:
time: 317 us; the launch traced here: 316 us
  blocking collectives  122 us (38%)
  starting transfers between devices  73 us (23%)
  local copies, waits for them, and re-layouts  49.8 us (16%)
  Pallas kernels  41.5 us (13%)
  waiting for transfers between devices  28.3 us (9%)
    all_to_all x11, blocking collectives, exchange(): return lax.all_to_all(blocks, 'layer', 0, 0, tiled=True)  122 us
    unnamed x38, local copies, waits for them, and re-layouts  47.5 us
    ppermute x18, starting transfers between devices, swap(): return lax.ppermute(x, 'sweep', swap_pairs)  29.4 us
    pallas_call x14, Pallas kernels, call(): pl.pallas_call(body, in_specs=[pl.BlockSpec(memory_space=pltpu.VMEM)] * l...  28.5 us
    ppermute x6, starting transfers between devices, hop(): return lax.ppermute(x, 'sweep', pairs)  26.3 us
    ppermute x18, waiting for transfers between devices, swap(): return lax.ppermute(x, 'sweep', swap_pairs)  18.9 us
    all_to_all x3, starting transfers between devices, exchange(): return lax.all_to_all(blocks, 'layer', 0, 0, tiled=True)  17.3 us
    pallas_call x1, Pallas kernels, pick_halves(): pl.pallas_call(body, grid_spec=pltpu.PrefetchScalarGridSpec(num_scalar_pr...  7.95 us
  transfers between devices with their start and end apart: 27, of which 19 were waited for; matrix products, arithmetic and copies ran while one was open for 0% of the time, Pallas kernels for 2%

profile of v1, /device:TPU:1, one launch (start us, length us, event | category | flops | bytes accessed | tf_op | source)
XLA Modules:
  0.0 315.8 jit_solution(229987890596312567)
XLA Ops:
  0.0 5.8 %copy-done.10 = bf16[1,2,512,8192]{3,2,1,0:T(8,128)(2,1)S(1)} copy-done((bf16[1,2,512,8192]{3,2,1,0:T(8,128)(2,1)S(1)}, bf16[1,2,512,8192]{3,2,1,0:T(8,128)(2,1)}, u32[]{:S(2)}) %copy-start.10) | copy-done | bytes 16777240
  5.8 7.9 %pick_halves.1 = bf16[2,512,4096]{2,1,0:T(8,128)(2,1)} custom-call(s32[1]{0:T(128)} %bitcast.5.half_ref, bf16[2,512,8192]{2,1,0:T(8,128)(2,1)S(1)} %bitcast.12), custom_call_target="tpu_custom_call" | custom-call | tf_op jit(solution)/shard_map/pick_halves/pallas_call | solution.py:21
  15.2 5.8 %collective-permute-done.1 = f32[32,256]{1,0:T(8,128)S(1)} collective-permute-done((f32[32,256]{1,0:T(8,128)S(1)}, f32[32,256]{1,0:T(8,128)S(1)}, u32[]{:S(2)}, u32[]{:S(2)}) %collective-permute-start.1) | collective-permute-done | bytes 32800 | tf_op jit(solution)/shard_map/ppermute | solution.py:147
  21.8 6.8 %all-to-all-start = ((bf16[16,32,256]{2,1,0:T(8,128)(2,1)}), bf16[16,32,256]{2,1,0:T(8,128)(2,1)S(1)}, u32[]{:S(2)}, u32[]{:S(2)}) async-start(bf16[16,32,256]{2,1,0:T(8,128)(2,1)} %broadcast_in_dim.24), calls=%async_computation | async-start | bytes 524288 | tf_op jit(solution)/shard_map/all_to_all | solution.py:154
  28.6 5.8 %copy-done.11 = bf16[1,2,512,8192]{3,2,1,0:T(8,128)(2,1)S(1)} copy-done((bf16[1,2,512,8192]{3,2,1,0:T(8,128)(2,1)S(1)}, bf16[1,2,512,8192]{3,2,1,0:T(8,128)(2,1)}, u32[]{:S(2)}) %copy-start.11) | copy-done | bytes 16777240
  39.1 3.4 %copy-done.1 = bf16[2,512,4096]{2,1,0:T(8,128)(2,1)S(1)} copy-done((bf16[2,512,4096]{2,1,0:T(8,128)(2,1)S(1)}, bf16[2,512,4096]{2,1,0:T(8,128)(2,1)}, u32[]{:S(2)}) %copy-start.1) | copy-done | bytes 8388632
  48.7 3.5 %collective-permute-start.4 = (bf16[32,256]{1,0:T(8,128)(2,1)S(1)}, bf16[32,256]{1,0:T(8,128)(2,1)S(1)}, u32[]{:S(2)}, u32[]{:S(2)}) collective-permute-start(bf16[32,256]{1,0:T(8,128)(2,1)S(1)} %add_convert_fusion.11), channel_id=1, source_target_pairs={{0,32},{32,0},{16,48},{48,16},{1,33},{33,1},{17,49},{49,17},{2,34}... | collective-permute-start | bytes 49160 | tf_op jit(solution)/shard_map/ppermute | solution.py:151
  54.0 6.9 %all-to-all-start.1 = ((bf16[16,32,256]{2,1,0:T(8,128)(2,1)}), bf16[16,32,256]{2,1,0:T(8,128)(2,1)S(1)}, u32[]{:S(2)}, u32[]{:S(2)}) async-start(bf16[16,32,256]{2,1,0:T(8,128)(2,1)} %broadcast_in_dim.26), calls=%async_computation.1 | async-start | bytes 524288 | tf_op jit(solution)/shard_map/all_to_all | solution.py:154
  61.0 5.8 %copy-done.12 = bf16[1,2,512,8192]{3,2,1,0:T(8,128)(2,1)S(1)} copy-done((bf16[1,2,512,8192]{3,2,1,0:T(8,128)(2,1)S(1)}, bf16[1,2,512,8192]{3,2,1,0:T(8,128)(2,1)}, u32[]{:S(2)}) %copy-start.12) | copy-done | bytes 16777240
  66.7 3.6 %load_half.3.g_ref = bf16[2,512,4096]{2,1,0:T(8,128)(2,1)S(1)} custom-call(s32[1]{0:T(128)} %bitcast.6.own_ref, s32[1]{0:T(128)} %bitcast.3.half_ref, bf16[2,512,8192]{2,1,0:T(8,128)(2,1)S(1)} %bitcast.14, bf16[2,512,4096]{2,1,0:T(8,128)(2,1)} %collective-permute-done.2.received_ref), custom_call_target="tpu_custom_call" | custom-call | tf_op jit(solution)/shard_map/load_half/pallas_call | solution.py:71
  80.9 14.2 %all_to_all.70.x_ref = bf16[16,32,256]{2,1,0:T(8,128)(2,1)S(1)} all-to-all(bf16[16,32,256]{2,1,0:T(8,128)(2,1)S(1)} %broadcast_in_dim.27), channel_id=1, replica_groups=mesh['sweep'=8,'layer'=16] {'layer'}, dimensions={0} | all-to-all | bytes 524288 | tf_op jit(solution)/shard_map/all_to_all | solution.py:154
  104.4 10.7 %all_to_all.71.x_ref = bf16[16,32,256]{2,1,0:T(8,128)(2,1)S(1)} all-to-all(bf16[16,32,256]{2,1,0:T(8,128)(2,1)S(1)} %broadcast_in_dim.28), channel_id=1, replica_groups=mesh['sweep'=8,'layer'=16] {'layer'}, dimensions={0} | all-to-all | bytes 524288 | tf_op jit(solution)/shard_map/all_to_all | solution.py:154
  120.6 10.7 %all_to_all.72.x_ref = bf16[16,32,256]{2,1,0:T(8,128)(2,1)S(1)} all-to-all(bf16[16,32,256]{2,1,0:T(8,128)(2,1)S(1)} %broadcast_in_dim.29), channel_id=1, replica_groups=mesh['sweep'=8,'layer'=16] {'layer'}, dimensions={0} | all-to-all | bytes 524288 | tf_op jit(solution)/shard_map/all_to_all | solution.py:154
  137.4 10.7 %all_to_all.73.x_ref = bf16[16,32,256]{2,1,0:T(8,128)(2,1)S(1)} all-to-all(bf16[16,32,256]{2,1,0:T(8,128)(2,1)S(1)} %broadcast_in_dim.30), channel_id=1, replica_groups=mesh['sweep'=8,'layer'=16] {'layer'}, dimensions={0} | all-to-all | bytes 524288 | tf_op jit(solution)/shard_map/all_to_all | solution.py:154
  154.2 3.5 %all-to-all-start.6 = ((bf16[16,32,256]{2,1,0:T(8,128)(2,1)}), bf16[16,32,256]{2,1,0:T(8,128)(2,1)S(1)}, u32[]{:S(2)}, u32[]{:S(2)}) async-start(bf16[16,32,256]{2,1,0:T(8,128)(2,1)} %broadcast_in_dim.31), calls=%async_computation.6 | async-start | bytes 524288 | tf_op jit(solution)/shard_map/all_to_all | solution.py:154
  158.3 7.1 %all-to-all-done.6.x_ref = bf16[16,32,256]{2,1,0:T(8,128)(2,1)S(1)} async-done(((bf16[16,32,256]{2,1,0:T(8,128)(2,1)}), bf16[16,32,256]{2,1,0:T(8,128)(2,1)S(1)}, u32[]{:S(2)}, u32[]{:S(2)}) %all-to-all-start.6) | async-done | bytes 262176 | tf_op jit(solution)/shard_map/all_to_all | solution.py:154
  180.2 10.8 %all_to_all.74 = bf16[16,32,256]{2,1,0:T(8,128)(2,1)S(1)} all-to-all(bf16[16,32,256]{2,1,0:T(8,128)(2,1)S(1)} %up_product.7), channel_id=1, replica_groups=mesh['sweep'=8,'layer'=16] {'layer'}, dimensions={0} | all-to-all | bytes 524288 | tf_op jit(solution)/shard_map/all_to_all | solution.py:154
  199.5 10.7 %all_to_all.75 = bf16[16,32,256]{2,1,0:T(8,128)(2,1)S(1)} all-to-all(bf16[16,32,256]{2,1,0:T(8,128)(2,1)S(1)} %up_product.8), channel_id=1, replica_groups=mesh['sweep'=8,'layer'=16] {'layer'}, dimensions={0} | all-to-all | bytes 524288 | tf_op jit(solution)/shard_map/all_to_all | solution.py:154
  218.0 10.7 %all_to_all.76 = bf16[16,32,256]{2,1,0:T(8,128)(2,1)S(1)} all-to-all(bf16[16,32,256]{2,1,0:T(8,128)(2,1)S(1)} %up_product.9), channel_id=1, replica_groups=mesh['sweep'=8,'layer'=16] {'layer'}, dimensions={0} | all-to-all | bytes 524288 | tf_op jit(solution)/shard_map/all_to_all | solution.py:154
  234.1 10.7 %all_to_all.77 = bf16[16,32,256]{2,1,0:T(8,128)(2,1)S(1)} all-to-all(bf16[16,32,256]{2,1,0:T(8,128)(2,1)S(1)} %up_product.10), channel_id=1, replica_groups=mesh['sweep'=8,'layer'=16] {'layer'}, dimensions={0} | all-to-all | bytes 524288 | tf_op jit(solution)/shard_map/all_to_all | solution.py:154
  249.2 10.7 %all_to_all.78 = bf16[16,32,256]{2,1,0:T(8,128)(2,1)S(1)} all-to-all(bf16[16,32,256]{2,1,0:T(8,128)(2,1)S(1)} %up_product.11), channel_id=1, replica_groups=mesh['sweep'=8,'layer'=16] {'layer'}, dimensions={0} | all-to-all | bytes 524288 | tf_op jit(solution)/shard_map/all_to_all | solution.py:154
  260.0 20.1 %collective-permute-start.20 = (bf16[32,256]{1,0:T(8,128)(2,1)S(1)}, bf16[32,256]{1,0:T(8,128)(2,1)S(1)}, u32[]{:S(2)}, u32[]{:S(2)}) collective-permute-start(bf16[32,256]{1,0:T(8,128)(2,1)S(1)} %add_convert_fusion.3), channel_id=1, source_target_pairs={{32,0},{0,32},{48,16},{16,48},{33,1},{1,33},{49,17},{17,49},{34,2}... | collective-permute-start | bytes 49160 | tf_op jit(solution)/shard_map/ppermute | solution.py:151
  286.4 10.7 %all_to_all.79 = bf16[16,32,256]{2,1,0:T(8,128)(2,1)S(1)} all-to-all(bf16[16,32,256]{2,1,0:T(8,128)(2,1)S(1)} %up_product.12), channel_id=1, replica_groups=mesh['sweep'=8,'layer'=16] {'layer'}, dimensions={0} | all-to-all | bytes 524288 | tf_op jit(solution)/shard_map/all_to_all | solution.py:154
  301.6 10.7 %all_to_all.80 = bf16[16,32,256]{2,1,0:T(8,128)(2,1)S(1)} all-to-all(bf16[16,32,256]{2,1,0:T(8,128)(2,1)S(1)} %up_product.13), channel_id=1, replica_groups=mesh['sweep'=8,'layer'=16] {'layer'}, dimensions={0} | all-to-all | bytes 524288 | tf_op jit(solution)/shard_map/all_to_all | solution.py:154
  (146 shorter events, 107.6 us)
Async XLA Ops:
  13.7 14.9 %collective-permute-start.2 = (bf16[2,512,4096]{2,1,0:T(8,128)(2,1)}, bf16[2,512,4096]{2,1,0:T(8,128)(2,1)}, u32[]{:S(2)}, u32[]{:S(2)}) collective-permute-start(bf16[2,512,4096]{2,1,0:T(8,128)(2,1)} %pick_halves.1), channel_id=1, source_target_pairs={{0,16},{16,0},{32,48},{48,32},{64,80},{80,64},{96,112},{112,96},{1... | collective-permute-start | bytes 25165832 | tf_op jit(solution)/shard_map/ppermute | solution.py:147
  15.2 5.9 %collective-permute-start.1 = (f32[32,256]{1,0:T(8,128)S(1)}, f32[32,256]{1,0:T(8,128)S(1)}, u32[]{:S(2)}, u32[]{:S(2)}) collective-permute-start(f32[32,256]{1,0:T(8,128)S(1)} %constant_dynamic-slice_fusion), channel_id=1, source_target_pairs={{0,16},{16,0},{32,48},{48,32},{64,80},{80,64},{96,112},{112,96},{1... | collective-permute-start | bytes 98312 | tf_op jit(solution)/shard_map/ppermute | solution.py:147
  21.8 17.4 %all-to-all-start = ((bf16[16,32,256]{2,1,0:T(8,128)(2,1)}), bf16[16,32,256]{2,1,0:T(8,128)(2,1)S(1)}, u32[]{:S(2)}, u32[]{:S(2)}) async-start(bf16[16,32,256]{2,1,0:T(8,128)(2,1)} %broadcast_in_dim.24), calls=%async_computation | async-start | bytes 524288 | tf_op jit(solution)/shard_map/all_to_all | solution.py:154
  45.1 3.6 %collective-permute-start.3 = (f32[32,256]{1,0:T(8,128)S(1)}, f32[32,256]{1,0:T(8,128)S(1)}, u32[]{:S(2)}, u32[]{:S(2)}) collective-permute-start(f32[32,256]{1,0:T(8,128)S(1)} %get-tuple-element.20), channel_id=1, source_target_pairs={{0,16},{16,0},{32,48},{48,32},{64,80},{80,64},{96,112},{112,96},{1... | collective-permute-start | bytes 98312 | tf_op jit(solution)/shard_map/ppermute | solution.py:147
  48.7 4.7 %collective-permute-start.4 = (bf16[32,256]{1,0:T(8,128)(2,1)S(1)}, bf16[32,256]{1,0:T(8,128)(2,1)S(1)}, u32[]{:S(2)}, u32[]{:S(2)}) collective-permute-start(bf16[32,256]{1,0:T(8,128)(2,1)S(1)} %add_convert_fusion.11), channel_id=1, source_target_pairs={{0,32},{32,0},{16,48},{48,16},{1,33},{33,1},{17,49},{49,17},{2,34}... | collective-permute-start | bytes 49160 | tf_op jit(solution)/shard_map/ppermute | solution.py:151
  54.0 19.6 %all-to-all-start.1 = ((bf16[16,32,256]{2,1,0:T(8,128)(2,1)}), bf16[16,32,256]{2,1,0:T(8,128)(2,1)S(1)}, u32[]{:S(2)}, u32[]{:S(2)}) async-start(bf16[16,32,256]{2,1,0:T(8,128)(2,1)} %broadcast_in_dim.26), calls=%async_computation.1 | async-start | bytes 524288 | tf_op jit(solution)/shard_map/all_to_all | solution.py:154
  79.6 1.3 collective-permute-start.5
  101.1 2.6 collective-permute-start.6
  117.7 2.8 collective-permute-start.8
  133.8 2.8 collective-permute-start.9
  150.6 2.8 collective-permute-start.11
  154.2 11.2 %all-to-all-start.6 = ((bf16[16,32,256]{2,1,0:T(8,128)(2,1)}), bf16[16,32,256]{2,1,0:T(8,128)(2,1)S(1)}, u32[]{:S(2)}, u32[]{:S(2)}) async-start(bf16[16,32,256]{2,1,0:T(8,128)(2,1)} %broadcast_in_dim.31), calls=%async_computation.6 | async-start | bytes 524288 | tf_op jit(solution)/shard_map/all_to_all | solution.py:154
  157.8 15.4 %collective-permute-start = (f32[32,256]{1,0:T(8,128)S(1)}, f32[32,256]{1,0:T(8,128)S(1)}, u32[]{:S(2)}, u32[]{:S(2)}) collective-permute-start(f32[32,256]{1,0:T(8,128)S(1)} %constant_dynamic-slice_fusion.1), channel_id=1, source_target_pairs={{0,16},{16,0},{32,48},{48,32},{64,80},{80,64},{96,112},{112,96},{1... | collective-permute-start | bytes 98312 | tf_op jit(solution)/shard_map/ppermute | solution.py:147
  171.4 2.6 collective-permute-start.12
  174.0 1.3 collective-permute-start.13
  191.8 2.8 collective-permute-start.15
  210.3 2.8 collective-permute-start.16
  228.8 0.7 collective-permute-start.17
  229.5 3.0 collective-permute-start.18
  244.9 2.8 collective-permute-start.19
  260.0 21.2 %collective-permute-start.20 = (bf16[32,256]{1,0:T(8,128)(2,1)S(1)}, bf16[32,256]{1,0:T(8,128)(2,1)S(1)}, u32[]{:S(2)}, u32[]{:S(2)}) collective-permute-start(bf16[32,256]{1,0:T(8,128)(2,1)S(1)} %add_convert_fusion.3), channel_id=1, source_target_pairs={{32,0},{0,32},{48,16},{16,48},{33,1},{1,33},{49,17},{17,49},{34,2}... | collective-permute-start | bytes 49160 | tf_op jit(solution)/shard_map/ppermute | solution.py:151
  281.3 3.6 %collective-permute-start.21 = (bf16[32,256]{1,0:T(8,128)(2,1)S(1)}, bf16[32,256]{1,0:T(8,128)(2,1)S(1)}, u32[]{:S(2)}, u32[]{:S(2)}) collective-permute-start(bf16[32,256]{1,0:T(8,128)(2,1)S(1)} %collective-permute-done.20), channel_id=1, source_target_pairs={{0,16},{16,0},{32,48},{48,32},{64,80},{80,64},{96,112},{112,96},{1... | collective-permute-start | bytes 49160 | tf_op jit(solution)/shard_map/ppermute | solution.py:147
  297.2 2.8 collective-permute-start.22
  312.4 2.8 collective-permute-start.23
  (22 other events, 223.0 us)

commit v2 on v1

v2 whole, which is shorter than its diff:
```python
import jax
import jax.numpy as jnp
from jax import lax
from jax.experimental import pallas as pl
from jax.experimental.pallas import tpu as pltpu
from jax.sharding import PartitionSpec as P

F32, BF16 = jnp.float32, jnp.bfloat16
MIB = 1 << 20
VMEM = pl.BlockSpec(memory_space=pltpu.VMEM)
HBM = pl.BlockSpec(memory_space=pltpu.HBM)
SMEM = pl.BlockSpec(memory_space=pltpu.SMEM)


def copy_all(copies):
    for copy in copies:
        copy.start()
    for copy in copies:
        copy.wait()


def second_halves(matrix, chips):
    parts, rows, cols = matrix.shape
    wide = cols // (2 * chips)

    def body(matrix_ref, out_ref, sems):
        copy_all(
            [
                pltpu.make_async_copy(
                    matrix_ref.at[:, :, pl.ds((2 * i + 1) * wide, wide)],
                    out_ref.at[:, :, pl.ds(i * wide, wide)],
                    sems.at[i],
                )
                for i in range(chips)
            ]
        )

    return pl.pallas_call(
        body,
        in_specs=[HBM],
        out_specs=HBM,
        out_shape=pltpu.HBM((parts, rows, cols // 2), BF16),
        scratch_shapes=[pltpu.SemaphoreType.DMA((chips,))],
        compiler_params=pltpu.CompilerParams(vmem_limit_bytes=56 * MIB),
        name="second_halves",
    )(matrix)


def load_half(core, on_core, matrix, received, after, chips):
    parts, rows, cols = matrix.shape
    wide = cols // (2 * chips)

    def body(core_ref, matrix_ref, received_ref, after_ref, out_ref, sems):
        @pl.when(core_ref[0] == on_core)
        def _():
            copy_all(
                [
                    pltpu.make_async_copy(
                        matrix_ref.at[:, :, pl.ds(2 * i * wide, wide)],
                        out_ref.at[:, :, pl.ds(i * wide, wide)],
                        sems.at[i],
                    )
                    for i in range(chips)
                ]
            )

        @pl.when(core_ref[0] != on_core)
        def _():
            copy_all(
                [
                    pltpu.make_async_copy(
                        received_ref.at[:, :, pl.ds(i * wide, wide)],
                        out_ref.at[:, :, pl.ds(i * wide, wide)],
                        sems.at[i],
                    )
                    for i in range(chips)
                ]
            )

    return pl.pallas_call(
        body,
        in_specs=[SMEM, HBM, HBM, VMEM],
        out_specs=VMEM,
        out_shape=pltpu.VMEM((parts, rows, cols // 2), BF16),
        scratch_shapes=[pltpu.SemaphoreType.DMA((chips,))],
        compiler_params=pltpu.CompilerParams(vmem_limit_bytes=40 * MIB),
        name="load_half",
    )(core, matrix, received, after)


def vmem_call(body, out_shape, name, flops):
    def call(*args):
        return pl.pallas_call(
            body,
            in_specs=[VMEM] * len(args),
            out_specs=jax.tree.map(lambda _: VMEM, out_shape),
            out_shape=out_shape,
            compiler_params=pltpu.CompilerParams(vmem_limit_bytes=8 * MIB),
            cost_estimate=pl.CostEstimate(flops=flops, bytes_accessed=1 << 16, transcendentals=0),
            name=name,
        )(*args)

    return call


def down_body(x_ref, g_ref, first_ref, base_ref, mine_ref, theirs_ref):
    chips, rhs, wide = x_ref.shape
    contract = (((1,), (1,)), ((), ()))
    with_real = with_imag = None
    for i in range(chips):
        at = slice(i * wide, (i + 1) * wide)
        r = lax.dot_general(x_ref[i], g_ref[0, :, at], contract, preferred_element_type=F32)
        m = lax.dot_general(x_ref[i], g_ref[1, :, at], contract, preferred_element_type=F32)
        with_real = r if i == 0 else with_real + r
        with_imag = m if i == 0 else with_imag + m
    n = rhs // 2
    real = with_real[:n] - with_imag[n:]
    imag = with_imag[:n] + with_real[n:]
    first = jnp.concatenate([real[:, :wide], imag[:, :wide]], axis=0)
    second = jnp.concatenate([real[:, wide:], imag[:, wide:]], axis=0)
    keeps_first = first_ref[0:1, 0:1] == 1
    mine_ref[...] = jnp.where(keeps_first, first, second) + base_ref[...]
    theirs_ref[...] = jnp.where(keeps_first, second, first)


def up_body(x_ref, g_ref, out_ref):
    chips, rhs, wide = out_ref.shape
    n = rhs // 2
    x = x_ref[...]
    for i in range(chips):
        at = slice(i * wide, (i + 1) * wide)
        r = jnp.dot(x, g_ref[0, :, at], preferred_element_type=F32)
        m = jnp.dot(x, g_ref[1, :, at], preferred_element_type=F32)
        out_ref[i, :n] = (r[:n] - m[n:]).astype(BF16)
        out_ref[i, n:] = (m[:n] + r[n:]).astype(BF16)


def make_masks(me, count, shape):
    def body(me_ref, out_ref):
        index = me_ref[0]
        for p in range(count):
            out_ref[p] = jnp.full(shape, jnp.where(index // 2 == p, 1, 0), jnp.int32)
        out_ref[count] = jnp.full(shape, jnp.where(index % 2 == 0, 1, 0), jnp.int32)

    return pl.pallas_call(
        body,
        in_specs=[SMEM],
        out_specs=VMEM,
        out_shape=pltpu.VMEM((count + 1, *shape), jnp.int32),
        name="make_masks",
    )(me)


def local(green, down_source, up_source):
    planes = lax.axis_size("sweep") // 2
    chips = lax.axis_size("layer")
    matrix = green[0]
    rows, cols = matrix.shape[1:]
    wide = rows // 2
    rhs = 2 * down_source.shape[2]
    me = lax.axis_index("sweep")
    masks = make_masks(me.astype(jnp.int32).reshape(1), planes, (rhs, wide))
    tile_0 = masks[planes, :8, :128]
    tile_1 = 1 - tile_0
    masks = [masks[p] == 1 for p in range(planes + 1)]
    on_0 = masks.pop()

    def swap(x):
        return lax.ppermute(x, "sweep", [(i, i ^ 1) for i in range(2 * planes)])

    def hop(x, a, b):
        pairs = [p for c in range(2) for p in ((2 * a + c, 2 * b + c), (2 * b + c, 2 * a + c))]
        return lax.ppermute(x, "sweep", pairs)

    def exchange(blocks):
        return lax.all_to_all(blocks, "layer", 0, 0, tiled=True)

    down_own = down_source.reshape(rhs, rows)
    down_got = swap(down_own[:, :wide])
    received = swap(second_halves(matrix, chips))
    base_a = jnp.where(on_0, down_own[:, wide:], down_got)
    base_b = jnp.where(on_0, down_got, down_own[:, wide:])
    up_own = up_source.reshape(rhs, rows)
    up_other = swap(up_own)
    up_a = jnp.where(on_0, up_own[:, :wide], up_other[:, wide:])
    up_b_rest = jnp.where(on_0, up_other[:, :wide], up_own[:, wide:])

    core = (me % 2).astype(jnp.int32).reshape(1)
    tie = lambda *values: lax.optimization_barrier(values)

    flops = 8 * rhs * rows * cols // 2
    part = jax.ShapeDtypeStruct((rhs, wide), F32)
    down_call = vmem_call(down_body, (part, part), "down_product", flops)
    up_call = vmem_call(up_body, jax.ShapeDtypeStruct((chips, rhs, wide), BF16), "up_product", flops)

    def spread(x):
        return exchange(jnp.broadcast_to(x.astype(BF16), (chips, rhs, wide)))

    def down_product(blocks, mat, keeps_first, base):
        mine, theirs = down_call(blocks, mat, keeps_first, base)
        return mine + swap(theirs)

    def up_product(x, other, first_on_0, mat, base):
        x, other = x.astype(BF16), other.astype(BF16)
        halves = [jnp.where(on_0, x, other), jnp.where(on_0, other, x)]
        full = jnp.concatenate(halves if first_on_0 else halves[::-1], axis=1)
        blocks = exchange(up_call(full, mat))
        return base + jnp.sum(blocks.astype(F32), axis=0)

    down_a, down_b = base_a, base_b
    matrix_a = matrix_b = None
    x, tile_0, tile_1, on_0, masks = tie(base_a, tile_0, tile_1, on_0, masks)
    for p in range(planes):
        if p > 0:
            if p == 1:
                matrix_a = load_half(core, 0, matrix, received, x, chips)
            x = hop(x.astype(BF16), p - 1, p)
            if p == 1:
                x, matrix_a, up_a, up_b_rest = tie(x, matrix_a, up_a, up_b_rest)
            x = down_product(spread(x), matrix_a, tile_1, base_a)
            down_a = jnp.where(masks[p], x, down_a)
        blocks = spread(x)
        if p == 0:
            matrix_b = load_half(core, 1, matrix, received, blocks, chips)
        x = down_product(blocks, matrix_b, tile_0, base_b)
        down_b = jnp.where(masks[p], x, down_b)

    rest = up_b_rest + down_b
    base_b = swap(rest)
    base_a = up_a + swap(down_a)
    base_a, base_b, rest = tie(base_a, base_b, rest)
    total_a, total_b = base_a, base_b
    x = None
    for p in reversed(range(planes)):
        if p < planes - 1:
            x = hop(x.astype(BF16), p + 1, p)
            x = up_product(x, swap(x), True, matrix_b, base_b)
            total_b = jnp.where(masks[p], x, total_b)
            other = swap(x.astype(BF16))
        else:
            x, other = base_b, rest
        x = up_product(x, other, False, matrix_a, base_a)
        total_a = jnp.where(masks[p], x, total_a)

    got = swap(jnp.where(on_0, total_b, total_a))
    out = jnp.concatenate([jnp.where(on_0, total_a, total_b), got], axis=1)
    return out.reshape(1, 2, rhs // 2, rows)


def solution(mesh):
    in_specs = (
        P("sweep", None, "layer", None),
        P("sweep", None, None, "layer"),
        P("sweep", None, None, "layer"),
    )
    out_specs = P("sweep", None, None, "layer")
    return jax.shard_map(local, mesh=mesh, in_specs=in_specs, out_specs=out_specs, check_vma=False)
```

time: 317 us -> 524 us (1.65)
  Pallas kernels: 41.5 us -> 291 us
  local copies, waits for them, and re-layouts: 49.8 us -> 0.86 us
  blocking collectives: 122 us -> 139 us
  starting transfers between devices: 73 us -> 63.3 us
    pallas_call x17 -> x18, Pallas kernels: 41.5 us -> 291 us  [the longest x1 255 us: second_halves(): pl.pallas_call(body, in_specs=[HBM], out_specs=HBM, out_shape=pltpu.HBM((...]
    unnamed x38 -> x4, local copies, waits for them, and re-layouts: 47.5 us -> 0.01 us
    all_to_all x11 -> x13, blocking collectives: 122 us -> 139 us  [exchange(): return lax.all_to_all(blocks, 'layer', 0, 0, tiled=True)]
    all_to_all x3 -> x1, starting transfers between devices: 17.3 us -> 6.84 us  [exchange(): return lax.all_to_all(blocks, 'layer', 0, 0, tiled=True)]
    ppermute x18 -> x19, starting transfers between devices: 29.4 us -> 30.7 us  [swap(): return lax.ppermute(x, 'sweep', [(i, i ^ 1) for i in range(2 * planes)])]
    ppermute x18 -> x19, waiting for transfers between devices: 18.9 us -> 18.1 us  [swap(): return lax.ppermute(x, 'sweep', [(i, i ^ 1) for i in range(2 * planes)])]
  transfers between devices with their start and end apart: 27 -> 26, of which waited for: 19 -> 18; matrix products, arithmetic and copies ran while one was open for 0% -> 0% of each run, Pallas kernels for 2% -> 1%
where the time goes in v2:
time: 524 us; the launch traced here: 523 us
  Pallas kernels  291 us (56%)
  blocking collectives  139 us (27%)
  starting transfers between devices  63.3 us (12%)
  waiting for transfers between devices  27 us (5%)
    pallas_call x1, Pallas kernels, second_halves(): pl.pallas_call(body, in_specs=[HBM], out_specs=HBM, out_shape=pltpu.HBM((...  255 us
    all_to_all x13, blocking collectives, exchange(): return lax.all_to_all(blocks, 'layer', 0, 0, tiled=True)  139 us
    ppermute x19, starting transfers between devices, swap(): return lax.ppermute(x, 'sweep', [(i, i ^ 1) for i in range(2 * planes)])  30.7 us
    pallas_call x14, Pallas kernels, call(): pl.pallas_call(body, in_specs=[VMEM] * len(args), out_specs=jax.tree.map(...  28.5 us
    ppermute x6, starting transfers between devices, hop(): return lax.ppermute(x, 'sweep', pairs)  25.7 us
    ppermute x19, waiting for transfers between devices, swap(): return lax.ppermute(x, 'sweep', [(i, i ^ 1) for i in range(2 * planes)])  18.1 us
  transfers between devices with their start and end apart: 26, of which 18 were waited for; matrix products, arithmetic and copies ran while one was open for 0% of the time, Pallas kernels for 1%

profile of v2, /device:TPU:1, one launch (start us, length us, event | category | flops | bytes accessed | tf_op | source)
XLA Modules:
  0.0 523.4 jit_solution(5692306424325981375)
XLA Ops:
  0.0 255.4 %second_halves.1 = bf16[2,512,4096]{2,1,0:T(8,128)(2,1)} custom-call(bf16[2,512,8192]{2,1,0:T(8,128)(2,1)} %bitcast.21), custom_call_target="tpu_custom_call" | custom-call | tf_op jit(solution)/shard_map/second_halves/pallas_call | solution.py:38
  257.5 5.5 %collective-permute-done.4 = f32[32,512]{1,0:T(8,128)S(1)} collective-permute-done((f32[32,512]{1,0:T(8,128)S(1)}, f32[32,512]{1,0:T(8,128)S(1)}, u32[]{:S(2)}, u32[]{:S(2)}) %collective-permute-start.4) | collective-permute-done | bytes 65568 | tf_op jit(solution)/shard_map/ppermute | solution.py:169
  263.7 6.8 %all-to-all-start = ((bf16[16,32,256]{2,1,0:T(8,128)(2,1)}), bf16[16,32,256]{2,1,0:T(8,128)(2,1)S(1)}, u32[]{:S(2)}, u32[]{:S(2)}) async-start(bf16[16,32,256]{2,1,0:T(8,128)(2,1)} %broadcast_in_dim.21), calls=%async_computation | async-start | bytes 524288 | tf_op jit(solution)/shard_map/all_to_all | solution.py:176
  270.6 7.8 %all-to-all-done.after_ref.x_ref = bf16[16,32,256]{2,1,0:T(8,128)(2,1)S(1)} async-done(((bf16[16,32,256]{2,1,0:T(8,128)(2,1)}), bf16[16,32,256]{2,1,0:T(8,128)(2,1)S(1)}, u32[]{:S(2)}, u32[]{:S(2)}) %all-to-all-start) | async-done | bytes 262176 | tf_op jit(solution)/shard_map/all_to_all | solution.py:176
  278.3 3.6 load_half.2.g_ref
  282.0 2.5 down_product.7
  287.2 3.5 collective-permute-start.3
  290.7 3.7 load_half.3.g_ref
  294.4 10.6 %all_to_all.70.x_ref = bf16[16,32,256]{2,1,0:T(8,128)(2,1)S(1)} all-to-all(bf16[16,32,256]{2,1,0:T(8,128)(2,1)S(1)} %broadcast_in_dim.22), channel_id=1, replica_groups=mesh['sweep'=8,'layer'=16] {'layer'}, dimensions={0} | all-to-all | bytes 524288 | tf_op jit(solution)/shard_map/all_to_all | solution.py:176
  310.6 10.7 %all_to_all.71.x_ref = bf16[16,32,256]{2,1,0:T(8,128)(2,1)S(1)} all-to-all(bf16[16,32,256]{2,1,0:T(8,128)(2,1)S(1)} %broadcast_in_dim.23), channel_id=1, replica_groups=mesh['sweep'=8,'layer'=16] {'layer'}, dimensions={0} | all-to-all | bytes 524288 | tf_op jit(solution)/shard_map/all_to_all | solution.py:176
  321.3 2.5 down_product.9
  327.4 10.7 %all_to_all.72.x_ref = bf16[16,32,256]{2,1,0:T(8,128)(2,1)S(1)} all-to-all(bf16[16,32,256]{2,1,0:T(8,128)(2,1)S(1)} %broadcast_in_dim.24), channel_id=1, replica_groups=mesh['sweep'=8,'layer'=16] {'layer'}, dimensions={0} | all-to-all | bytes 524288 | tf_op jit(solution)/shard_map/all_to_all | solution.py:176
  343.5 10.7 %all_to_all.73.x_ref = bf16[16,32,256]{2,1,0:T(8,128)(2,1)S(1)} all-to-all(bf16[16,32,256]{2,1,0:T(8,128)(2,1)S(1)} %broadcast_in_dim.25), channel_id=1, replica_groups=mesh['sweep'=8,'layer'=16] {'layer'}, dimensions={0} | all-to-all | bytes 524288 | tf_op jit(solution)/shard_map/all_to_all | solution.py:176
  360.3 10.7 %all_to_all.74.x_ref = bf16[16,32,256]{2,1,0:T(8,128)(2,1)S(1)} all-to-all(bf16[16,32,256]{2,1,0:T(8,128)(2,1)S(1)} %broadcast_in_dim.26), channel_id=1, replica_groups=mesh['sweep'=8,'layer'=16] {'layer'}, dimensions={0} | all-to-all | bytes 524288 | tf_op jit(solution)/shard_map/all_to_all | solution.py:176
  376.5 10.7 %all_to_all.75.x_ref = bf16[16,32,256]{2,1,0:T(8,128)(2,1)S(1)} all-to-all(bf16[16,32,256]{2,1,0:T(8,128)(2,1)S(1)} %broadcast_in_dim.27), channel_id=1, replica_groups=mesh['sweep'=8,'layer'=16] {'layer'}, dimensions={0} | all-to-all | bytes 524288 | tf_op jit(solution)/shard_map/all_to_all | solution.py:176
  395.4 10.7 %all_to_all.76 = bf16[16,32,256]{2,1,0:T(8,128)(2,1)S(1)} all-to-all(bf16[16,32,256]{2,1,0:T(8,128)(2,1)S(1)} %up_product.7), channel_id=1, replica_groups=mesh['sweep'=8,'layer'=16] {'layer'}, dimensions={0} | all-to-all | bytes 524288 | tf_op jit(solution)/shard_map/all_to_all | solution.py:176
  411.2 10.7 %all_to_all.77 = bf16[16,32,256]{2,1,0:T(8,128)(2,1)S(1)} all-to-all(bf16[16,32,256]{2,1,0:T(8,128)(2,1)S(1)} %up_product.8), channel_id=1, replica_groups=mesh['sweep'=8,'layer'=16] {'layer'}, dimensions={0} | all-to-all | bytes 524288 | tf_op jit(solution)/shard_map/all_to_all | solution.py:176
  426.4 10.7 %all_to_all.78 = bf16[16,32,256]{2,1,0:T(8,128)(2,1)S(1)} all-to-all(bf16[16,32,256]{2,1,0:T(8,128)(2,1)S(1)} %up_product.9), channel_id=1, replica_groups=mesh['sweep'=8,'layer'=16] {'layer'}, dimensions={0} | all-to-all | bytes 524288 | tf_op jit(solution)/shard_map/all_to_all | solution.py:176
  442.2 10.7 %all_to_all.79 = bf16[16,32,256]{2,1,0:T(8,128)(2,1)S(1)} all-to-all(bf16[16,32,256]{2,1,0:T(8,128)(2,1)S(1)} %up_product.10), channel_id=1, replica_groups=mesh['sweep'=8,'layer'=16] {'layer'}, dimensions={0} | all-to-all | bytes 524288 | tf_op jit(solution)/shard_map/all_to_all | solution.py:176
  457.4 10.7 %all_to_all.80 = bf16[16,32,256]{2,1,0:T(8,128)(2,1)S(1)} all-to-all(bf16[16,32,256]{2,1,0:T(8,128)(2,1)S(1)} %up_product.11), channel_id=1, replica_groups=mesh['sweep'=8,'layer'=16] {'layer'}, dimensions={0} | all-to-all | bytes 524288 | tf_op jit(solution)/shard_map/all_to_all | solution.py:176
  468.2 19.6 %collective-permute-start.21 = (bf16[32,256]{1,0:T(8,128)(2,1)S(1)}, bf16[32,256]{1,0:T(8,128)(2,1)S(1)}, u32[]{:S(2)}, u32[]{:S(2)}) collective-permute-start(bf16[32,256]{1,0:T(8,128)(2,1)S(1)} %add_convert_fusion.3), channel_id=1, source_target_pairs={{32,0},{0,32},{48,16},{16,48},{33,1},{1,33},{49,17},{17,49},{34,2}... | collective-permute-start | bytes 49160 | tf_op jit(solution)/shard_map/ppermute | solution.py:173
  488.9 2.8 collective-permute-start.22
  494.0 10.7 %all_to_all.81 = bf16[16,32,256]{2,1,0:T(8,128)(2,1)S(1)} all-to-all(bf16[16,32,256]{2,1,0:T(8,128)(2,1)S(1)} %up_product.12), channel_id=1, replica_groups=mesh['sweep'=8,'layer'=16] {'layer'}, dimensions={0} | all-to-all | bytes 524288 | tf_op jit(solution)/shard_map/all_to_all | solution.py:176
  509.1 10.7 %all_to_all.82 = bf16[16,32,256]{2,1,0:T(8,128)(2,1)S(1)} all-to-all(bf16[16,32,256]{2,1,0:T(8,128)(2,1)S(1)} %up_product.13), channel_id=1, replica_groups=mesh['sweep'=8,'layer'=16] {'layer'}, dimensions={0} | all-to-all | bytes 524288 | tf_op jit(solution)/shard_map/all_to_all | solution.py:176
  (115 shorter events, 69.9 us)
Async XLA Ops:
  255.4 23.0 %collective-permute-start.1 = (bf16[2,512,4096]{2,1,0:T(8,128)(2,1)}, bf16[2,512,4096]{2,1,0:T(8,128)(2,1)}, u32[]{:S(2)}, u32[]{:S(2)}) collective-permute-start(bf16[2,512,4096]{2,1,0:T(8,128)(2,1)} %second_halves.1), channel_id=1, source_target_pairs={{0,16},{16,0},{32,48},{48,32},{64,80},{80,64},{96,112},{112,96},{1... | collective-permute-start | bytes 25165832 | tf_op jit(solution)/shard_map/ppermute | solution.py:169
  256.9 6.0 %collective-permute-start = (f32[32,256]{1,0:T(8,128)S(1)}, f32[32,256]{1,0:T(8,128)S(1)}, u32[]{:S(2)}, u32[]{:S(2)}) collective-permute-start(f32[32,256]{1,0:T(8,128)S(1)} %slice.51), channel_id=1, source_target_pairs={{0,16},{16,0},{32,48},{48,32},{64,80},{80,64},{96,112},{112,96},{1... | collective-permute-start | bytes 98312 | tf_op jit(solution)/shard_map/ppermute | solution.py:169
  257.0 5.9 %collective-permute-start.4 = (f32[32,512]{1,0:T(8,128)S(1)}, f32[32,512]{1,0:T(8,128)S(1)}, u32[]{:S(2)}, u32[]{:S(2)}) collective-permute-start(f32[32,512]{1,0:T(8,128)S(1)} %bitcast.24), channel_id=1, source_target_pairs={{0,16},{16,0},{32,48},{48,32},{64,80},{80,64},{96,112},{112,96},{1... | collective-permute-start | bytes 196616 | tf_op jit(solution)/shard_map/ppermute | solution.py:169
  263.7 14.6 %all-to-all-start = ((bf16[16,32,256]{2,1,0:T(8,128)(2,1)}), bf16[16,32,256]{2,1,0:T(8,128)(2,1)S(1)}, u32[]{:S(2)}, u32[]{:S(2)}) async-start(bf16[16,32,256]{2,1,0:T(8,128)(2,1)} %broadcast_in_dim.21), calls=%async_computation | async-start | bytes 524288 | tf_op jit(solution)/shard_map/all_to_all | solution.py:176
  284.5 2.6 collective-permute-start.2
  287.2 7.2 %collective-permute-start.3 = (bf16[32,256]{1,0:T(8,128)(2,1)S(1)}, bf16[32,256]{1,0:T(8,128)(2,1)S(1)}, u32[]{:S(2)}, u32[]{:S(2)}) collective-permute-start(bf16[32,256]{1,0:T(8,128)(2,1)S(1)} %get-tuple-element.68), channel_id=1, source_target_pairs={{0,32},{32,0},{16,48},{48,16},{1,33},{33,1},{17,49},{49,17},{2,34}... | collective-permute-start | bytes 49160 | tf_op jit(solution)/shard_map/ppermute | solution.py:173
  307.6 2.9 collective-permute-start.5
  323.8 2.8 collective-permute-start.6
  340.6 2.8 collective-permute-start.8
  356.8 2.8 collective-permute-start.9
  373.6 2.8 collective-permute-start.11
  389.7 2.8 collective-permute-start.13
  391.7 1.3 collective-permute-start.12
  392.6 1.3 collective-permute-start.14
  406.2 0.7 collective-permute-start.15
  406.9 2.8 collective-permute-start.16
  422.0 2.8 collective-permute-start.17
  437.2 0.7 collective-permute-start.18
  437.9 2.8 collective-permute-start.19
  453.0 2.8 collective-permute-start.20
  468.2 20.7 %collective-permute-start.21 = (bf16[32,256]{1,0:T(8,128)(2,1)S(1)}, bf16[32,256]{1,0:T(8,128)(2,1)S(1)}, u32[]{:S(2)}, u32[]{:S(2)}) collective-permute-start(bf16[32,256]{1,0:T(8,128)(2,1)S(1)} %add_convert_fusion.3), channel_id=1, source_target_pairs={{32,0},{0,32},{48,16},{16,48},{33,1},{1,33},{49,17},{17,49},{34,2}... | collective-permute-start | bytes 49160 | tf_op jit(solution)/shard_map/ppermute | solution.py:173
  488.9 3.6 collective-permute-start.22
  504.8 2.8 collective-permute-start.23
  520.0 2.8 collective-permute-start.24
  (4 other events, 515.2 us)

commit v3 on v2

--- a/solution.py
+++ b/solution.py
@@ -23,24 +23,37 @@
     parts, rows, cols = matrix.shape
     wide = cols // (2 * chips)
 
-    def body(matrix_ref, out_ref, sems):
-        copy_all(
-            [
-                pltpu.make_async_copy(
-                    matrix_ref.at[:, :, pl.ds((2 * i + 1) * wide, wide)],
-                    out_ref.at[:, :, pl.ds(i * wide, wide)],
-                    sems.at[i],
-                )
-                for i in range(chips)
-            ]
-        )
+    def body(matrix_ref, out_ref, held, in_sems, out_sems):
+        taken = [
+            pltpu.make_async_copy(
+                matrix_ref.at[:, :, pl.ds((2 * i + 1) * wide, wide)], held.at[i], in_sems.at[i]
+            )
+            for i in range(chips)
+        ]
+        put = [
+            pltpu.make_async_copy(
+                held.at[i], out_ref.at[:, :, pl.ds(i * wide, wide)], out_sems.at[i]
+            )
+            for i in range(chips)
+        ]
+        for copy in taken:
+            copy.start()
+        for i in range(chips):
+            taken[i].wait()
+            put[i].start()
+        for copy in put:
+            copy.wait()
 
     return pl.pallas_call(
         body,
         in_specs=[HBM],
         out_specs=HBM,
         out_shape=pltpu.HBM((parts, rows, cols // 2), BF16),
-        scratch_shapes=[pltpu.SemaphoreType.DMA((chips,))],
+        scratch_shapes=[
+            pltpu.VMEM((chips, parts, rows, wide), BF16),
+            pltpu.SemaphoreType.DMA((chips,)),
+            pltpu.SemaphoreType.DMA((chips,)),
+        ],
         compiler_params=pltpu.CompilerParams(vmem_limit_bytes=56 * MIB),
         name="second_halves",
     )(matrix)
@@ -177,16 +190,14 @@
 
     down_own = down_source.reshape(rhs, rows)
     down_got = swap(down_own[:, :wide])
-    received = swap(second_halves(matrix, chips))
+    tie = lambda *values: lax.optimization_barrier(values)
+    sent, down_got = tie(second_halves(matrix, chips), down_got)
+    received = swap(sent)
     base_a = jnp.where(on_0, down_own[:, wide:], down_got)
     base_b = jnp.where(on_0, down_got, down_own[:, wide:])
     up_own = up_source.reshape(rhs, rows)
-    up_other = swap(up_own)
-    up_a = jnp.where(on_0, up_own[:, :wide], up_other[:, wide:])
-    up_b_rest = jnp.where(on_0, up_other[:, :wide], up_own[:, wide:])
 
     core = (me % 2).astype(jnp.int32).reshape(1)
-    tie = lambda *values: lax.optimization_barrier(values)
 
     flops = 8 * rhs * rows * cols // 2
     part = jax.ShapeDtypeStruct((rhs, wide), F32)
@@ -214,6 +225,10 @@
         if p > 0:
             if p == 1:
                 matrix_a = load_half(core, 0, matrix, received, x, chips)
+                x, up_own = tie(x, up_own)
+                up_other = swap(up_own)
+                up_a = jnp.where(on_0, up_own[:, :wide], up_other[:, wide:])
+                up_b_rest = jnp.where(on_0, up_other[:, :wide], up_own[:, wide:])
             x = hop(x.astype(BF16), p - 1, p)
             if p == 1:
                 x, matrix_a, up_a, up_b_rest = tie(x, matrix_a, up_a, up_b_rest)

time: 524 us -> 271 us (0.52)
  Pallas kernels: 291 us -> 42.8 us
  waiting for transfers between devices: 27 us -> 21.3 us
    pallas_call x1, Pallas kernels: 255 us -> 6.93 us  [second_halves(): pl.pallas_call(body, in_specs=[HBM], out_specs=HBM, out_shape=pltpu.HBM((...]
    ppermute x19, waiting for transfers between devices: 18.1 us -> 12.7 us  [swap(): return lax.ppermute(x, 'sweep', [(i, i ^ 1) for i in range(2 * planes)])]
  transfers between devices with their start and end apart: 26 -> 26, of which waited for: 18 -> 17; matrix products, arithmetic and copies ran while one was open for 0% -> 0% of each run, Pallas kernels for 1% -> 4%
where the time goes in v3:
time: 271 us; the launch traced here: 270 us
  blocking collectives  139 us (51%)
  starting transfers between devices  63.5 us (23%)
  Pallas kernels  42.8 us (16%)
  waiting for transfers between devices  21.3 us (8%)
    all_to_all x13, blocking collectives, exchange(): return lax.all_to_all(blocks, 'layer', 0, 0, tiled=True)  139 us
    ppermute x19, starting transfers between devices, swap(): return lax.ppermute(x, 'sweep', [(i, i ^ 1) for i in range(2 * planes)])  30.9 us
    pallas_call x14, Pallas kernels, call(): pl.pallas_call(body, in_specs=[VMEM] * len(args), out_specs=jax.tree.map(...  28.5 us
    ppermute x6, starting transfers between devices, hop(): return lax.ppermute(x, 'sweep', pairs)  25.7 us
    ppermute x19, waiting for transfers between devices, swap(): return lax.ppermute(x, 'sweep', [(i, i ^ 1) for i in range(2 * planes)])  12.7 us
    all_to_all x1, waiting for transfers between devices, exchange(): return lax.all_to_all(blocks, 'layer', 0, 0, tiled=True)  7.46 us
    pallas_call x2, Pallas kernels, load_half(): pl.pallas_call(body, in_specs=[SMEM, HBM, HBM, VMEM], out_specs=VMEM, out...  7.32 us
    pallas_call x1, Pallas kernels, second_halves(): pl.pallas_call(body, in_specs=[HBM], out_specs=HBM, out_shape=pltpu.HBM((...  6.93 us
  transfers between devices with their start and end apart: 26, of which 17 were waited for; matrix products, arithmetic and copies ran while one was open for 0% of the time, Pallas kernels for 4%

profile of v3, /device:TPU:1, one launch (start us, length us, event | category | flops | bytes accessed | tf_op | source)
XLA Modules:
  0.0 270.3 jit_solution(10691117619975431168)
XLA Ops:
  2.2 6.9 %second_halves.1 = bf16[2,512,4096]{2,1,0:T(8,128)(2,1)} custom-call(bf16[2,512,8192]{2,1,0:T(8,128)(2,1)} %bitcast.21), custom_call_target="tpu_custom_call" | custom-call | tf_op jit(solution)/shard_map/second_halves/pallas_call | solution.py:47
  10.1 6.8 %all-to-all-start = ((bf16[16,32,256]{2,1,0:T(8,128)(2,1)}), bf16[16,32,256]{2,1,0:T(8,128)(2,1)S(1)}, u32[]{:S(2)}, u32[]{:S(2)}) async-start(bf16[16,32,256]{2,1,0:T(8,128)(2,1)} %broadcast_in_dim.21), calls=%async_computation | async-start | bytes 524288 | tf_op jit(solution)/shard_map/all_to_all | solution.py:189
  17.0 7.5 %all-to-all-done.after_ref.x_ref = bf16[16,32,256]{2,1,0:T(8,128)(2,1)S(1)} async-done(((bf16[16,32,256]{2,1,0:T(8,128)(2,1)}), bf16[16,32,256]{2,1,0:T(8,128)(2,1)S(1)}, u32[]{:S(2)}, u32[]{:S(2)}) %all-to-all-start) | async-done | bytes 262176 | tf_op jit(solution)/shard_map/all_to_all | solution.py:189
  24.4 3.6 %load_half.2.g_ref = bf16[2,512,4096]{2,1,0:T(8,128)(2,1)S(1)} custom-call(s32[1]{0:T(128)} %bitcast.9.core_ref, bf16[2,512,8192]{2,1,0:T(8,128)(2,1)} %bitcast.22, bf16[2,512,4096]{2,1,0:T(8,128)(2,1)} %collective-permute-done.1.received_ref, bf16[16,32,256]{2,1,0:T(8,128)(2,1)S(1)} %all-to-all-done.after_ref.x_ref), custom_call_target="tpu_custom_call" | custom-call | tf_op jit(solution)/shard_map/load_half/pallas_call | solution.py:93
  28.1 2.5 down_product.7
  34.0 3.5 %collective-permute-start.3 = (bf16[32,256]{1,0:T(8,128)(2,1)S(1)}, bf16[32,256]{1,0:T(8,128)(2,1)S(1)}, u32[]{:S(2)}, u32[]{:S(2)}) collective-permute-start(bf16[32,256]{1,0:T(8,128)(2,1)S(1)} %convert_element_type.70), channel_id=1, source_target_pairs={{0,32},{32,0},{16,48},{48,16},{1,33},{33,1},{17,49},{49,17},{2,34}... | collective-permute-start | bytes 49160 | tf_op jit(solution)/shard_map/ppermute | solution.py:186
  37.5 3.7 %load_half.3.g_ref = bf16[2,512,4096]{2,1,0:T(8,128)(2,1)S(1)} custom-call(s32[1]{0:T(128)} %bitcast.9.core_ref, bf16[2,512,8192]{2,1,0:T(8,128)(2,1)} %bitcast.23, bf16[2,512,4096]{2,1,0:T(8,128)(2,1)} %collective-permute-done.1.received_ref, f32[32,256]{1,0:T(8,128)S(1)} %add.53.after_ref), custom_call_target="tpu_custom_call" | custom-call | tf_op jit(solution)/shard_map/load_half/pallas_call | solution.py:93
  41.3 10.6 %all_to_all.70.x_ref = bf16[16,32,256]{2,1,0:T(8,128)(2,1)S(1)} all-to-all(bf16[16,32,256]{2,1,0:T(8,128)(2,1)S(1)} %broadcast_in_dim.22), channel_id=1, replica_groups=mesh['sweep'=8,'layer'=16] {'layer'}, dimensions={0} | all-to-all | bytes 524288 | tf_op jit(solution)/shard_map/all_to_all | solution.py:189
  51.9 2.5 down_product.8
  57.4 10.7 %all_to_all.71.x_ref = bf16[16,32,256]{2,1,0:T(8,128)(2,1)S(1)} all-to-all(bf16[16,32,256]{2,1,0:T(8,128)(2,1)S(1)} %broadcast_in_dim.23), channel_id=1, replica_groups=mesh['sweep'=8,'layer'=16] {'layer'}, dimensions={0} | all-to-all | bytes 524288 | tf_op jit(solution)/shard_map/all_to_all | solution.py:189
  74.2 10.7 %all_to_all.72.x_ref = bf16[16,32,256]{2,1,0:T(8,128)(2,1)S(1)} all-to-all(bf16[16,32,256]{2,1,0:T(8,128)(2,1)S(1)} %broadcast_in_dim.24), channel_id=1, replica_groups=mesh['sweep'=8,'layer'=16] {'layer'}, dimensions={0} | all-to-all | bytes 524288 | tf_op jit(solution)/shard_map/all_to_all | solution.py:189
  90.4 10.7 %all_to_all.73.x_ref = bf16[16,32,256]{2,1,0:T(8,128)(2,1)S(1)} all-to-all(bf16[16,32,256]{2,1,0:T(8,128)(2,1)S(1)} %broadcast_in_dim.25), channel_id=1, replica_groups=mesh['sweep'=8,'layer'=16] {'layer'}, dimensions={0} | all-to-all | bytes 524288 | tf_op jit(solution)/shard_map/all_to_all | solution.py:189
  101.1 2.5 down_product.11
  107.2 10.7 %all_to_all.74.x_ref = bf16[16,32,256]{2,1,0:T(8,128)(2,1)S(1)} all-to-all(bf16[16,32,256]{2,1,0:T(8,128)(2,1)S(1)} %broadcast_in_dim.26), channel_id=1, replica_groups=mesh['sweep'=8,'layer'=16] {'layer'}, dimensions={0} | all-to-all | bytes 524288 | tf_op jit(solution)/shard_map/all_to_all | solution.py:189
  123.3 10.7 %all_to_all.75.x_ref = bf16[16,32,256]{2,1,0:T(8,128)(2,1)S(1)} all-to-all(bf16[16,32,256]{2,1,0:T(8,128)(2,1)S(1)} %broadcast_in_dim.27), channel_id=1, replica_groups=mesh['sweep'=8,'layer'=16] {'layer'}, dimensions={0} | all-to-all | bytes 524288 | tf_op jit(solution)/shard_map/all_to_all | solution.py:189
  142.3 10.7 %all_to_all.76 = bf16[16,32,256]{2,1,0:T(8,128)(2,1)S(1)} all-to-all(bf16[16,32,256]{2,1,0:T(8,128)(2,1)S(1)} %up_product.7), channel_id=1, replica_groups=mesh['sweep'=8,'layer'=16] {'layer'}, dimensions={0} | all-to-all | bytes 524288 | tf_op jit(solution)/shard_map/all_to_all | solution.py:189
  158.1 10.7 %all_to_all.77 = bf16[16,32,256]{2,1,0:T(8,128)(2,1)S(1)} all-to-all(bf16[16,32,256]{2,1,0:T(8,128)(2,1)S(1)} %up_product.8), channel_id=1, replica_groups=mesh['sweep'=8,'layer'=16] {'layer'}, dimensions={0} | all-to-all | bytes 524288 | tf_op jit(solution)/shard_map/all_to_all | solution.py:189
  173.3 10.7 %all_to_all.78 = bf16[16,32,256]{2,1,0:T(8,128)(2,1)S(1)} all-to-all(bf16[16,32,256]{2,1,0:T(8,128)(2,1)S(1)} %up_product.9), channel_id=1, replica_groups=mesh['sweep'=8,'layer'=16] {'layer'}, dimensions={0} | all-to-all | bytes 524288 | tf_op jit(solution)/shard_map/all_to_all | solution.py:189
  189.1 10.7 %all_to_all.79 = bf16[16,32,256]{2,1,0:T(8,128)(2,1)S(1)} all-to-all(bf16[16,32,256]{2,1,0:T(8,128)(2,1)S(1)} %up_product.10), channel_id=1, replica_groups=mesh['sweep'=8,'layer'=16] {'layer'}, dimensions={0} | all-to-all | bytes 524288 | tf_op jit(solution)/shard_map/all_to_all | solution.py:189
  204.2 10.7 %all_to_all.80 = bf16[16,32,256]{2,1,0:T(8,128)(2,1)S(1)} all-to-all(bf16[16,32,256]{2,1,0:T(8,128)(2,1)S(1)} %up_product.11), channel_id=1, replica_groups=mesh['sweep'=8,'layer'=16] {'layer'}, dimensions={0} | all-to-all | bytes 524288 | tf_op jit(solution)/shard_map/all_to_all | solution.py:189
  215.0 19.6 %collective-permute-start.21 = (bf16[32,256]{1,0:T(8,128)(2,1)S(1)}, bf16[32,256]{1,0:T(8,128)(2,1)S(1)}, u32[]{:S(2)}, u32[]{:S(2)}) collective-permute-start(bf16[32,256]{1,0:T(8,128)(2,1)S(1)} %add_convert_fusion.3), channel_id=1, source_target_pairs={{32,0},{0,32},{48,16},{16,48},{33,1},{1,33},{49,17},{17,49},{34,2}... | collective-permute-start | bytes 49160 | tf_op jit(solution)/shard_map/ppermute | solution.py:186
  235.7 2.8 %collective-permute-start.22 = (bf16[32,256]{1,0:T(8,128)(2,1)S(1)}, bf16[32,256]{1,0:T(8,128)(2,1)S(1)}, u32[]{:S(2)}, u32[]{:S(2)}) collective-permute-start(bf16[32,256]{1,0:T(8,128)(2,1)S(1)} %collective-permute-done.21), channel_id=1, source_target_pairs={{0,16},{16,0},{32,48},{48,32},{64,80},{80,64},{96,112},{112,96},{1... | collective-permute-start | bytes 49160 | tf_op jit(solution)/shard_map/ppermute | solution.py:182
  240.9 10.7 %all_to_all.81 = bf16[16,32,256]{2,1,0:T(8,128)(2,1)S(1)} all-to-all(bf16[16,32,256]{2,1,0:T(8,128)(2,1)S(1)} %up_product.12), channel_id=1, replica_groups=mesh['sweep'=8,'layer'=16] {'layer'}, dimensions={0} | all-to-all | bytes 524288 | tf_op jit(solution)/shard_map/all_to_all | solution.py:189
  256.0 10.7 %all_to_all.82 = bf16[16,32,256]{2,1,0:T(8,128)(2,1)S(1)} all-to-all(bf16[16,32,256]{2,1,0:T(8,128)(2,1)S(1)} %up_product.13), channel_id=1, replica_groups=mesh['sweep'=8,'layer'=16] {'layer'}, dimensions={0} | all-to-all | bytes 524288 | tf_op jit(solution)/shard_map/all_to_all | solution.py:189
  (117 shorter events, 68.3 us)
Async XLA Ops:
  0.8 8.4 %collective-permute-start = (f32[32,256]{1,0:T(8,128)S(1)}, f32[32,256]{1,0:T(8,128)S(1)}, u32[]{:S(2)}, u32[]{:S(2)}) collective-permute-start(f32[32,256]{1,0:T(8,128)S(1)} %slice.51), channel_id=1, source_target_pairs={{0,16},{16,0},{32,48},{48,32},{64,80},{80,64},{96,112},{112,96},{1... | collective-permute-start | bytes 98312 | tf_op jit(solution)/shard_map/ppermute | solution.py:182
  9.1 15.3 %collective-permute-start.1 = (bf16[2,512,4096]{2,1,0:T(8,128)(2,1)}, bf16[2,512,4096]{2,1,0:T(8,128)(2,1)}, u32[]{:S(2)}, u32[]{:S(2)}) collective-permute-start(bf16[2,512,4096]{2,1,0:T(8,128)(2,1)} %second_halves.1), channel_id=1, source_target_pairs={{0,16},{16,0},{32,48},{48,32},{64,80},{80,64},{96,112},{112,96},{1... | collective-permute-start | bytes 25165832 | tf_op jit(solution)/shard_map/ppermute | solution.py:182
  10.1 14.3 %all-to-all-start = ((bf16[16,32,256]{2,1,0:T(8,128)(2,1)}), bf16[16,32,256]{2,1,0:T(8,128)(2,1)S(1)}, u32[]{:S(2)}, u32[]{:S(2)}) async-start(bf16[16,32,256]{2,1,0:T(8,128)(2,1)} %broadcast_in_dim.21), calls=%async_computation | async-start | bytes 524288 | tf_op jit(solution)/shard_map/all_to_all | solution.py:189
  30.6 2.9 %collective-permute-start.2 = (f32[32,256]{1,0:T(8,128)S(1)}, f32[32,256]{1,0:T(8,128)S(1)}, u32[]{:S(2)}, u32[]{:S(2)}) collective-permute-start(f32[32,256]{1,0:T(8,128)S(1)} %get-tuple-element.45), channel_id=1, source_target_pairs={{0,16},{16,0},{32,48},{48,32},{64,80},{80,64},{96,112},{112,96},{1... | collective-permute-start | bytes 98312 | tf_op jit(solution)/shard_map/ppermute | solution.py:182
  33.6 7.7 %collective-permute-start.4 = (f32[32,512]{1,0:T(8,128)S(1)}, f32[32,512]{1,0:T(8,128)S(1)}, u32[]{:S(2)}, u32[]{:S(2)}) collective-permute-start(f32[32,512]{1,0:T(8,128)S(1)} %bitcast.27), channel_id=1, source_target_pairs={{0,16},{16,0},{32,48},{48,32},{64,80},{80,64},{96,112},{112,96},{1... | collective-permute-start | bytes 196616 | tf_op jit(solution)/shard_map/ppermute | solution.py:182
  34.0 7.3 %collective-permute-start.3 = (bf16[32,256]{1,0:T(8,128)(2,1)S(1)}, bf16[32,256]{1,0:T(8,128)(2,1)S(1)}, u32[]{:S(2)}, u32[]{:S(2)}) collective-permute-start(bf16[32,256]{1,0:T(8,128)(2,1)S(1)} %convert_element_type.70), channel_id=1, source_target_pairs={{0,32},{32,0},{16,48},{48,16},{1,33},{33,1},{17,49},{49,17},{2,34}... | collective-permute-start | bytes 49160 | tf_op jit(solution)/shard_map/ppermute | solution.py:186
  54.5 2.9 %collective-permute-start.5 = (f32[32,256]{1,0:T(8,128)S(1)}, f32[32,256]{1,0:T(8,128)S(1)}, u32[]{:S(2)}, u32[]{:S(2)}) collective-permute-start(f32[32,256]{1,0:T(8,128)S(1)} %get-tuple-element.54), channel_id=1, source_target_pairs={{0,16},{16,0},{32,48},{48,32},{64,80},{80,64},{96,112},{112,96},{1... | collective-permute-start | bytes 98312 | tf_op jit(solution)/shard_map/ppermute | solution.py:182
  70.7 2.8 %collective-permute-start.6 = (f32[32,256]{1,0:T(8,128)S(1)}, f32[32,256]{1,0:T(8,128)S(1)}, u32[]{:S(2)}, u32[]{:S(2)}) collective-permute-start(f32[32,256]{1,0:T(8,128)S(1)} %get-tuple-element.56), channel_id=1, source_target_pairs={{0,16},{16,0},{32,48},{48,32},{64,80},{80,64},{96,112},{112,96},{1... | collective-permute-start | bytes 98312 | tf_op jit(solution)/shard_map/ppermute | solution.py:182
  87.5 2.8 %collective-permute-start.8 = (f32[32,256]{1,0:T(8,128)S(1)}, f32[32,256]{1,0:T(8,128)S(1)}, u32[]{:S(2)}, u32[]{:S(2)}) collective-permute-start(f32[32,256]{1,0:T(8,128)S(1)} %get-tuple-element.58), channel_id=1, source_target_pairs={{0,16},{16,0},{32,48},{48,32},{64,80},{80,64},{96,112},{112,96},{1... | collective-permute-start | bytes 98312 | tf_op jit(solution)/shard_map/ppermute | solution.py:182
  103.7 2.8 %collective-permute-start.9 = (f32[32,256]{1,0:T(8,128)S(1)}, f32[32,256]{1,0:T(8,128)S(1)}, u32[]{:S(2)}, u32[]{:S(2)}) collective-permute-start(f32[32,256]{1,0:T(8,128)S(1)} %get-tuple-element.60), channel_id=1, source_target_pairs={{0,16},{16,0},{32,48},{48,32},{64,80},{80,64},{96,112},{112,96},{1... | collective-permute-start | bytes 98312 | tf_op jit(solution)/shard_map/ppermute | solution.py:182
  120.5 2.8 %collective-permute-start.11 = (f32[32,256]{1,0:T(8,128)S(1)}, f32[32,256]{1,0:T(8,128)S(1)}, u32[]{:S(2)}, u32[]{:S(2)}) collective-permute-start(f32[32,256]{1,0:T(8,128)S(1)} %get-tuple-element.62), channel_id=1, source_target_pairs={{0,16},{16,0},{32,48},{48,32},{64,80},{80,64},{96,112},{112,96},{1... | collective-permute-start | bytes 98312 | tf_op jit(solution)/shard_map/ppermute | solution.py:182
  136.6 2.8 %collective-permute-start.13 = (f32[32,256]{1,0:T(8,128)S(1)}, f32[32,256]{1,0:T(8,128)S(1)}, u32[]{:S(2)}, u32[]{:S(2)}) collective-permute-start(f32[32,256]{1,0:T(8,128)S(1)} %get-tuple-element.67), channel_id=1, source_target_pairs={{0,16},{16,0},{32,48},{48,32},{64,80},{80,64},{96,112},{112,96},{1... | collective-permute-start | bytes 98312 | tf_op jit(solution)/shard_map/ppermute | solution.py:182
  138.6 1.3 collective-permute-start.12
  139.5 1.3 collective-permute-start.14
  153.1 0.7 collective-permute-start.15
  153.8 2.8 %collective-permute-start.16 = (bf16[32,256]{1,0:T(8,128)(2,1)S(1)}, bf16[32,256]{1,0:T(8,128)(2,1)S(1)}, u32[]{:S(2)}, u32[]{:S(2)}) collective-permute-start(bf16[32,256]{1,0:T(8,128)(2,1)S(1)} %collective-permute-done.15), channel_id=1, source_target_pairs={{0,16},{16,0},{32,48},{48,32},{64,80},{80,64},{96,112},{112,96},{1... | collective-permute-start | bytes 49160 | tf_op jit(solution)/shard_map/ppermute | solution.py:182
  168.9 2.8 %collective-permute-start.17 = (bf16[32,256]{1,0:T(8,128)(2,1)S(1)}, bf16[32,256]{1,0:T(8,128)(2,1)S(1)}, u32[]{:S(2)}, u32[]{:S(2)}) collective-permute-start(bf16[32,256]{1,0:T(8,128)(2,1)S(1)} %add_convert_fusion), channel_id=1, source_target_pairs={{0,16},{16,0},{32,48},{48,32},{64,80},{80,64},{96,112},{112,96},{1... | collective-permute-start | bytes 49160 | tf_op jit(solution)/shard_map/ppermute | solution.py:182
  184.1 0.7 collective-permute-start.18
  184.7 2.8 %collective-permute-start.19 = (bf16[32,256]{1,0:T(8,128)(2,1)S(1)}, bf16[32,256]{1,0:T(8,128)(2,1)S(1)}, u32[]{:S(2)}, u32[]{:S(2)}) collective-permute-start(bf16[32,256]{1,0:T(8,128)(2,1)S(1)} %collective-permute-done.18), channel_id=1, source_target_pairs={{0,16},{16,0},{32,48},{48,32},{64,80},{80,64},{96,112},{112,96},{1... | collective-permute-start | bytes 49160 | tf_op jit(solution)/shard_map/ppermute | solution.py:182
  199.9 2.8 %collective-permute-start.20 = (bf16[32,256]{1,0:T(8,128)(2,1)S(1)}, bf16[32,256]{1,0:T(8,128)(2,1)S(1)}, u32[]{:S(2)}, u32[]{:S(2)}) collective-permute-start(bf16[32,256]{1,0:T(8,128)(2,1)S(1)} %add_convert_fusion.4), channel_id=1, source_target_pairs={{0,16},{16,0},{32,48},{48,32},{64,80},{80,64},{96,112},{112,96},{1... | collective-permute-start | bytes 49160 | tf_op jit(solution)/shard_map/ppermute | solution.py:182
  215.0 20.7 %collective-permute-start.21 = (bf16[32,256]{1,0:T(8,128)(2,1)S(1)}, bf16[32,256]{1,0:T(8,128)(2,1)S(1)}, u32[]{:S(2)}, u32[]{:S(2)}) collective-permute-start(bf16[32,256]{1,0:T(8,128)(2,1)S(1)} %add_convert_fusion.3), channel_id=1, source_target_pairs={{32,0},{0,32},{48,16},{16,48},{33,1},{1,33},{49,17},{17,49},{34,2}... | collective-permute-start | bytes 49160 | tf_op jit(solution)/shard_map/ppermute | solution.py:186
  235.7 3.6 %collective-permute-start.22 = (bf16[32,256]{1,0:T(8,128)(2,1)S(1)}, bf16[32,256]{1,0:T(8,128)(2,1)S(1)}, u32[]{:S(2)}, u32[]{:S(2)}) collective-permute-start(bf16[32,256]{1,0:T(8,128)(2,1)S(1)} %collective-permute-done.21), channel_id=1, source_target_pairs={{0,16},{16,0},{32,48},{48,32},{64,80},{80,64},{96,112},{112,96},{1... | collective-permute-start | bytes 49160 | tf_op jit(solution)/shard_map/ppermute | solution.py:182
  251.7 2.8 %collective-permute-start.23 = (bf16[32,256]{1,0:T(8,128)(2,1)S(1)}, bf16[32,256]{1,0:T(8,128)(2,1)S(1)}, u32[]{:S(2)}, u32[]{:S(2)}) collective-permute-start(bf16[32,256]{1,0:T(8,128)(2,1)S(1)} %add_convert_fusion.2), channel_id=1, source_target_pairs={{0,16},{16,0},{32,48},{48,32},{64,80},{80,64},{96,112},{112,96},{1... | collective-permute-start | bytes 49160 | tf_op jit(solution)/shard_map/ppermute | solution.py:182
  266.9 2.8 %collective-permute-start.24 = (f32[32,256]{1,0:T(8,128)S(1)}, f32[32,256]{1,0:T(8,128)S(1)}, u32[]{:S(2)}, u32[]{:S(2)}) collective-permute-start(f32[32,256]{1,0:T(8,128)S(1)} %select_n.145), channel_id=1, source_target_pairs={{0,16},{16,0},{32,48},{48,32},{64,80},{80,64},{96,112},{112,96},{1... | collective-permute-start | bytes 98312 | tf_op jit(solution)/shard_map/ppermute | solution.py:182
  (4 other events, 14.0 us)

commit v4 on v3

v4 whole, which is shorter than its diff:
```python
import jax
import jax.numpy as jnp
from jax import lax
from jax.experimental import pallas as pl
from jax.experimental.pallas import tpu as pltpu
from jax.sharding import PartitionSpec as P

F32, BF16 = jnp.float32, jnp.bfloat16
MIB = 1 << 20
VMEM = pl.BlockSpec(memory_space=pltpu.VMEM)
HBM = pl.BlockSpec(memory_space=pltpu.HBM)
SMEM = pl.BlockSpec(memory_space=pltpu.SMEM)


def down_sums(x, g, sums):
    contract = (((1,), (1,)), ((), ()))
    r = lax.dot_general(x, g[0], contract, preferred_element_type=F32)
    m = lax.dot_general(x, g[1], contract, preferred_element_type=F32)
    return (r, m) if sums is None else (sums[0] + r, sums[1] + m)


def complex_of(sums, n):
    with_real, with_imag = sums
    return with_real[:n] - with_imag[n:], with_imag[:n] + with_real[n:]


def write_down(sums, first_ref, base_ref, mine_ref, theirs_ref):
    n, wide = base_ref.shape[0] // 2, base_ref.shape[1]
    real, imag = complex_of(sums, n)
    first = jnp.concatenate([real[:, :wide], imag[:, :wide]], axis=0)
    second = jnp.concatenate([real[:, wide:], imag[:, wide:]], axis=0)
    keeps_first = first_ref[0:1, 0:1] == 1
    mine_ref[...] = jnp.where(keeps_first, first, second) + base_ref[...]
    theirs_ref[...] = jnp.where(keeps_first, second, first)


def whole_product(blocks, matrix):
    chips, rhs, wide = blocks.shape
    parts, rows, cols = matrix.shape

    def body(x_ref, matrix_ref, out_ref, held, sems):
        copies = [
            pltpu.make_async_copy(matrix_ref.at[:, :, pl.ds(i * wide, wide)], held.at[i], sems.at[i])
            for i in range(chips)
        ]
        for copy in copies:
            copy.start()
        sums = None
        for i in range(chips):
            copies[i].wait()
            sums = down_sums(x_ref[i], held.at[i], sums)
        out_ref[...] = jnp.concatenate(complex_of(sums, rhs // 2), axis=0)

    return pl.pallas_call(
        body,
        in_specs=[VMEM, HBM],
        out_specs=VMEM,
        out_shape=jax.ShapeDtypeStruct((rhs, rows), F32),
        scratch_shapes=[
            pltpu.VMEM((chips, parts, rows, wide), BF16),
            pltpu.SemaphoreType.DMA((chips,)),
        ],
        compiler_params=pltpu.CompilerParams(vmem_limit_bytes=56 * MIB),
        cost_estimate=pl.CostEstimate(
            flops=8 * rhs * rows * cols, bytes_accessed=2 * parts * rows * cols, transcendentals=0
        ),
        name="whole_product",
    )(blocks, matrix)


def load_product(me, on_core, matrix, received, blocks, keeps_first, base):
    chips, rhs, wide = blocks.shape
    parts, rows, cols = matrix.shape

    def body(me_ref, matrix_ref, received_ref, x_ref, first_ref, base_ref, mine_ref, theirs_ref, out_ref, sems):
        def copy(source_ref, at, i):
            here = pl.ds(i * wide, wide)
            return pltpu.make_async_copy(source_ref.at[:, :, pl.ds(at, wide)], out_ref.at[:, :, here], sems.at[i])

        @pl.when(me_ref[0] % 2 == on_core)
        def _():
            for i in range(chips):
                copy(matrix_ref, 2 * i * wide, i).start()

        @pl.when(me_ref[0] % 2 != on_core)
        def _():
            for i in range(chips):
                copy(received_ref, (2 * i + 1) * wide, i).start()

        sums = None
        for i in range(chips):
            copy(received_ref, i * wide, i).wait()
            sums = down_sums(x_ref[i], out_ref.at[:, :, pl.ds(i * wide, wide)], sums)
        write_down(sums, first_ref, base_ref, mine_ref, theirs_ref)

    part = jax.ShapeDtypeStruct((rhs, wide), F32)
    return pl.pallas_call(
        body,
        in_specs=[SMEM, HBM, HBM, VMEM, VMEM, VMEM],
        out_specs=[VMEM, VMEM, VMEM],
        out_shape=[part, part, pltpu.VMEM((parts, rows, cols // 2), BF16)],
        scratch_shapes=[pltpu.SemaphoreType.DMA((chips,))],
        compiler_params=pltpu.CompilerParams(vmem_limit_bytes=40 * MIB),
        cost_estimate=pl.CostEstimate(
            flops=4 * rhs * rows * cols, bytes_accessed=parts * rows * cols, transcendentals=0
        ),
        name="load_product",
    )(me, matrix, received, blocks, keeps_first, base)


def vmem_call(body, out_shape, name, flops):
    def call(*args):
        return pl.pallas_call(
            body,
            in_specs=[VMEM] * len(args),
            out_specs=jax.tree.map(lambda _: VMEM, out_shape),
            out_shape=out_shape,
            compiler_params=pltpu.CompilerParams(vmem_limit_bytes=8 * MIB),
            cost_estimate=pl.CostEstimate(flops=flops, bytes_accessed=1 << 16, transcendentals=0),
            name=name,
        )(*args)

    return call


def down_body(x_ref, g_ref, first_ref, base_ref, mine_ref, theirs_ref):
    chips, rhs, wide = x_ref.shape
    sums = None
    for i in range(chips):
        sums = down_sums(x_ref[i], g_ref.at[:, :, pl.ds(i * wide, wide)], sums)
    write_down(sums, first_ref, base_ref, mine_ref, theirs_ref)


def up_body(x_ref, g_ref, out_ref):
    chips, rhs, wide = out_ref.shape
    n = rhs // 2
    x = x_ref[...]
    for i in range(chips):
        at = slice(i * wide, (i + 1) * wide)
        r = jnp.dot(x, g_ref[0, :, at], preferred_element_type=F32)
        m = jnp.dot(x, g_ref[1, :, at], preferred_element_type=F32)
        out_ref[i, :n] = (r[:n] - m[n:]).astype(BF16)
        out_ref[i, n:] = (m[:n] + r[n:]).astype(BF16)


def make_masks(me, count, shape):
    def body(me_ref, out_ref):
        index = me_ref[0]
        for p in range(count):
            out_ref[p] = jnp.full(shape, jnp.where(index // 2 == p, 1, 0), jnp.int32)
        out_ref[count] = jnp.full(shape, jnp.where(index % 2 == 0, 1, 0), jnp.int32)

    return pl.pallas_call(
        body,
        in_specs=[SMEM],
        out_specs=VMEM,
        out_shape=pltpu.VMEM((count + 1, *shape), jnp.int32),
        name="make_masks",
    )(me)


def local(green, down_source, up_source):
    planes = lax.axis_size("sweep") // 2
    chips = lax.axis_size("layer")
    matrix = green[0]
    rows, cols = matrix.shape[1:]
    wide = rows // 2
    rhs = 2 * down_source.shape[2]

    def swap(x):
        return lax.ppermute(x, "sweep", [(i, i ^ 1) for i in range(2 * planes)])

    def trade(x, pairs):
        return lax.ppermute(x, "sweep", [p for a, b in pairs for p in ((a, b), (b, a))])

    def hop(x, a, b):
        return trade(x, [(2 * a + c, 2 * b + c) for c in range(2)])

    def hop_across(x, a, b):
        return trade(x, [(2 * a + c, 2 * b + 1 - c) for c in range(2)])

    def exchange(blocks):
        return lax.all_to_all(blocks, "layer", 0, 0, tiled=True)

    def spread(x):
        return exchange(jnp.broadcast_to(x.astype(BF16), (chips, *x.shape)))

    tie = lambda *values: lax.optimization_barrier(values)
    me = lax.axis_index("sweep").astype(jnp.int32).reshape(1)
    masks = make_masks(me, planes, (rhs, wide))
    tile_0 = masks[planes, :8, :128]
    tile_1 = 1 - tile_0
    masks = [masks[p] == 1 for p in range(planes + 1)]
    on_0 = masks.pop()

    flops = 4 * rhs * rows * cols
    part = jax.ShapeDtypeStruct((rhs, wide), F32)
    down_call = vmem_call(down_body, (part, part), "down_product", flops)
    up_call = vmem_call(up_body, jax.ShapeDtypeStruct((chips, rhs, wide), BF16), "up_product", flops)

    def up_product(x, other, first_on_0, mat, base):
        x, other = x.astype(BF16), other.astype(BF16)
        halves = [jnp.where(on_0, x, other), jnp.where(on_0, other, x)]
        full = jnp.concatenate(halves if first_on_0 else halves[::-1], axis=1)
        blocks = exchange(up_call(full, mat))
        return base + jnp.sum(blocks.astype(F32), axis=0)

    down_own, up_own = down_source.reshape(rhs, rows), up_source.reshape(rhs, rows)
    x = swap(down_own.astype(BF16))
    down_got, up_other = swap(down_own[:, :wide]), swap(up_own)
    x, down_got, up_other, matrix, me, tile_0, tile_1, on_0, masks = tie(
        x, down_got, up_other, matrix, me, tile_0, tile_1, on_0, masks
    )
    received = swap(matrix)
    whole = whole_product(spread(x), matrix) + down_own
    x_1 = trade(whole[:, wide:].astype(BF16), [(1, 3)])
    x_0 = trade(whole[:, :wide].astype(BF16), [(1, 2)])
    base_a = jnp.where(on_0, down_own[:, wide:], down_got)
    base_b = jnp.where(on_0, down_got, down_own[:, wide:])
    up_a = jnp.where(on_0, up_own[:, :wide], up_other[:, wide:])
    up_b = jnp.where(on_0, up_other[:, wide:], up_own[:, :wide])
    up_b_rest = jnp.where(on_0, up_other[:, :wide], up_own[:, wide:])
    down_a = base_a
    x = jnp.where(on_0, x_0, x_1)

    x, base_a, base_b, up_a, up_b, up_b_rest = tie(x, base_a, base_b, up_a, up_b, up_b_rest)
    for p in range(1, planes):
        if p > 1:
            x = hop(x.astype(BF16), p - 1, p)
        if p == 2:
            x, down_b = tie(x, down_b)
        blocks = spread(x)
        if p == 1:
            blocks, received = tie(blocks, received)
            mine, theirs, matrix_a = load_product(me, 0, matrix, received, blocks, tile_1, base_a)
        else:
            mine, theirs = down_call(blocks, matrix_a, tile_1, base_a)
        x = mine + swap(theirs)
        down_a = jnp.where(masks[p], x, down_a)
        blocks = spread(x)
        if p == 1:
            mine, theirs, matrix_b = load_product(me, 1, matrix, received, blocks, tile_0, base_b)
        else:
            mine, theirs = down_call(blocks, matrix_b, tile_0, base_b)
        if p == planes - 1:
            break
        x = mine + swap(theirs)
        if p == 1:
            whole, x = tie(whole, x)
            down_b = jnp.where(on_0, swap(whole[:, :wide]), whole[:, wide:])
        down_b = jnp.where(masks[p], x, down_b)

    mine, theirs, down_a, down_b = tie(mine, theirs, down_a, down_b)
    rest = up_b_rest + (mine + swap(theirs))
    x = up_b + (theirs + swap(mine))
    base_b = up_b + swap(down_b)
    base_a = up_a + swap(down_a)
    x, rest, base_a, base_b = tie(x, rest, base_a, base_b)
    total_a, total_b = base_a, jnp.where(masks[planes - 1], x, base_b)
    for p in reversed(range(planes)):
        if p < planes - 1:
            x = x.astype(BF16)
            x = up_product(hop(x, p + 1, p), hop_across(x, p + 1, p), True, matrix_b, base_b)
            total_b = jnp.where(masks[p], x, total_b)
            rest = swap(x.astype(BF16))
        x = up_product(x, rest, False, matrix_a, base_a)
        total_a = jnp.where(masks[p], x, total_a)

    got = swap(jnp.where(on_0, total_b, total_a))
    out = jnp.concatenate([jnp.where(on_0, total_a, total_b), got], axis=1)
    return out.reshape(1, 2, rhs // 2, rows)


def solution(mesh):
    in_specs = (
        P("sweep", None, "layer", None),
        P("sweep", None, None, "layer"),
        P("sweep", None, None, "layer"),
    )
    out_specs = P("sweep", None, None, "layer")
    return jax.shard_map(local, mesh=mesh, in_specs=in_specs, out_specs=out_specs, check_vma=False)
```

time: 271 us -> 277 us (1.022)
  blocking collectives: 139 us -> 158 us
  waiting for transfers between devices: 21.3 us -> 15.8 us
  Pallas kernels: 42.8 us -> 37.5 us
  starting transfers between devices: 63.5 us -> 60.5 us
    all_to_all x13 -> x14, blocking collectives: 139 us -> 158 us  [exchange(): return lax.all_to_all(blocks, 'layer', 0, 0, tiled=True)]
    ppermute x6 -> x10, starting transfers between devices: 25.7 us -> 37.9 us  [trade(): lax.ppermute(x, 'sweep', [p for a, b in pairs for p in ((a, b), (b, a))])]
    ppermute x19 -> x18, starting transfers between devices: 30.9 us -> 22.6 us  [swap(): return lax.ppermute(x, 'sweep', [(i, i ^ 1) for i in range(2 * planes)])]
    pallas_call x14 -> x11, Pallas kernels: 28.5 us -> 20.9 us  [call(): pl.pallas_call(body, in_specs=[VMEM] * len(args), out_specs=jax.tree.map(...]
    all_to_all x1 -> x0, waiting for transfers between devices: 7.46 us -> none  [exchange(): return lax.all_to_all(blocks, 'layer', 0, 0, tiled=True)]
    all_to_all x1 -> x0, starting transfers between devices: 6.84 us -> none  [exchange(): return lax.all_to_all(blocks, 'layer', 0, 0, tiled=True)]
    ppermute x6 -> x10, waiting for transfers between devices: 1.13 us -> 4.75 us  [trade(): lax.ppermute(x, 'sweep', [p for a, b in pairs for p in ((a, b), (b, a))])]
    ppermute x19 -> x18, waiting for transfers between devices: 12.7 us -> 11 us  [swap(): return lax.ppermute(x, 'sweep', [(i, i ^ 1) for i in range(2 * planes)])]
  transfers between devices with their start and end apart: 26 -> 28, of which waited for: 17 -> 18; matrix products, arithmetic and copies ran while one was open for 0% -> 1% of each run, Pallas kernels for 4% -> 3%
where the time goes in v4:
time: 277 us; the launch traced here: 276 us
  blocking collectives  158 us (57%)
  starting transfers between devices  60.5 us (22%)
  Pallas kernels  37.5 us (14%)
  waiting for transfers between devices  15.8 us (6%)
  other arithmetic  3.02 us (1%)
    all_to_all x14, blocking collectives, exchange(): return lax.all_to_all(blocks, 'layer', 0, 0, tiled=True)  158 us
    ppermute x10, starting transfers between devices, trade(): lax.ppermute(x, 'sweep', [p for a, b in pairs for p in ((a, b), (b, a))])  37.9 us
    ppermute x18, starting transfers between devices, swap(): return lax.ppermute(x, 'sweep', [(i, i ^ 1) for i in range(2 * planes)])  22.6 us
    pallas_call x11, Pallas kernels, call(): pl.pallas_call(body, in_specs=[VMEM] * len(args), out_specs=jax.tree.map(...  20.9 us
    ppermute x18, waiting for transfers between devices, swap(): return lax.ppermute(x, 'sweep', [(i, i ^ 1) for i in range(2 * planes)])  11 us
    pallas_call x1, Pallas kernels, whole_product(): pl.pallas_call(body, in_specs=[VMEM, HBM], out_specs=VMEM, out_shape=jax....  8.44 us
    pallas_call x2, Pallas kernels, load_product(): pl.pallas_call(body, in_specs=[SMEM, HBM, HBM, VMEM, VMEM, VMEM], out_spe...  8.1 us
  transfers between devices with their start and end apart: 28, of which 18 were waited for; matrix products, arithmetic and copies ran while one was open for 1% of the time, Pallas kernels for 3%

profile of v4, /device:TPU:1, one launch (start us, length us, event | category | flops | bytes accessed | tf_op | source)
XLA Modules:
  0.0 276.2 jit_solution(2212791682676537337)
XLA Ops:
  5.1 16.9 %all_to_all.70.x_ref = bf16[16,32,512]{2,1,0:T(8,128)(2,1)} all-to-all(bf16[16,32,512]{2,1,0:T(8,128)(2,1)S(1)} %broadcast_in_dim.21), channel_id=1, replica_groups=mesh['sweep'=8,'layer'=16] {'layer'}, dimensions={0} | all-to-all | bytes 1048576 | tf_op jit(solution)/shard_map/all_to_all | solution.py:183
  22.0 8.4 %whole_product.1 = f32[32,512]{1,0:T(8,128)} custom-call(bf16[16,32,512]{2,1,0:T(8,128)(2,1)} %all_to_all.70.x_ref, bf16[2,512,8192]{2,1,0:T(8,128)(2,1)} %bitcast.23), custom_call_target="tpu_custom_call" | custom-call | flops 1073741824 | bytes 16777216 | tf_op jit(solution)/shard_map/whole_product/pallas_call | solution.py:54
  31.4 3.5 %collective-permute-start.4 = (bf16[32,256]{1,0:T(8,128)(2,1)S(1)}, bf16[32,256]{1,0:T(8,128)(2,1)S(1)}, u32[]{:S(2)}, u32[]{:S(2)}) collective-permute-start(bf16[32,256]{1,0:T(8,128)(2,1)S(1)} %get-tuple-element.134), channel_id=1, source_target_pairs={{16,48},{48,16},{17,49},{49,17},{18,50},{50,18},{19,51},{51,19},{2... | collective-permute-start | bytes 49160 | tf_op jit(solution)/shard_map/ppermute | solution.py:174
  34.9 2.8 %collective-permute-start.3 = (bf16[32,256]{1,0:T(8,128)(2,1)S(1)}, bf16[32,256]{1,0:T(8,128)(2,1)S(1)}, u32[]{:S(2)}, u32[]{:S(2)}) collective-permute-start(bf16[32,256]{1,0:T(8,128)(2,1)S(1)} %get-tuple-element.135), channel_id=1, source_target_pairs={{16,32},{32,16},{17,33},{33,17},{18,34},{34,18},{19,35},{35,19},{2... | collective-permute-start | bytes 49160 | tf_op jit(solution)/shard_map/ppermute | solution.py:174
  40.0 11.3 %all_to_all.71.x_ref = bf16[16,32,256]{2,1,0:T(8,128)(2,1)S(1)} all-to-all(bf16[16,32,256]{2,1,0:T(8,128)(2,1)S(1)} %broadcast_in_dim.22), channel_id=1, replica_groups=mesh['sweep'=8,'layer'=16] {'layer'}, dimensions={0} | all-to-all | bytes 524288 | tf_op jit(solution)/shard_map/all_to_all | solution.py:183
  51.3 4.1 %load_product.2 = (f32[32,256]{1,0:T(8,128)S(1)}, f32[32,256]{1,0:T(8,128)S(1)}, bf16[2,512,4096]{2,1,0:T(8,128)(2,1)S(1)}) custom-call(s32[1]{0:T(128)} %bitcast.3.me_ref, bf16[2,512,8192]{2,1,0:T(8,128)(2,1)} %bitcast.24, bf16[2,512,8192]{2,1,0:T(8,128)(2,1)} %collective-permute-done.5.received_ref, bf16[16,32,256]{2,1,0:T(8,128)(2,1)S(1)} %all_to_all.71.x_ref, ...), custom_call_target="tpu_custom_call" | custom-call | flops 536870912 | bytes 8388608 | tf_op jit(solution)/shard_map/load_product/pallas_call | solution.py:97
  56.7 11.0 %all_to_all.72.x_ref = bf16[16,32,256]{2,1,0:T(8,128)(2,1)S(1)} all-to-all(bf16[16,32,256]{2,1,0:T(8,128)(2,1)S(1)} %broadcast_in_dim.23), channel_id=1, replica_groups=mesh['sweep'=8,'layer'=16] {'layer'}, dimensions={0} | all-to-all | bytes 524288 | tf_op jit(solution)/shard_map/all_to_all | solution.py:183
  67.7 4.1 %load_product.3 = (f32[32,256]{1,0:T(8,128)S(1)}, f32[32,256]{1,0:T(8,128)S(1)}, bf16[2,512,4096]{2,1,0:T(8,128)(2,1)S(1)}) custom-call(s32[1]{0:T(128)} %bitcast.3.me_ref, bf16[2,512,8192]{2,1,0:T(8,128)(2,1)} %bitcast.25, bf16[2,512,8192]{2,1,0:T(8,128)(2,1)} %collective-permute-done.5.received_ref, bf16[16,32,256]{2,1,0:T(8,128)(2,1)S(1)} %all_to_all.72.x_ref, ...), custom_call_target="tpu_custom_call" | custom-call | flops 536870912 | bytes 8388608 | tf_op jit(solution)/shard_map/load_product/pallas_call | solution.py:97
  76.4 10.7 %all_to_all.73.x_ref = bf16[16,32,256]{2,1,0:T(8,128)(2,1)S(1)} all-to-all(bf16[16,32,256]{2,1,0:T(8,128)(2,1)S(1)} %broadcast_in_dim.24), channel_id=1, replica_groups=mesh['sweep'=8,'layer'=16] {'layer'}, dimensions={0} | all-to-all | bytes 524288 | tf_op jit(solution)/shard_map/all_to_all | solution.py:183
  87.1 2.5 down_product.4
  92.5 10.7 %all_to_all.74.x_ref = bf16[16,32,256]{2,1,0:T(8,128)(2,1)S(1)} all-to-all(bf16[16,32,256]{2,1,0:T(8,128)(2,1)S(1)} %broadcast_in_dim.25), channel_id=1, replica_groups=mesh['sweep'=8,'layer'=16] {'layer'}, dimensions={0} | all-to-all | bytes 524288 | tf_op jit(solution)/shard_map/all_to_all | solution.py:183
  103.2 2.5 down_product.5
  109.3 10.7 %all_to_all.75.x_ref = bf16[16,32,256]{2,1,0:T(8,128)(2,1)S(1)} all-to-all(bf16[16,32,256]{2,1,0:T(8,128)(2,1)S(1)} %broadcast_in_dim.26), channel_id=1, replica_groups=mesh['sweep'=8,'layer'=16] {'layer'}, dimensions={0} | all-to-all | bytes 524288 | tf_op jit(solution)/shard_map/all_to_all | solution.py:183
  125.5 10.7 %all_to_all.76.x_ref = bf16[16,32,256]{2,1,0:T(8,128)(2,1)S(1)} all-to-all(bf16[16,32,256]{2,1,0:T(8,128)(2,1)S(1)} %broadcast_in_dim.27), channel_id=1, replica_groups=mesh['sweep'=8,'layer'=16] {'layer'}, dimensions={0} | all-to-all | bytes 524288 | tf_op jit(solution)/shard_map/all_to_all | solution.py:183
  144.0 10.9 %all_to_all.77 = bf16[16,32,256]{2,1,0:T(8,128)(2,1)S(1)} all-to-all(bf16[16,32,256]{2,1,0:T(8,128)(2,1)S(1)} %up_product.7), channel_id=1, replica_groups=mesh['sweep'=8,'layer'=16] {'layer'}, dimensions={0} | all-to-all | bytes 524288 | tf_op jit(solution)/shard_map/all_to_all | solution.py:183
  157.9 10.9 %all_to_all.78 = bf16[16,32,256]{2,1,0:T(8,128)(2,1)S(1)} all-to-all(bf16[16,32,256]{2,1,0:T(8,128)(2,1)S(1)} %up_product.8), channel_id=1, replica_groups=mesh['sweep'=8,'layer'=16] {'layer'}, dimensions={0} | all-to-all | bytes 524288 | tf_op jit(solution)/shard_map/all_to_all | solution.py:183
  168.9 2.8 %collective-permute-start.20 = (bf16[32,256]{1,0:T(8,128)(2,1)S(1)}, bf16[32,256]{1,0:T(8,128)(2,1)S(1)}, u32[]{:S(2)}, u32[]{:S(2)}) collective-permute-start(bf16[32,256]{1,0:T(8,128)(2,1)S(1)} %add_convert_fusion.5), channel_id=1, source_target_pairs={{0,16},{16,0},{32,48},{48,32},{64,80},{80,64},{96,112},{112,96},{1... | collective-permute-start | bytes 49160 | tf_op jit(solution)/shard_map/ppermute | solution.py:171
  174.1 10.7 %all_to_all.79 = bf16[16,32,256]{2,1,0:T(8,128)(2,1)S(1)} all-to-all(bf16[16,32,256]{2,1,0:T(8,128)(2,1)S(1)} %up_product.9), channel_id=1, replica_groups=mesh['sweep'=8,'layer'=16] {'layer'}, dimensions={0} | all-to-all | bytes 524288 | tf_op jit(solution)/shard_map/all_to_all | solution.py:183
  187.8 10.9 %all_to_all.80 = bf16[16,32,256]{2,1,0:T(8,128)(2,1)S(1)} all-to-all(bf16[16,32,256]{2,1,0:T(8,128)(2,1)S(1)} %up_product.10), channel_id=1, replica_groups=mesh['sweep'=8,'layer'=16] {'layer'}, dimensions={0} | all-to-all | bytes 524288 | tf_op jit(solution)/shard_map/all_to_all | solution.py:183
  198.8 3.0 %collective-permute-start.23 = (bf16[32,256]{1,0:T(8,128)(2,1)S(1)}, bf16[32,256]{1,0:T(8,128)(2,1)S(1)}, u32[]{:S(2)}, u32[]{:S(2)}) collective-permute-start(bf16[32,256]{1,0:T(8,128)(2,1)S(1)} %add_convert_fusion.3), channel_id=1, source_target_pairs={{0,16},{16,0},{32,48},{48,32},{64,80},{80,64},{96,112},{112,96},{1... | collective-permute-start | bytes 49160 | tf_op jit(solution)/shard_map/ppermute | solution.py:171
  204.1 10.8 %all_to_all.81 = bf16[16,32,256]{2,1,0:T(8,128)(2,1)S(1)} all-to-all(bf16[16,32,256]{2,1,0:T(8,128)(2,1)S(1)} %up_product.11), channel_id=1, replica_groups=mesh['sweep'=8,'layer'=16] {'layer'}, dimensions={0} | all-to-all | bytes 524288 | tf_op jit(solution)/shard_map/all_to_all | solution.py:183
  215.0 25.7 %collective-permute-start.25 = (bf16[32,256]{1,0:T(8,128)(2,1)S(1)}, bf16[32,256]{1,0:T(8,128)(2,1)S(1)}, u32[]{:S(2)}, u32[]{:S(2)}) collective-permute-start(bf16[32,256]{1,0:T(8,128)(2,1)S(1)} %add_convert_fusion.2), channel_id=1, source_target_pairs={{32,16},{16,32},{48,0},{0,48},{33,17},{17,33},{49,1},{1,49},{34,18... | collective-permute-start | bytes 49160 | tf_op jit(solution)/shard_map/ppermute | solution.py:174
  246.7 10.9 %all_to_all.82 = bf16[16,32,256]{2,1,0:T(8,128)(2,1)S(1)} all-to-all(bf16[16,32,256]{2,1,0:T(8,128)(2,1)S(1)} %up_product.12), channel_id=1, replica_groups=mesh['sweep'=8,'layer'=16] {'layer'}, dimensions={0} | all-to-all | bytes 524288 | tf_op jit(solution)/shard_map/all_to_all | solution.py:183
  261.9 10.7 %all_to_all.83 = bf16[16,32,256]{2,1,0:T(8,128)(2,1)S(1)} all-to-all(bf16[16,32,256]{2,1,0:T(8,128)(2,1)S(1)} %up_product.13), channel_id=1, replica_groups=mesh['sweep'=8,'layer'=16] {'layer'}, dimensions={0} | all-to-all | bytes 524288 | tf_op jit(solution)/shard_map/all_to_all | solution.py:183
  (121 shorter events, 58.2 us)
Async XLA Ops:
  0.9 2.8 %collective-permute-start = (bf16[32,512]{1,0:T(8,128)(2,1)S(1)}, bf16[32,512]{1,0:T(8,128)(2,1)S(1)}, u32[]{:S(2)}, u32[]{:S(2)}) collective-permute-start(bf16[32,512]{1,0:T(8,128)(2,1)S(1)} %bitcast_convert_fusion), channel_id=1, source_target_pairs={{0,16},{16,0},{32,48},{48,32},{64,80},{80,64},{96,112},{112,96},{1... | collective-permute-start | bytes 98312 | tf_op jit(solution)/shard_map/ppermute | solution.py:171
  3.1 1.2 collective-permute-start.1
  3.1 1.6 collective-permute-start.2
  4.7 46.6 %collective-permute-start.5 = (bf16[2,512,8192]{2,1,0:T(8,128)(2,1)}, bf16[2,512,8192]{2,1,0:T(8,128)(2,1)}, u32[]{:S(2)}, u32[]{:S(2)}) collective-permute-start(bf16[2,512,8192]{2,1,0:T(8,128)(2,1)} %bitcast.22), channel_id=1, source_target_pairs={{0,16},{16,0},{32,48},{48,32},{64,80},{80,64},{96,112},{112,96},{1... | collective-permute-start | bytes 50331656 | tf_op jit(solution)/shard_map/ppermute | solution.py:171
  31.4 6.4 %collective-permute-start.4 = (bf16[32,256]{1,0:T(8,128)(2,1)S(1)}, bf16[32,256]{1,0:T(8,128)(2,1)S(1)}, u32[]{:S(2)}, u32[]{:S(2)}) collective-permute-start(bf16[32,256]{1,0:T(8,128)(2,1)S(1)} %get-tuple-element.134), channel_id=1, source_target_pairs={{16,48},{48,16},{17,49},{49,17},{18,50},{50,18},{19,51},{51,19},{2... | collective-permute-start | bytes 49160 | tf_op jit(solution)/shard_map/ppermute | solution.py:174
  34.9 5.1 %collective-permute-start.3 = (bf16[32,256]{1,0:T(8,128)(2,1)S(1)}, bf16[32,256]{1,0:T(8,128)(2,1)S(1)}, u32[]{:S(2)}, u32[]{:S(2)}) collective-permute-start(bf16[32,256]{1,0:T(8,128)(2,1)S(1)} %get-tuple-element.135), channel_id=1, source_target_pairs={{16,32},{32,16},{17,33},{33,17},{18,34},{34,18},{19,35},{35,19},{2... | collective-permute-start | bytes 49160 | tf_op jit(solution)/shard_map/ppermute | solution.py:174
  55.4 1.3 collective-permute-start.6
  71.7 2.6 collective-permute-start.7
  74.3 1.3 collective-permute-start.9
  89.6 2.8 %collective-permute-start.10 = (f32[32,256]{1,0:T(8,128)S(1)}, f32[32,256]{1,0:T(8,128)S(1)}, u32[]{:S(2)}, u32[]{:S(2)}) collective-permute-start(f32[32,256]{1,0:T(8,128)S(1)} %get-tuple-element.76), channel_id=1, source_target_pairs={{0,16},{16,0},{32,48},{48,32},{64,80},{80,64},{96,112},{112,96},{1... | collective-permute-start | bytes 98312 | tf_op jit(solution)/shard_map/ppermute | solution.py:171
  105.8 2.8 %collective-permute-start.11 = (f32[32,256]{1,0:T(8,128)S(1)}, f32[32,256]{1,0:T(8,128)S(1)}, u32[]{:S(2)}, u32[]{:S(2)}) collective-permute-start(f32[32,256]{1,0:T(8,128)S(1)} %get-tuple-element.79), channel_id=1, source_target_pairs={{0,16},{16,0},{32,48},{48,32},{64,80},{80,64},{96,112},{112,96},{1... | collective-permute-start | bytes 98312 | tf_op jit(solution)/shard_map/ppermute | solution.py:171
  122.6 2.8 %collective-permute-start.13 = (f32[32,256]{1,0:T(8,128)S(1)}, f32[32,256]{1,0:T(8,128)S(1)}, u32[]{:S(2)}, u32[]{:S(2)}) collective-permute-start(f32[32,256]{1,0:T(8,128)S(1)} %get-tuple-element.81), channel_id=1, source_target_pairs={{0,16},{16,0},{32,48},{48,32},{64,80},{80,64},{96,112},{112,96},{1... | collective-permute-start | bytes 98312 | tf_op jit(solution)/shard_map/ppermute | solution.py:171
  138.7 2.8 %collective-permute-start.15 = (f32[32,256]{1,0:T(8,128)S(1)}, f32[32,256]{1,0:T(8,128)S(1)}, u32[]{:S(2)}, u32[]{:S(2)}) collective-permute-start(f32[32,256]{1,0:T(8,128)S(1)} %get-tuple-element.87), channel_id=1, source_target_pairs={{0,16},{16,0},{32,48},{48,32},{64,80},{80,64},{96,112},{112,96},{1... | collective-permute-start | bytes 98312 | tf_op jit(solution)/shard_map/ppermute | solution.py:171
  140.7 1.2 collective-permute-start.16
  140.8 1.3 collective-permute-start.17
  141.2 1.2 collective-permute-start.14
  155.0 1.3 collective-permute-start.19
  168.9 3.7 %collective-permute-start.20 = (bf16[32,256]{1,0:T(8,128)(2,1)S(1)}, bf16[32,256]{1,0:T(8,128)(2,1)S(1)}, u32[]{:S(2)}, u32[]{:S(2)}) collective-permute-start(bf16[32,256]{1,0:T(8,128)(2,1)S(1)} %add_convert_fusion.5), channel_id=1, source_target_pairs={{0,16},{16,0},{32,48},{48,32},{64,80},{80,64},{96,112},{112,96},{1... | collective-permute-start | bytes 49160 | tf_op jit(solution)/shard_map/ppermute | solution.py:171
  184.9 1.3 collective-permute-start.22
  198.8 3.8 %collective-permute-start.23 = (bf16[32,256]{1,0:T(8,128)(2,1)S(1)}, bf16[32,256]{1,0:T(8,128)(2,1)S(1)}, u32[]{:S(2)}, u32[]{:S(2)}) collective-permute-start(bf16[32,256]{1,0:T(8,128)(2,1)S(1)} %add_convert_fusion.3), channel_id=1, source_target_pairs={{0,16},{16,0},{32,48},{48,32},{64,80},{80,64},{96,112},{112,96},{1... | collective-permute-start | bytes 49160 | tf_op jit(solution)/shard_map/ppermute | solution.py:171
  215.0 27.6 %collective-permute-start.25 = (bf16[32,256]{1,0:T(8,128)(2,1)S(1)}, bf16[32,256]{1,0:T(8,128)(2,1)S(1)}, u32[]{:S(2)}, u32[]{:S(2)}) collective-permute-start(bf16[32,256]{1,0:T(8,128)(2,1)S(1)} %add_convert_fusion.2), channel_id=1, source_target_pairs={{32,16},{16,32},{48,0},{0,48},{33,17},{17,33},{49,1},{1,49},{34,18... | collective-permute-start | bytes 49160 | tf_op jit(solution)/shard_map/ppermute | solution.py:174
  240.7 4.5 %collective-permute-start.24 = (bf16[32,256]{1,0:T(8,128)(2,1)S(1)}, bf16[32,256]{1,0:T(8,128)(2,1)S(1)}, u32[]{:S(2)}, u32[]{:S(2)}) collective-permute-start(bf16[32,256]{1,0:T(8,128)(2,1)S(1)} %add_convert_fusion.2), channel_id=1, source_target_pairs={{32,0},{0,32},{48,16},{16,48},{33,1},{1,33},{49,17},{17,49},{34,2}... | collective-permute-start | bytes 49160 | tf_op jit(solution)/shard_map/ppermute | solution.py:174
  257.7 2.6 collective-permute-start.26
  272.7 2.8 %collective-permute-start.27 = (f32[32,256]{1,0:T(8,128)S(1)}, f32[32,256]{1,0:T(8,128)S(1)}, u32[]{:S(2)}, u32[]{:S(2)}) collective-permute-start(f32[32,256]{1,0:T(8,128)S(1)} %select_n.145), channel_id=1, source_target_pairs={{0,16},{16,0},{32,48},{48,32},{64,80},{80,64},{96,112},{112,96},{1... | collective-permute-start | bytes 98312 | tf_op jit(solution)/shard_map/ppermute | solution.py:171
  (6 other events, 71.0 us)

commit v5 on v4

--- a/solution.py
+++ b/solution.py
@@ -34,45 +34,54 @@
     theirs_ref[...] = jnp.where(keeps_first, second, first)
 
 
-def whole_product(blocks, matrix):
-    chips, rhs, wide = blocks.shape
+def second_halves(matrix, first, count, chips):
     parts, rows, cols = matrix.shape
-
-    def body(x_ref, matrix_ref, out_ref, held, sems):
-        copies = [
-            pltpu.make_async_copy(matrix_ref.at[:, :, pl.ds(i * wide, wide)], held.at[i], sems.at[i])
-            for i in range(chips)
-        ]
-        for copy in copies:
+    wide = cols // (2 * chips)
+
+    def body(matrix_ref, out_ref, held, in_sems, out_sems):
+        taken, put = [], []
+        for i in range(count):
+            at = (2 * (first + i) + 1) * wide
+            taken.append(
+                pltpu.make_async_copy(matrix_ref.at[:, :, pl.ds(at, wide)], held.at[i], in_sems.at[i])
+            )
+            put.append(
+                pltpu.make_async_copy(held.at[i], out_ref.at[:, :, pl.ds(i * wide, wide)], out_sems.at[i])
+            )
+        for copy in taken:
             copy.start()
-        sums = None
-        for i in range(chips):
-            copies[i].wait()
-            sums = down_sums(x_ref[i], held.at[i], sums)
-        out_ref[...] = jnp.concatenate(complex_of(sums, rhs // 2), axis=0)
+        for i in range(count):
+            taken[i].wait()
+            put[i].start()
+        for copy in put:
+            copy.wait()
 
     return pl.pallas_call(
         body,
-        in_specs=[VMEM, HBM],
-        out_specs=VMEM,
-        out_shape=jax.ShapeDtypeStruct((rhs, rows), F32),
+        in_specs=[HBM],
+        out_specs=HBM,
+        out_shape=pltpu.HBM((parts, rows, count * wide), BF16),
         scratch_shapes=[
-            pltpu.VMEM((chips, parts, rows, wide), BF16),
-            pltpu.SemaphoreType.DMA((chips,)),
+            pltpu.VMEM((count, parts, rows, wide), BF16),
+            pltpu.SemaphoreType.DMA((count,)),
+            pltpu.SemaphoreType.DMA((count,)),
         ],
         compiler_params=pltpu.CompilerParams(vmem_limit_bytes=56 * MIB),
-        cost_estimate=pl.CostEstimate(
-            flops=8 * rhs * rows * cols, bytes_accessed=2 * parts * rows * cols, transcendentals=0
-        ),
-        name="whole_product",
-    )(blocks, matrix)
+        name="second_halves",
+    )(matrix)
 
 
 def load_product(me, on_core, matrix, received, blocks, keeps_first, base):
     chips, rhs, wide = blocks.shape
     parts, rows, cols = matrix.shape
 
-    def body(me_ref, matrix_ref, received_ref, x_ref, first_ref, base_ref, mine_ref, theirs_ref, out_ref, sems):
+    pieces = len(received)
+    per = chips // pieces
+
+    def body(me_ref, matrix_ref, *refs):
+        received_refs = refs[:pieces]
+        x_ref, first_ref, base_ref, mine_ref, theirs_ref, out_ref, sems = refs[pieces:]
+
         def copy(source_ref, at, i):
             here = pl.ds(i * wide, wide)
             return pltpu.make_async_copy(source_ref.at[:, :, pl.ds(at, wide)], out_ref.at[:, :, here], sems.at[i])
@@ -85,18 +94,18 @@
         @pl.when(me_ref[0] % 2 != on_core)
         def _():
             for i in range(chips):
-                copy(received_ref, (2 * i + 1) * wide, i).start()
+                copy(received_refs[i // per], i % per * wide, i).start()
 
         sums = None
         for i in range(chips):
-            copy(received_ref, i * wide, i).wait()
+            copy(matrix_ref, i * wide, i).wait()
             sums = down_sums(x_ref[i], out_ref.at[:, :, pl.ds(i * wide, wide)], sums)
         write_down(sums, first_ref, base_ref, mine_ref, theirs_ref)
 
     part = jax.ShapeDtypeStruct((rhs, wide), F32)
     return pl.pallas_call(
         body,
-        in_specs=[SMEM, HBM, HBM, VMEM, VMEM, VMEM],
+        in_specs=[SMEM, HBM, *[HBM] * pieces, VMEM, VMEM, VMEM],
         out_specs=[VMEM, VMEM, VMEM],
         out_shape=[part, part, pltpu.VMEM((parts, rows, cols // 2), BF16)],
         scratch_shapes=[pltpu.SemaphoreType.DMA((chips,))],
@@ -105,7 +114,7 @@
             flops=4 * rhs * rows * cols, bytes_accessed=parts * rows * cols, transcendentals=0
         ),
         name="load_product",
-    )(me, matrix, received, blocks, keeps_first, base)
+    )(me, matrix, *received, blocks, keeps_first, base)
 
 
 def vmem_call(body, out_shape, name, flops):
@@ -170,14 +179,9 @@
     def swap(x):
         return lax.ppermute(x, "sweep", [(i, i ^ 1) for i in range(2 * planes)])
 
-    def trade(x, pairs):
-        return lax.ppermute(x, "sweep", [p for a, b in pairs for p in ((a, b), (b, a))])
-
     def hop(x, a, b):
-        return trade(x, [(2 * a + c, 2 * b + c) for c in range(2)])
-
-    def hop_across(x, a, b):
-        return trade(x, [(2 * a + c, 2 * b + 1 - c) for c in range(2)])
+        pairs = [p for c in range(2) for p in ((2 * a + c, 2 * b + c), (2 * b + c, 2 * a + c))]
+        return lax.ppermute(x, "sweep", pairs)
 
     def exchange(blocks):
         return lax.all_to_all(blocks, "layer", 0, 0, tiled=True)
@@ -198,57 +202,49 @@
     down_call = vmem_call(down_body, (part, part), "down_product", flops)
     up_call = vmem_call(up_body, jax.ShapeDtypeStruct((chips, rhs, wide), BF16), "up_product", flops)
 
-    def up_product(x, other, first_on_0, mat, base):
-        x, other = x.astype(BF16), other.astype(BF16)
+    def ordered(x, other, first_on_0):
         halves = [jnp.where(on_0, x, other), jnp.where(on_0, other, x)]
-        full = jnp.concatenate(halves if first_on_0 else halves[::-1], axis=1)
-        blocks = exchange(up_call(full, mat))
-        return base + jnp.sum(blocks.astype(F32), axis=0)
+        return jnp.concatenate(halves if first_on_0 else halves[::-1], axis=1).astype(BF16)
+
+    def up_product(full, mat, base):
+        return base + jnp.sum(exchange(up_call(full, mat)).astype(F32), axis=0)
 
     down_own, up_own = down_source.reshape(rhs, rows), up_source.reshape(rhs, rows)
-    x = swap(down_own.astype(BF16))
-    down_got, up_other = swap(down_own[:, :wide]), swap(up_own)
-    x, down_got, up_other, matrix, me, tile_0, tile_1, on_0, masks = tie(
-        x, down_got, up_other, matrix, me, tile_0, tile_1, on_0, masks
-    )
-    received = swap(matrix)
-    whole = whole_product(spread(x), matrix) + down_own
-    x_1 = trade(whole[:, wide:].astype(BF16), [(1, 3)])
-    x_0 = trade(whole[:, :wide].astype(BF16), [(1, 2)])
+    down_got, matrix = tie(swap(down_own[:, :wide]), matrix)
+    pieces = 1
+    received = [
+        swap(second_halves(matrix, j * chips // pieces, chips // pieces, chips)) for j in range(pieces)
+    ]
     base_a = jnp.where(on_0, down_own[:, wide:], down_got)
     base_b = jnp.where(on_0, down_got, down_own[:, wide:])
-    up_a = jnp.where(on_0, up_own[:, :wide], up_other[:, wide:])
-    up_b = jnp.where(on_0, up_other[:, wide:], up_own[:, :wide])
-    up_b_rest = jnp.where(on_0, up_other[:, :wide], up_own[:, wide:])
-    down_a = base_a
-    x = jnp.where(on_0, x_0, x_1)
-
-    x, base_a, base_b, up_a, up_b, up_b_rest = tie(x, base_a, base_b, up_a, up_b, up_b_rest)
-    for p in range(1, planes):
-        if p > 1:
+    down_a, down_b = base_a, base_b
+
+    x, me, tile_0, tile_1, on_0, masks = tie(base_a, me, tile_0, tile_1, on_0, masks)
+    for p in range(planes):
+        if p > 0:
             x = hop(x.astype(BF16), p - 1, p)
-        if p == 2:
-            x, down_b = tie(x, down_b)
+            if p == 1:
+                x, up_a, up_b, up_b_rest = tie(x, up_a, up_b, up_b_rest)
+                mine, theirs, matrix_a = load_product(me, 0, matrix, received, spread(x), tile_1, base_a)
+            else:
+                mine, theirs = down_call(spread(x), matrix_a, tile_1, base_a)
+            x = mine + swap(theirs)
+            down_a = jnp.where(masks[p], x, down_a)
         blocks = spread(x)
-        if p == 1:
-            blocks, received = tie(blocks, received)
-            mine, theirs, matrix_a = load_product(me, 0, matrix, received, blocks, tile_1, base_a)
-        else:
-            mine, theirs = down_call(blocks, matrix_a, tile_1, base_a)
-        x = mine + swap(theirs)
-        down_a = jnp.where(masks[p], x, down_a)
-        blocks = spread(x)
-        if p == 1:
+        if p == 0:
             mine, theirs, matrix_b = load_product(me, 1, matrix, received, blocks, tile_0, base_b)
         else:
             mine, theirs = down_call(blocks, matrix_b, tile_0, base_b)
         if p == planes - 1:
             break
         x = mine + swap(theirs)
-        if p == 1:
-            whole, x = tie(whole, x)
-            down_b = jnp.where(on_0, swap(whole[:, :wide]), whole[:, wide:])
         down_b = jnp.where(masks[p], x, down_b)
+        if p == 0:
+            x, up_own = tie(x, up_own)
+            up_other = swap(up_own)
+            up_a = jnp.where(on_0, up_own[:, :wide], up_other[:, wide:])
+            up_b = jnp.where(on_0, up_other[:, wide:], up_own[:, :wide])
+            up_b_rest = jnp.where(on_0, up_other[:, :wide], up_own[:, wide:])
 
     mine, theirs, down_a, down_b = tie(mine, theirs, down_a, down_b)
     rest = up_b_rest + (mine + swap(theirs))
@@ -257,14 +253,16 @@
     base_a = up_a + swap(down_a)
     x, rest, base_a, base_b = tie(x, rest, base_a, base_b)
     total_a, total_b = base_a, jnp.where(masks[planes - 1], x, base_b)
+    full = ordered(x, rest, False)
     for p in reversed(range(planes)):
         if p < planes - 1:
-            x = x.astype(BF16)
-            x = up_product(hop(x, p + 1, p), hop_across(x, p + 1, p), True, matrix_b, base_b)
+            x = up_product(hop(full, p + 1, p), matrix_b, base_b)
             total_b = jnp.where(masks[p], x, total_b)
-            rest = swap(x.astype(BF16))
-        x = up_product(x, rest, False, matrix_a, base_a)
+            full = ordered(x.astype(BF16), swap(x.astype(BF16)), False)
+        x = up_product(full, matrix_a, base_a)
         total_a = jnp.where(masks[p], x, total_a)
+        if p > 0:
+            full = ordered(x.astype(BF16), swap(x.astype(BF16)), True)
 
     got = swap(jnp.where(on_0, total_b, total_a))
     out = jnp.concatenate([jnp.where(on_0, total_a, total_b), got], axis=1)

time: 277 us -> 270 us (0.975)
  blocking collectives: 158 us -> 154 us
    ppermute x10 -> x6, starting transfers between devices: 37.9 us -> 26.6 us  [hop(): return lax.ppermute(x, 'sweep', pairs)]
    ppermute x18 -> x20, starting transfers between devices: 22.6 us -> 31.4 us  [swap(): return lax.ppermute(x, 'sweep', [(i, i ^ 1) for i in range(2 * planes)])]
    all_to_all x14, blocking collectives: 158 us -> 154 us  [exchange(): return lax.all_to_all(blocks, 'layer', 0, 0, tiled=True)]
    pallas_call x11 -> x12, Pallas kernels: 20.9 us -> 23.4 us  [call(): pl.pallas_call(body, in_specs=[VMEM] * len(args), out_specs=jax.tree.map(...]
    ppermute x18 -> x20, waiting for transfers between devices: 11 us -> 13 us  [swap(): return lax.ppermute(x, 'sweep', [(i, i ^ 1) for i in range(2 * planes)])]
  transfers between devices with their start and end apart: 28 -> 26, of which waited for: 18 -> 20; matrix products, arithmetic and copies ran while one was open for 1% -> 0% of each run, Pallas kernels for 3% -> 0%
where the time goes in v5:
time: 270 us; the launch traced here: 269 us
  blocking collectives  154 us (57%)
  starting transfers between devices  58 us (21%)
  Pallas kernels  38.6 us (14%)
  waiting for transfers between devices  15.4 us (6%)
    all_to_all x14, blocking collectives, exchange(): return lax.all_to_all(blocks, 'layer', 0, 0, tiled=True)  154 us
    ppermute x20, starting transfers between devices, swap(): return lax.ppermute(x, 'sweep', [(i, i ^ 1) for i in range(2 * planes)])  31.4 us
    ppermute x6, starting transfers between devices, hop(): return lax.ppermute(x, 'sweep', pairs)  26.6 us
    pallas_call x12, Pallas kernels, call(): pl.pallas_call(body, in_specs=[VMEM] * len(args), out_specs=jax.tree.map(...  23.4 us
    ppermute x20, waiting for transfers between devices, swap(): return lax.ppermute(x, 'sweep', [(i, i ^ 1) for i in range(2 * planes)])  13 us
    pallas_call x2, Pallas kernels, load_product(): pl.pallas_call(body, in_specs=[SMEM, HBM, *[HBM] * pieces, VMEM, VMEM, VM...  8.14 us
    pallas_call x1, Pallas kernels, second_halves(): pl.pallas_call(body, in_specs=[HBM], out_specs=HBM, out_shape=pltpu.HBM((...  6.97 us
  transfers between devices with their start and end apart: 26, of which 20 were waited for; matrix products, arithmetic and copies ran while one was open for 0% of the time, Pallas kernels for 0%

profile of v5, /device:TPU:1, one launch (start us, length us, event | category | flops | bytes accessed | tf_op | source)
XLA Modules:
  0.0 269.0 jit_solution(8942529732265484541)
XLA Ops:
  3.0 7.0 %second_halves.1 = bf16[2,512,4096]{2,1,0:T(8,128)(2,1)} custom-call(bf16[2,512,8192]{2,1,0:T(8,128)(2,1)} %bitcast.20), custom_call_target="tpu_custom_call" | custom-call | tf_op jit(solution)/shard_map/second_halves/pallas_call | solution.py:59
  10.6 14.4 %all_to_all.70.refs_1_ = bf16[16,32,256]{2,1,0:T(8,128)(2,1)S(1)} all-to-all(bf16[16,32,256]{2,1,0:T(8,128)(2,1)S(1)} %broadcast_in_dim.21), channel_id=1, replica_groups=mesh['sweep'=8,'layer'=16] {'layer'}, dimensions={0} | all-to-all | bytes 524288 | tf_op jit(solution)/shard_map/all_to_all | solution.py:187
  25.0 4.1 %load_product.2 = (f32[32,256]{1,0:T(8,128)S(1)}, f32[32,256]{1,0:T(8,128)S(1)}, bf16[2,512,4096]{2,1,0:T(8,128)(2,1)S(1)}) custom-call(s32[1]{0:T(128)} %bitcast.me_ref, bf16[2,512,8192]{2,1,0:T(8,128)(2,1)} %bitcast.21, bf16[2,512,4096]{2,1,0:T(8,128)(2,1)} %collective-permute-done.1.refs_0_, bf16[16,32,256]{2,1,0:T(8,128)(2,1)S(1)} %all_to_all.70.refs_1_, ...), custom_call_target="tpu_custom_call" | custom-call | flops 536870912 | bytes 8388608 | tf_op jit(solution)/shard_map/load_product/pallas_call | solution.py:106
  32.2 3.5 %collective-permute-start.3 = (bf16[32,256]{1,0:T(8,128)(2,1)S(1)}, bf16[32,256]{1,0:T(8,128)(2,1)S(1)}, u32[]{:S(2)}, u32[]{:S(2)}) collective-permute-start(bf16[32,256]{1,0:T(8,128)(2,1)S(1)} %convert_element_type.68), channel_id=1, source_target_pairs={{0,32},{32,0},{16,48},{48,16},{1,33},{33,1},{17,49},{49,17},{2,34}... | collective-permute-start | bytes 49160 | tf_op jit(solution)/shard_map/ppermute | solution.py:184
  36.9 11.3 %all_to_all.71.refs_1_ = bf16[16,32,256]{2,1,0:T(8,128)(2,1)S(1)} all-to-all(bf16[16,32,256]{2,1,0:T(8,128)(2,1)S(1)} %broadcast_in_dim.22), channel_id=1, replica_groups=mesh['sweep'=8,'layer'=16] {'layer'}, dimensions={0} | all-to-all | bytes 524288 | tf_op jit(solution)/shard_map/all_to_all | solution.py:187
  48.1 4.1 %load_product.3 = (f32[32,256]{1,0:T(8,128)S(1)}, f32[32,256]{1,0:T(8,128)S(1)}, bf16[2,512,4096]{2,1,0:T(8,128)(2,1)S(1)}) custom-call(s32[1]{0:T(128)} %bitcast.me_ref, bf16[2,512,8192]{2,1,0:T(8,128)(2,1)} %bitcast.22, bf16[2,512,4096]{2,1,0:T(8,128)(2,1)} %collective-permute-done.1.refs_0_, bf16[16,32,256]{2,1,0:T(8,128)(2,1)S(1)} %all_to_all.71.refs_1_, ...), custom_call_target="tpu_custom_call" | custom-call | flops 536870912 | bytes 8388608 | tf_op jit(solution)/shard_map/load_product/pallas_call | solution.py:106
  52.2 2.6 collective-permute-start.5
  55.7 10.7 %all_to_all.72.x_ref = bf16[16,32,256]{2,1,0:T(8,128)(2,1)S(1)} all-to-all(bf16[16,32,256]{2,1,0:T(8,128)(2,1)S(1)} %broadcast_in_dim.23), channel_id=1, replica_groups=mesh['sweep'=8,'layer'=16] {'layer'}, dimensions={0} | all-to-all | bytes 524288 | tf_op jit(solution)/shard_map/all_to_all | solution.py:187
  66.4 2.5 down_product.5
  72.5 10.7 %all_to_all.73.x_ref = bf16[16,32,256]{2,1,0:T(8,128)(2,1)S(1)} all-to-all(bf16[16,32,256]{2,1,0:T(8,128)(2,1)S(1)} %broadcast_in_dim.24), channel_id=1, replica_groups=mesh['sweep'=8,'layer'=16] {'layer'}, dimensions={0} | all-to-all | bytes 524288 | tf_op jit(solution)/shard_map/all_to_all | solution.py:187
  88.6 10.7 %all_to_all.74.x_ref = bf16[16,32,256]{2,1,0:T(8,128)(2,1)S(1)} all-to-all(bf16[16,32,256]{2,1,0:T(8,128)(2,1)S(1)} %broadcast_in_dim.25), channel_id=1, replica_groups=mesh['sweep'=8,'layer'=16] {'layer'}, dimensions={0} | all-to-all | bytes 524288 | tf_op jit(solution)/shard_map/all_to_all | solution.py:187
  99.4 2.5 down_product.7
  105.5 10.7 %all_to_all.75.x_ref = bf16[16,32,256]{2,1,0:T(8,128)(2,1)S(1)} all-to-all(bf16[16,32,256]{2,1,0:T(8,128)(2,1)S(1)} %broadcast_in_dim.26), channel_id=1, replica_groups=mesh['sweep'=8,'layer'=16] {'layer'}, dimensions={0} | all-to-all | bytes 524288 | tf_op jit(solution)/shard_map/all_to_all | solution.py:187
  116.2 2.5 down_product.8
  121.6 10.7 %all_to_all.76.x_ref = bf16[16,32,256]{2,1,0:T(8,128)(2,1)S(1)} all-to-all(bf16[16,32,256]{2,1,0:T(8,128)(2,1)S(1)} %broadcast_in_dim.27), channel_id=1, replica_groups=mesh['sweep'=8,'layer'=16] {'layer'}, dimensions={0} | all-to-all | bytes 524288 | tf_op jit(solution)/shard_map/all_to_all | solution.py:187
  140.2 11.0 %all_to_all.77 = bf16[16,32,256]{2,1,0:T(8,128)(2,1)S(1)} all-to-all(bf16[16,32,256]{2,1,0:T(8,128)(2,1)S(1)} %up_product.7), channel_id=1, replica_groups=mesh['sweep'=8,'layer'=16] {'layer'}, dimensions={0} | all-to-all | bytes 524288 | tf_op jit(solution)/shard_map/all_to_all | solution.py:187
  156.0 10.7 %all_to_all.78 = bf16[16,32,256]{2,1,0:T(8,128)(2,1)S(1)} all-to-all(bf16[16,32,256]{2,1,0:T(8,128)(2,1)S(1)} %up_product.8), channel_id=1, replica_groups=mesh['sweep'=8,'layer'=16] {'layer'}, dimensions={0} | all-to-all | bytes 524288 | tf_op jit(solution)/shard_map/all_to_all | solution.py:187
  171.2 10.7 %all_to_all.79 = bf16[16,32,256]{2,1,0:T(8,128)(2,1)S(1)} all-to-all(bf16[16,32,256]{2,1,0:T(8,128)(2,1)S(1)} %up_product.9), channel_id=1, replica_groups=mesh['sweep'=8,'layer'=16] {'layer'}, dimensions={0} | all-to-all | bytes 524288 | tf_op jit(solution)/shard_map/all_to_all | solution.py:187
  187.0 10.7 %all_to_all.80 = bf16[16,32,256]{2,1,0:T(8,128)(2,1)S(1)} all-to-all(bf16[16,32,256]{2,1,0:T(8,128)(2,1)S(1)} %up_product.10), channel_id=1, replica_groups=mesh['sweep'=8,'layer'=16] {'layer'}, dimensions={0} | all-to-all | bytes 524288 | tf_op jit(solution)/shard_map/all_to_all | solution.py:187
  202.1 10.7 %all_to_all.81 = bf16[16,32,256]{2,1,0:T(8,128)(2,1)S(1)} all-to-all(bf16[16,32,256]{2,1,0:T(8,128)(2,1)S(1)} %up_product.11), channel_id=1, replica_groups=mesh['sweep'=8,'layer'=16] {'layer'}, dimensions={0} | all-to-all | bytes 524288 | tf_op jit(solution)/shard_map/all_to_all | solution.py:187
  215.8 20.4 %collective-permute-start.23 = (bf16[32,512]{1,0:T(8,128)(2,1)S(1)}, bf16[32,512]{1,0:T(8,128)(2,1)S(1)}, u32[]{:S(2)}, u32[]{:S(2)}) collective-permute-start(bf16[32,512]{1,0:T(8,128)(2,1)S(1)} %pad_maximum_fusion.6), channel_id=1, source_target_pairs={{32,0},{0,32},{48,16},{16,48},{33,1},{1,33},{49,17},{17,49},{34,2}... | collective-permute-start | bytes 98312 | tf_op jit(solution)/shard_map/ppermute | solution.py:184
  239.0 10.5 %all_to_all.82 = bf16[16,32,256]{2,1,0:T(8,128)(2,1)S(1)} all-to-all(bf16[16,32,256]{2,1,0:T(8,128)(2,1)S(1)} %up_product.12), channel_id=1, replica_groups=mesh['sweep'=8,'layer'=16] {'layer'}, dimensions={0} | all-to-all | bytes 524288 | tf_op jit(solution)/shard_map/all_to_all | solution.py:187
  249.5 2.8 %collective-permute-start.24 = (bf16[32,256]{1,0:T(8,128)(2,1)S(1)}, bf16[32,256]{1,0:T(8,128)(2,1)S(1)}, u32[]{:S(2)}, u32[]{:S(2)}) collective-permute-start(bf16[32,256]{1,0:T(8,128)(2,1)S(1)} %add_convert_fusion.1), channel_id=1, source_target_pairs={{0,16},{16,0},{32,48},{48,32},{64,80},{80,64},{96,112},{112,96},{1... | collective-permute-start | bytes 49160 | tf_op jit(solution)/shard_map/ppermute | solution.py:180
  254.7 10.7 %all_to_all.83 = bf16[16,32,256]{2,1,0:T(8,128)(2,1)S(1)} all-to-all(bf16[16,32,256]{2,1,0:T(8,128)(2,1)S(1)} %up_product.13), channel_id=1, replica_groups=mesh['sweep'=8,'layer'=16] {'layer'}, dimensions={0} | all-to-all | bytes 524288 | tf_op jit(solution)/shard_map/all_to_all | solution.py:187
  (117 shorter events, 62.0 us)
Async XLA Ops:
  0.8 2.3 collective-permute-start
  10.0 15.0 %collective-permute-start.1 = (bf16[2,512,4096]{2,1,0:T(8,128)(2,1)}, bf16[2,512,4096]{2,1,0:T(8,128)(2,1)}, u32[]{:S(2)}, u32[]{:S(2)}) collective-permute-start(bf16[2,512,4096]{2,1,0:T(8,128)(2,1)} %second_halves.1), channel_id=1, source_target_pairs={{0,16},{16,0},{32,48},{48,32},{64,80},{80,64},{96,112},{112,96},{1... | collective-permute-start | bytes 25165832 | tf_op jit(solution)/shard_map/ppermute | solution.py:180
  29.1 2.6 collective-permute-start.2
  31.7 4.0 %collective-permute-start.4 = (f32[32,512]{1,0:T(8,128)S(1)}, f32[32,512]{1,0:T(8,128)S(1)}, u32[]{:S(2)}, u32[]{:S(2)}) collective-permute-start(f32[32,512]{1,0:T(8,128)S(1)} %bitcast.26), channel_id=1, source_target_pairs={{0,16},{16,0},{32,48},{48,32},{64,80},{80,64},{96,112},{112,96},{1... | collective-permute-start | bytes 196616 | tf_op jit(solution)/shard_map/ppermute | solution.py:180
  32.2 4.7 %collective-permute-start.3 = (bf16[32,256]{1,0:T(8,128)(2,1)S(1)}, bf16[32,256]{1,0:T(8,128)(2,1)S(1)}, u32[]{:S(2)}, u32[]{:S(2)}) collective-permute-start(bf16[32,256]{1,0:T(8,128)(2,1)S(1)} %convert_element_type.68), channel_id=1, source_target_pairs={{0,32},{32,0},{16,48},{48,16},{1,33},{33,1},{17,49},{49,17},{2,34}... | collective-permute-start | bytes 49160 | tf_op jit(solution)/shard_map/ppermute | solution.py:184
  52.2 3.5 %collective-permute-start.5 = (f32[32,256]{1,0:T(8,128)S(1)}, f32[32,256]{1,0:T(8,128)S(1)}, u32[]{:S(2)}, u32[]{:S(2)}) collective-permute-start(f32[32,256]{1,0:T(8,128)S(1)} %get-tuple-element.61), channel_id=1, source_target_pairs={{0,16},{16,0},{32,48},{48,32},{64,80},{80,64},{96,112},{112,96},{1... | collective-permute-start | bytes 98312 | tf_op jit(solution)/shard_map/ppermute | solution.py:180
  69.0 2.8 %collective-permute-start.6 = (f32[32,256]{1,0:T(8,128)S(1)}, f32[32,256]{1,0:T(8,128)S(1)}, u32[]{:S(2)}, u32[]{:S(2)}) collective-permute-start(f32[32,256]{1,0:T(8,128)S(1)} %get-tuple-element.64), channel_id=1, source_target_pairs={{0,16},{16,0},{32,48},{48,32},{64,80},{80,64},{96,112},{112,96},{1... | collective-permute-start | bytes 98312 | tf_op jit(solution)/shard_map/ppermute | solution.py:180
  85.8 2.8 %collective-permute-start.8 = (f32[32,256]{1,0:T(8,128)S(1)}, f32[32,256]{1,0:T(8,128)S(1)}, u32[]{:S(2)}, u32[]{:S(2)}) collective-permute-start(f32[32,256]{1,0:T(8,128)S(1)} %get-tuple-element.67), channel_id=1, source_target_pairs={{0,16},{16,0},{32,48},{48,32},{64,80},{80,64},{96,112},{112,96},{1... | collective-permute-start | bytes 98312 | tf_op jit(solution)/shard_map/ppermute | solution.py:180
  101.9 2.8 %collective-permute-start.9 = (f32[32,256]{1,0:T(8,128)S(1)}, f32[32,256]{1,0:T(8,128)S(1)}, u32[]{:S(2)}, u32[]{:S(2)}) collective-permute-start(f32[32,256]{1,0:T(8,128)S(1)} %get-tuple-element.69), channel_id=1, source_target_pairs={{0,16},{16,0},{32,48},{48,32},{64,80},{80,64},{96,112},{112,96},{1... | collective-permute-start | bytes 98312 | tf_op jit(solution)/shard_map/ppermute | solution.py:180
  104.8 0.7 collective-permute-start.10
  118.8 2.8 %collective-permute-start.11 = (f32[32,256]{1,0:T(8,128)S(1)}, f32[32,256]{1,0:T(8,128)S(1)}, u32[]{:S(2)}, u32[]{:S(2)}) collective-permute-start(f32[32,256]{1,0:T(8,128)S(1)} %get-tuple-element.71), channel_id=1, source_target_pairs={{0,16},{16,0},{32,48},{48,32},{64,80},{80,64},{96,112},{112,96},{1... | collective-permute-start | bytes 98312 | tf_op jit(solution)/shard_map/ppermute | solution.py:180
  134.9 2.8 %collective-permute-start.13 = (f32[32,256]{1,0:T(8,128)S(1)}, f32[32,256]{1,0:T(8,128)S(1)}, u32[]{:S(2)}, u32[]{:S(2)}) collective-permute-start(f32[32,256]{1,0:T(8,128)S(1)} %get-tuple-element.77), channel_id=1, source_target_pairs={{0,16},{16,0},{32,48},{48,32},{64,80},{80,64},{96,112},{112,96},{1... | collective-permute-start | bytes 98312 | tf_op jit(solution)/shard_map/ppermute | solution.py:180
  136.9 1.2 collective-permute-start.14
  137.0 1.3 collective-permute-start.15
  137.4 1.2 collective-permute-start.12
  151.2 2.6 collective-permute-start.16
  153.8 0.7 collective-permute-start.17
  166.8 2.8 %collective-permute-start.18 = (bf16[32,256]{1,0:T(8,128)(2,1)S(1)}, bf16[32,256]{1,0:T(8,128)(2,1)S(1)}, u32[]{:S(2)}, u32[]{:S(2)}) collective-permute-start(bf16[32,256]{1,0:T(8,128)(2,1)S(1)} %add_convert_fusion.5), channel_id=1, source_target_pairs={{0,16},{16,0},{32,48},{48,32},{64,80},{80,64},{96,112},{112,96},{1... | collective-permute-start | bytes 49160 | tf_op jit(solution)/shard_map/ppermute | solution.py:180
  182.0 2.8 %collective-permute-start.19 = (bf16[32,256]{1,0:T(8,128)(2,1)S(1)}, bf16[32,256]{1,0:T(8,128)(2,1)S(1)}, u32[]{:S(2)}, u32[]{:S(2)}) collective-permute-start(bf16[32,256]{1,0:T(8,128)(2,1)S(1)} %add_convert_fusion.4), channel_id=1, source_target_pairs={{0,16},{16,0},{32,48},{48,32},{64,80},{80,64},{96,112},{112,96},{1... | collective-permute-start | bytes 49160 | tf_op jit(solution)/shard_map/ppermute | solution.py:180
  197.8 2.8 %collective-permute-start.21 = (bf16[32,256]{1,0:T(8,128)(2,1)S(1)}, bf16[32,256]{1,0:T(8,128)(2,1)S(1)}, u32[]{:S(2)}, u32[]{:S(2)}) collective-permute-start(bf16[32,256]{1,0:T(8,128)(2,1)S(1)} %add_convert_fusion.3), channel_id=1, source_target_pairs={{0,16},{16,0},{32,48},{48,32},{64,80},{80,64},{96,112},{112,96},{1... | collective-permute-start | bytes 49160 | tf_op jit(solution)/shard_map/ppermute | solution.py:180
  212.9 2.8 %collective-permute-start.22 = (bf16[32,256]{1,0:T(8,128)(2,1)S(1)}, bf16[32,256]{1,0:T(8,128)(2,1)S(1)}, u32[]{:S(2)}, u32[]{:S(2)}) collective-permute-start(bf16[32,256]{1,0:T(8,128)(2,1)S(1)} %add_convert_fusion.2), channel_id=1, source_target_pairs={{0,16},{16,0},{32,48},{48,32},{64,80},{80,64},{96,112},{112,96},{1... | collective-permute-start | bytes 49160 | tf_op jit(solution)/shard_map/ppermute | solution.py:180
  215.8 21.7 %collective-permute-start.23 = (bf16[32,512]{1,0:T(8,128)(2,1)S(1)}, bf16[32,512]{1,0:T(8,128)(2,1)S(1)}, u32[]{:S(2)}, u32[]{:S(2)}) collective-permute-start(bf16[32,512]{1,0:T(8,128)(2,1)S(1)} %pad_maximum_fusion.6), channel_id=1, source_target_pairs={{32,0},{0,32},{48,16},{16,48},{33,1},{1,33},{49,17},{17,49},{34,2}... | collective-permute-start | bytes 98312 | tf_op jit(solution)/shard_map/ppermute | solution.py:184
  249.5 3.6 %collective-permute-start.24 = (bf16[32,256]{1,0:T(8,128)(2,1)S(1)}, bf16[32,256]{1,0:T(8,128)(2,1)S(1)}, u32[]{:S(2)}, u32[]{:S(2)}) collective-permute-start(bf16[32,256]{1,0:T(8,128)(2,1)S(1)} %add_convert_fusion.1), channel_id=1, source_target_pairs={{0,16},{16,0},{32,48},{48,32},{64,80},{80,64},{96,112},{112,96},{1... | collective-permute-start | bytes 49160 | tf_op jit(solution)/shard_map/ppermute | solution.py:180
  265.6 2.8 %collective-permute-start.25 = (f32[32,256]{1,0:T(8,128)S(1)}, f32[32,256]{1,0:T(8,128)S(1)}, u32[]{:S(2)}, u32[]{:S(2)}) collective-permute-start(f32[32,256]{1,0:T(8,128)S(1)} %select_n.141), channel_id=1, source_target_pairs={{0,16},{16,0},{32,48},{48,32},{64,80},{80,64},{96,112},{112,96},{1... | collective-permute-start | bytes 98312 | tf_op jit(solution)/shard_map/ppermute | solution.py:180
  (4 other events, 15.5 us)

commit v6 on v5

--- a/solution.py
+++ b/solution.py
@@ -71,50 +71,60 @@
     )(matrix)
 
 
-def load_product(me, on_core, matrix, received, blocks, keeps_first, base):
+def load_product(me, on_core, late, matrix, received, blocks, keeps_first, base):
     chips, rhs, wide = blocks.shape
     parts, rows, cols = matrix.shape
 
-    pieces = len(received)
-    per = chips // pieces
-
-    def body(me_ref, matrix_ref, *refs):
-        received_refs = refs[:pieces]
-        x_ref, first_ref, base_ref, mine_ref, theirs_ref, out_ref, sems = refs[pieces:]
+    def body(me_ref, matrix_ref, received_ref, x_ref, first_ref, base_ref, mine_ref, theirs_ref, out_ref, sems):
+        index = me_ref[0]
 
         def copy(source_ref, at, i):
             here = pl.ds(i * wide, wide)
-            return pltpu.make_async_copy(source_ref.at[:, :, pl.ds(at, wide)], out_ref.at[:, :, here], sems.at[i])
-
-        @pl.when(me_ref[0] % 2 == on_core)
+            return pltpu.make_async_copy(source_ref.at[:, :, pl.ds(at, wide)], out_ref.at[pl.ds(0, parts), :, here], sems.at[i])
+
+        @pl.when(index % 2 == on_core)
         def _():
             for i in range(chips):
                 copy(matrix_ref, 2 * i * wide, i).start()
 
-        @pl.when(me_ref[0] % 2 != on_core)
+        @pl.when(index % 2 != on_core)
         def _():
             for i in range(chips):
-                copy(received_refs[i // per], i % per * wide, i).start()
-
-        sums = None
-        for i in range(chips):
-            copy(matrix_ref, i * wide, i).wait()
-            sums = down_sums(x_ref[i], out_ref.at[:, :, pl.ds(i * wide, wide)], sums)
-        write_down(sums, first_ref, base_ref, mine_ref, theirs_ref)
+                copy(received_ref, i * wide, i).start()
+
+        @pl.when(index < late)
+        def _():
+            sums = None
+            for i in range(chips):
+                copy(matrix_ref, i * wide, i).wait()
+                sums = down_sums(x_ref[i], out_ref.at[:, :, pl.ds(i * wide, wide)], sums)
+            write_down(sums, first_ref, base_ref, mine_ref, theirs_ref)
+
+        @pl.when(index >= late)
+        def _():
+            for i in range(chips):
+                copy(matrix_ref, i * wide, i).wait()
+                at = slice(i * wide, (i + 1) * wide)
+                for part in range(parts):
+                    turned = out_ref[part, :, at].T
+                    out_ref[parts + part, :wide, at] = turned[:, :wide]
+                    out_ref[parts + part, wide:, at] = turned[:, wide:]
+            mine_ref[...] = base_ref[...]
+            theirs_ref[...] = base_ref[...]
 
     part = jax.ShapeDtypeStruct((rhs, wide), F32)
     return pl.pallas_call(
         body,
-        in_specs=[SMEM, HBM, *[HBM] * pieces, VMEM, VMEM, VMEM],
-        out_specs=[VMEM, VMEM, VMEM],
-        out_shape=[part, part, pltpu.VMEM((parts, rows, cols // 2), BF16)],
+        in_specs=[SMEM, HBM, HBM, VMEM, VMEM, VMEM],
+        out_specs=[VMEM] * 3,
+        out_shape=[part, part, pltpu.VMEM((2 * parts, rows, cols // 2), BF16)],
         scratch_shapes=[pltpu.SemaphoreType.DMA((chips,))],
-        compiler_params=pltpu.CompilerParams(vmem_limit_bytes=40 * MIB),
+        compiler_params=pltpu.CompilerParams(vmem_limit_bytes=(16 if on_core == 0 else 32) * MIB),
         cost_estimate=pl.CostEstimate(
             flops=4 * rhs * rows * cols, bytes_accessed=parts * rows * cols, transcendentals=0
         ),
         name="load_product",
-    )(me, matrix, *received, blocks, keeps_first, base)
+    )(me, matrix, received, blocks, keeps_first, base)
 
 
 def vmem_call(body, out_shape, name, flops):
@@ -140,6 +150,22 @@
     write_down(sums, first_ref, base_ref, mine_ref, theirs_ref)
 
 
+def turned_body(x_ref, g_ref, first_ref, base_ref, mine_ref, theirs_ref):
+    chips, rhs, wide = x_ref.shape
+    sums = None
+    for i in range(chips):
+        at = slice(i * wide, (i + 1) * wide)
+        terms = [
+            jnp.concatenate(
+                [jnp.dot(x_ref[i], g_ref[part, rows, at], preferred_element_type=F32) for rows in (slice(0, wide), slice(wide, 2 * wide))],
+                axis=1,
+            )
+            for part in (2, 3)
+        ]
+        sums = terms if sums is None else [total + term for total, term in zip(sums, terms)]
+    write_down(sums, first_ref, base_ref, mine_ref, theirs_ref)
+
+
 def up_body(x_ref, g_ref, out_ref):
     chips, rhs, wide = out_ref.shape
     n = rhs // 2
@@ -200,67 +226,77 @@
     flops = 4 * rhs * rows * cols
     part = jax.ShapeDtypeStruct((rhs, wide), F32)
     down_call = vmem_call(down_body, (part, part), "down_product", flops)
+    turned_call = vmem_call(turned_body, (part, part), "turned_product", flops)
     up_call = vmem_call(up_body, jax.ShapeDtypeStruct((chips, rhs, wide), BF16), "up_product", flops)
 
     def ordered(x, other, first_on_0):
         halves = [jnp.where(on_0, x, other), jnp.where(on_0, other, x)]
         return jnp.concatenate(halves if first_on_0 else halves[::-1], axis=1).astype(BF16)
 
-    def up_product(full, mat, base):
-        return base + jnp.sum(exchange(up_call(full, mat)).astype(F32), axis=0)
+    def up_product(full, mat, base, *beside):
+        blocks = up_call(full, mat)
+        if beside:
+            blocks, base, *beside = tie(blocks, base, *beside)
+        x = base + jnp.sum(exchange(blocks).astype(F32), axis=0)
+        return (x, base, *beside) if beside else x
 
     down_own, up_own = down_source.reshape(rhs, rows), up_source.reshape(rhs, rows)
-    down_got, matrix = tie(swap(down_own[:, :wide]), matrix)
-    pieces = 1
-    received = [
-        swap(second_halves(matrix, j * chips // pieces, chips // pieces, chips)) for j in range(pieces)
-    ]
+    down_got, up_other = swap(down_own[:, :wide]), swap(up_own)
+    sent, down_got, up_other = tie(second_halves(matrix, 0, chips, chips), down_got, up_other)
+    received = swap(sent)
+    up_a = jnp.where(on_0, up_own[:, :wide], up_other[:, wide:])
+    up_b = jnp.where(on_0, up_other[:, wide:], up_own[:, :wide])
+    up_b_rest = jnp.where(on_0, up_other[:, :wide], up_own[:, wide:])
     base_a = jnp.where(on_0, down_own[:, wide:], down_got)
     base_b = jnp.where(on_0, down_got, down_own[:, wide:])
     down_a, down_b = base_a, base_b
 
-    x, me, tile_0, tile_1, on_0, masks = tie(base_a, me, tile_0, tile_1, on_0, masks)
+    x, base_b, up_a, up_b, up_b_rest, me, tile_0, tile_1, on_0, masks = tie(
+        base_a, base_b, up_a, up_b, up_b_rest, me, tile_0, tile_1, on_0, masks
+    )
+    late = 4
     for p in range(planes):
         if p > 0:
-            x = hop(x.astype(BF16), p - 1, p)
+            blocks = spread(hop(x.astype(BF16), p - 1, p))
             if p == 1:
-                x, up_a, up_b, up_b_rest = tie(x, up_a, up_b, up_b_rest)
-                mine, theirs, matrix_a = load_product(me, 0, matrix, received, spread(x), tile_1, base_a)
+                mine, theirs, matrix_a = load_product(
+                    me, 0, late, matrix, received, blocks, tile_1, base_a
+                )
             else:
-                mine, theirs = down_call(spread(x), matrix_a, tile_1, base_a)
+                mine, theirs = turned_call(blocks, matrix_a, tile_1, base_a)
             x = mine + swap(theirs)
             down_a = jnp.where(masks[p], x, down_a)
         blocks = spread(x)
         if p == 0:
-            mine, theirs, matrix_b = load_product(me, 1, matrix, received, blocks, tile_0, base_b)
+            mine, theirs, matrix_b = load_product(me, 1, late, matrix, received, blocks, tile_0, base_b)
+        elif p == 1:
+            mine, theirs = down_call(blocks, matrix_b, tile_0, base_b)
         else:
-            mine, theirs = down_call(blocks, matrix_b, tile_0, base_b)
+            mine, theirs = turned_call(blocks, matrix_b, tile_0, base_b)
         if p == planes - 1:
             break
         x = mine + swap(theirs)
         down_b = jnp.where(masks[p], x, down_b)
-        if p == 0:
-            x, up_own = tie(x, up_own)
-            up_other = swap(up_own)
-            up_a = jnp.where(on_0, up_own[:, :wide], up_other[:, wide:])
-            up_b = jnp.where(on_0, up_other[:, wide:], up_own[:, :wide])
-            up_b_rest = jnp.where(on_0, up_other[:, :wide], up_own[:, wide:])
 
     mine, theirs, down_a, down_b = tie(mine, theirs, down_a, down_b)
     rest = up_b_rest + (mine + swap(theirs))
     x = up_b + (theirs + swap(mine))
+    x, rest, down_a, down_b = tie(x, rest, down_a, down_b)
     base_b = up_b + swap(down_b)
     base_a = up_a + swap(down_a)
-    x, rest, base_a, base_b = tie(x, rest, base_a, base_b)
-    total_a, total_b = base_a, jnp.where(masks[planes - 1], x, base_b)
+    last_b = x
     full = ordered(x, rest, False)
     for p in reversed(range(planes)):
         if p < planes - 1:
             x = up_product(hop(full, p + 1, p), matrix_b, base_b)
             total_b = jnp.where(masks[p], x, total_b)
             full = ordered(x.astype(BF16), swap(x.astype(BF16)), False)
-        x = up_product(full, matrix_a, base_a)
-        total_a = jnp.where(masks[p], x, total_a)
+        if p == planes - 1:
+            x, base_a, base_b, last_b = up_product(full, matrix_a, base_a, base_b, last_b)
+            total_a, total_b = x, jnp.where(masks[p], last_b, base_b)
+        else:
+            x = up_product(full, matrix_a, base_a)
+            total_a = jnp.where(masks[p], x, total_a)
         if p > 0:
             full = ordered(x.astype(BF16), swap(x.astype(BF16)), True)
 

time: 270 us -> 265 us (0.981)
  Pallas kernels: 38.6 us -> 34.4 us
    pallas_call x12, Pallas kernels: 23.4 us -> 19.3 us  [call(): pl.pallas_call(body, in_specs=[VMEM] * len(args), out_specs=jax.tree.map(...]
  transfers between devices with their start and end apart: 26 -> 26, of which waited for: 20 -> 17; matrix products, arithmetic and copies ran while one was open for 0% -> 0% of each run, Pallas kernels for 0% -> 3%
where the time goes in v6:
time: 265 us; the launch traced here: 264 us
  blocking collectives  154 us (58%)
  starting transfers between devices  58.1 us (22%)
  Pallas kernels  34.4 us (13%)
  waiting for transfers between devices  14.6 us (6%)
    all_to_all x14, blocking collectives, exchange(): return lax.all_to_all(blocks, 'layer', 0, 0, tiled=True)  154 us
    ppermute x20, starting transfers between devices, swap(): return lax.ppermute(x, 'sweep', [(i, i ^ 1) for i in range(2 * planes)])  31.5 us
    ppermute x6, starting transfers between devices, hop(): return lax.ppermute(x, 'sweep', pairs)  26.6 us
    pallas_call x12, Pallas kernels, call(): pl.pallas_call(body, in_specs=[VMEM] * len(args), out_specs=jax.tree.map(...  19.3 us
    ppermute x20, waiting for transfers between devices, swap(): return lax.ppermute(x, 'sweep', [(i, i ^ 1) for i in range(2 * planes)])  12.2 us
    pallas_call x2, Pallas kernels, load_product(): pl.pallas_call(body, in_specs=[SMEM, HBM, HBM, VMEM, VMEM, VMEM], out_spe...  8.12 us
    pallas_call x1, Pallas kernels, second_halves(): pl.pallas_call(body, in_specs=[HBM], out_specs=HBM, out_shape=pltpu.HBM((...  6.94 us
  transfers between devices with their start and end apart: 26, of which 17 were waited for; matrix products, arithmetic and copies ran while one was open for 0% of the time, Pallas kernels for 3%

profile of v6, /device:TPU:1, one launch (start us, length us, event | category | flops | bytes accessed | tf_op | source)
XLA Modules:
  0.0 264.2 jit_solution(16988574891031228995)
XLA Ops:
  2.3 6.9 %second_halves.1 = bf16[2,512,4096]{2,1,0:T(8,128)(2,1)} custom-call(bf16[2,512,8192]{2,1,0:T(8,128)(2,1)} %bitcast.20), custom_call_target="tpu_custom_call" | custom-call | tf_op jit(solution)/shard_map/second_halves/pallas_call | solution.py:59
  9.9 14.4 %all_to_all.70.x_ref = bf16[16,32,256]{2,1,0:T(8,128)(2,1)S(1)} all-to-all(bf16[16,32,256]{2,1,0:T(8,128)(2,1)S(1)} %broadcast_in_dim.21), channel_id=1, replica_groups=mesh['sweep'=8,'layer'=16] {'layer'}, dimensions={0} | all-to-all | bytes 524288 | tf_op jit(solution)/shard_map/all_to_all | solution.py:213
  24.3 4.1 %load_product.2 = (f32[32,256]{1,0:T(8,128)S(1)}, f32[32,256]{1,0:T(8,128)S(1)}, bf16[4,512,4096]{2,1,0:T(8,128)(2,1)S(1)}) custom-call(s32[1]{0:T(128)} %bitcast.me_ref, bf16[2,512,8192]{2,1,0:T(8,128)(2,1)} %bitcast.21, bf16[2,512,4096]{2,1,0:T(8,128)(2,1)} %collective-permute-done.2.received_ref, bf16[16,32,256]{2,1,0:T(8,128)(2,1)S(1)} %all_to_all.70.x_ref, ...), custom_call_target="tpu_custom_call" | custom-call | flops 536870912 | bytes 8388608 | tf_op jit(solution)/shard_map/load_product/pallas_call | solution.py:116
  31.0 3.5 %collective-permute-start.4 = (bf16[32,256]{1,0:T(8,128)(2,1)S(1)}, bf16[32,256]{1,0:T(8,128)(2,1)S(1)}, u32[]{:S(2)}, u32[]{:S(2)}) collective-permute-start(bf16[32,256]{1,0:T(8,128)(2,1)S(1)} %add_convert_fusion.10), channel_id=1, source_target_pairs={{0,32},{32,0},{16,48},{48,16},{1,33},{33,1},{17,49},{49,17},{2,34}... | collective-permute-start | bytes 49160 | tf_op jit(solution)/shard_map/ppermute | solution.py:210
  35.7 11.2 %all_to_all.71.x_ref = bf16[16,32,256]{2,1,0:T(8,128)(2,1)S(1)} all-to-all(bf16[16,32,256]{2,1,0:T(8,128)(2,1)S(1)} %broadcast_in_dim.22), channel_id=1, replica_groups=mesh['sweep'=8,'layer'=16] {'layer'}, dimensions={0} | all-to-all | bytes 524288 | tf_op jit(solution)/shard_map/all_to_all | solution.py:213
  46.9 4.1 %load_product.3 = (f32[32,256]{1,0:T(8,128)S(1)}, f32[32,256]{1,0:T(8,128)S(1)}, bf16[4,512,4096]{2,1,0:T(8,128)(2,1)S(1)}) custom-call(s32[1]{0:T(128)} %bitcast.me_ref, bf16[2,512,8192]{2,1,0:T(8,128)(2,1)} %bitcast.22, bf16[2,512,4096]{2,1,0:T(8,128)(2,1)} %collective-permute-done.2.received_ref, bf16[16,32,256]{2,1,0:T(8,128)(2,1)S(1)} %all_to_all.71.x_ref, ...), custom_call_target="tpu_custom_call" | custom-call | flops 536870912 | bytes 8388608 | tf_op jit(solution)/shard_map/load_product/pallas_call | solution.py:116
  51.0 2.9 %collective-permute-start.5 = (f32[32,256]{1,0:T(8,128)S(1)}, f32[32,256]{1,0:T(8,128)S(1)}, u32[]{:S(2)}, u32[]{:S(2)}) collective-permute-start(f32[32,256]{1,0:T(8,128)S(1)} %get-tuple-element.63), channel_id=1, source_target_pairs={{0,16},{16,0},{32,48},{48,32},{64,80},{80,64},{96,112},{112,96},{1... | collective-permute-start | bytes 98312 | tf_op jit(solution)/shard_map/ppermute | solution.py:206
  54.7 10.7 %all_to_all.72.x_ref = bf16[16,32,256]{2,1,0:T(8,128)(2,1)S(1)} all-to-all(bf16[16,32,256]{2,1,0:T(8,128)(2,1)S(1)} %broadcast_in_dim.23), channel_id=1, replica_groups=mesh['sweep'=8,'layer'=16] {'layer'}, dimensions={0} | all-to-all | bytes 524288 | tf_op jit(solution)/shard_map/all_to_all | solution.py:213
  65.5 2.5 down_product.1
  68.0 2.0 collective-permute-start.6
  71.5 10.7 %all_to_all.73.x_ref = bf16[16,32,256]{2,1,0:T(8,128)(2,1)S(1)} all-to-all(bf16[16,32,256]{2,1,0:T(8,128)(2,1)S(1)} %broadcast_in_dim.24), channel_id=1, replica_groups=mesh['sweep'=8,'layer'=16] {'layer'}, dimensions={0} | all-to-all | bytes 524288 | tf_op jit(solution)/shard_map/all_to_all | solution.py:213
  86.7 10.7 %all_to_all.74.x_ref = bf16[16,32,256]{2,1,0:T(8,128)(2,1)S(1)} all-to-all(bf16[16,32,256]{2,1,0:T(8,128)(2,1)S(1)} %broadcast_in_dim.25), channel_id=1, replica_groups=mesh['sweep'=8,'layer'=16] {'layer'}, dimensions={0} | all-to-all | bytes 524288 | tf_op jit(solution)/shard_map/all_to_all | solution.py:213
  102.5 10.7 %all_to_all.75.x_ref = bf16[16,32,256]{2,1,0:T(8,128)(2,1)S(1)} all-to-all(bf16[16,32,256]{2,1,0:T(8,128)(2,1)S(1)} %broadcast_in_dim.26), channel_id=1, replica_groups=mesh['sweep'=8,'layer'=16] {'layer'}, dimensions={0} | all-to-all | bytes 524288 | tf_op jit(solution)/shard_map/all_to_all | solution.py:213
  114.8 2.0 collective-permute-start.11
  117.7 10.7 %all_to_all.76.x_ref = bf16[16,32,256]{2,1,0:T(8,128)(2,1)S(1)} all-to-all(bf16[16,32,256]{2,1,0:T(8,128)(2,1)S(1)} %broadcast_in_dim.27), channel_id=1, replica_groups=mesh['sweep'=8,'layer'=16] {'layer'}, dimensions={0} | all-to-all | bytes 524288 | tf_op jit(solution)/shard_map/all_to_all | solution.py:213
  135.4 10.9 %all_to_all.77 = bf16[16,32,256]{2,1,0:T(8,128)(2,1)S(1)} all-to-all(bf16[16,32,256]{2,1,0:T(8,128)(2,1)S(1)} %up_product.7), channel_id=1, replica_groups=mesh['sweep'=8,'layer'=16] {'layer'}, dimensions={0} | all-to-all | bytes 524288 | tf_op jit(solution)/shard_map/all_to_all | solution.py:213
  151.2 10.7 %all_to_all.78 = bf16[16,32,256]{2,1,0:T(8,128)(2,1)S(1)} all-to-all(bf16[16,32,256]{2,1,0:T(8,128)(2,1)S(1)} %up_product.8), channel_id=1, replica_groups=mesh['sweep'=8,'layer'=16] {'layer'}, dimensions={0} | all-to-all | bytes 524288 | tf_op jit(solution)/shard_map/all_to_all | solution.py:213
  166.3 10.7 %all_to_all.79 = bf16[16,32,256]{2,1,0:T(8,128)(2,1)S(1)} all-to-all(bf16[16,32,256]{2,1,0:T(8,128)(2,1)S(1)} %up_product.9), channel_id=1, replica_groups=mesh['sweep'=8,'layer'=16] {'layer'}, dimensions={0} | all-to-all | bytes 524288 | tf_op jit(solution)/shard_map/all_to_all | solution.py:213
  182.2 10.7 %all_to_all.80 = bf16[16,32,256]{2,1,0:T(8,128)(2,1)S(1)} all-to-all(bf16[16,32,256]{2,1,0:T(8,128)(2,1)S(1)} %up_product.10), channel_id=1, replica_groups=mesh['sweep'=8,'layer'=16] {'layer'}, dimensions={0} | all-to-all | bytes 524288 | tf_op jit(solution)/shard_map/all_to_all | solution.py:213
  197.3 10.7 %all_to_all.81 = bf16[16,32,256]{2,1,0:T(8,128)(2,1)S(1)} all-to-all(bf16[16,32,256]{2,1,0:T(8,128)(2,1)S(1)} %up_product.11), channel_id=1, replica_groups=mesh['sweep'=8,'layer'=16] {'layer'}, dimensions={0} | all-to-all | bytes 524288 | tf_op jit(solution)/shard_map/all_to_all | solution.py:213
  210.9 20.4 %collective-permute-start.23 = (bf16[32,512]{1,0:T(8,128)(2,1)S(1)}, bf16[32,512]{1,0:T(8,128)(2,1)S(1)}, u32[]{:S(2)}, u32[]{:S(2)}) collective-permute-start(bf16[32,512]{1,0:T(8,128)(2,1)S(1)} %pad_maximum_fusion.6), channel_id=1, source_target_pairs={{32,0},{0,32},{48,16},{16,48},{33,1},{1,33},{49,17},{17,49},{34,2}... | collective-permute-start | bytes 98312 | tf_op jit(solution)/shard_map/ppermute | solution.py:210
  234.2 10.5 %all_to_all.82 = bf16[16,32,256]{2,1,0:T(8,128)(2,1)S(1)} all-to-all(bf16[16,32,256]{2,1,0:T(8,128)(2,1)S(1)} %up_product.12), channel_id=1, replica_groups=mesh['sweep'=8,'layer'=16] {'layer'}, dimensions={0} | all-to-all | bytes 524288 | tf_op jit(solution)/shard_map/all_to_all | solution.py:213
  244.7 2.8 %collective-permute-start.24 = (bf16[32,256]{1,0:T(8,128)(2,1)S(1)}, bf16[32,256]{1,0:T(8,128)(2,1)S(1)}, u32[]{:S(2)}, u32[]{:S(2)}) collective-permute-start(bf16[32,256]{1,0:T(8,128)(2,1)S(1)} %add_convert_fusion), channel_id=1, source_target_pairs={{0,16},{16,0},{32,48},{48,32},{64,80},{80,64},{96,112},{112,96},{1... | collective-permute-start | bytes 49160 | tf_op jit(solution)/shard_map/ppermute | solution.py:206
  249.9 10.7 %all_to_all.83 = bf16[16,32,256]{2,1,0:T(8,128)(2,1)S(1)} all-to-all(bf16[16,32,256]{2,1,0:T(8,128)(2,1)S(1)} %up_product.13), channel_id=1, replica_groups=mesh['sweep'=8,'layer'=16] {'layer'}, dimensions={0} | all-to-all | bytes 524288 | tf_op jit(solution)/shard_map/all_to_all | solution.py:213
  (116 shorter events, 58.2 us)
Async XLA Ops:
  0.0 9.2 %collective-permute-start.1 = (f32[32,512]{1,0:T(8,128)}, f32[32,512]{1,0:T(8,128)S(1)}, u32[]{:S(2)}, u32[]{:S(2)}) collective-permute-start(f32[32,512]{1,0:T(8,128)} %bitcast.23), channel_id=1, source_target_pairs={{0,16},{16,0},{32,48},{48,32},{64,80},{80,64},{96,112},{112,96},{1... | collective-permute-start | bytes 196616 | tf_op jit(solution)/shard_map/ppermute | solution.py:206
  2.2 7.0 %collective-permute-start = (f32[32,256]{1,0:T(8,128)S(1)}, f32[32,256]{1,0:T(8,128)S(1)}, u32[]{:S(2)}, u32[]{:S(2)}) collective-permute-start(f32[32,256]{1,0:T(8,128)S(1)} %slice.53), channel_id=1, source_target_pairs={{0,16},{16,0},{32,48},{48,32},{64,80},{80,64},{96,112},{112,96},{1... | collective-permute-start | bytes 98312 | tf_op jit(solution)/shard_map/ppermute | solution.py:206
  9.2 15.0 %collective-permute-start.2 = (bf16[2,512,4096]{2,1,0:T(8,128)(2,1)}, bf16[2,512,4096]{2,1,0:T(8,128)(2,1)}, u32[]{:S(2)}, u32[]{:S(2)}) collective-permute-start(bf16[2,512,4096]{2,1,0:T(8,128)(2,1)} %second_halves.1), channel_id=1, source_target_pairs={{0,16},{16,0},{32,48},{48,32},{64,80},{80,64},{96,112},{112,96},{1... | collective-permute-start | bytes 25165832 | tf_op jit(solution)/shard_map/ppermute | solution.py:206
  28.3 2.7 %collective-permute-start.3 = (f32[32,256]{1,0:T(8,128)S(1)}, f32[32,256]{1,0:T(8,128)S(1)}, u32[]{:S(2)}, u32[]{:S(2)}) collective-permute-start(f32[32,256]{1,0:T(8,128)S(1)} %get-tuple-element.60), channel_id=1, source_target_pairs={{0,16},{16,0},{32,48},{48,32},{64,80},{80,64},{96,112},{112,96},{1... | collective-permute-start | bytes 98312 | tf_op jit(solution)/shard_map/ppermute | solution.py:206
  31.0 4.7 %collective-permute-start.4 = (bf16[32,256]{1,0:T(8,128)(2,1)S(1)}, bf16[32,256]{1,0:T(8,128)(2,1)S(1)}, u32[]{:S(2)}, u32[]{:S(2)}) collective-permute-start(bf16[32,256]{1,0:T(8,128)(2,1)S(1)} %add_convert_fusion.10), channel_id=1, source_target_pairs={{0,32},{32,0},{16,48},{48,16},{1,33},{33,1},{17,49},{49,17},{2,34}... | collective-permute-start | bytes 49160 | tf_op jit(solution)/shard_map/ppermute | solution.py:210
  51.0 3.7 %collective-permute-start.5 = (f32[32,256]{1,0:T(8,128)S(1)}, f32[32,256]{1,0:T(8,128)S(1)}, u32[]{:S(2)}, u32[]{:S(2)}) collective-permute-start(f32[32,256]{1,0:T(8,128)S(1)} %get-tuple-element.63), channel_id=1, source_target_pairs={{0,16},{16,0},{32,48},{48,32},{64,80},{80,64},{96,112},{112,96},{1... | collective-permute-start | bytes 98312 | tf_op jit(solution)/shard_map/ppermute | solution.py:206
  68.0 2.8 %collective-permute-start.6 = (f32[32,256]{1,0:T(8,128)S(1)}, f32[32,256]{1,0:T(8,128)S(1)}, u32[]{:S(2)}, u32[]{:S(2)}) collective-permute-start(f32[32,256]{1,0:T(8,128)S(1)} %get-tuple-element.66), channel_id=1, source_target_pairs={{0,16},{16,0},{32,48},{48,32},{64,80},{80,64},{96,112},{112,96},{1... | collective-permute-start | bytes 98312 | tf_op jit(solution)/shard_map/ppermute | solution.py:206
  83.8 2.8 %collective-permute-start.8 = (f32[32,256]{1,0:T(8,128)S(1)}, f32[32,256]{1,0:T(8,128)S(1)}, u32[]{:S(2)}, u32[]{:S(2)}) collective-permute-start(f32[32,256]{1,0:T(8,128)S(1)} %get-tuple-element.69), channel_id=1, source_target_pairs={{0,16},{16,0},{32,48},{48,32},{64,80},{80,64},{96,112},{112,96},{1... | collective-permute-start | bytes 98312 | tf_op jit(solution)/shard_map/ppermute | solution.py:206
  99.0 2.8 %collective-permute-start.9 = (f32[32,256]{1,0:T(8,128)S(1)}, f32[32,256]{1,0:T(8,128)S(1)}, u32[]{:S(2)}, u32[]{:S(2)}) collective-permute-start(f32[32,256]{1,0:T(8,128)S(1)} %get-tuple-element.71), channel_id=1, source_target_pairs={{0,16},{16,0},{32,48},{48,32},{64,80},{80,64},{96,112},{112,96},{1... | collective-permute-start | bytes 98312 | tf_op jit(solution)/shard_map/ppermute | solution.py:206
  101.8 0.7 collective-permute-start.10
  114.8 2.8 %collective-permute-start.11 = (f32[32,256]{1,0:T(8,128)S(1)}, f32[32,256]{1,0:T(8,128)S(1)}, u32[]{:S(2)}, u32[]{:S(2)}) collective-permute-start(f32[32,256]{1,0:T(8,128)S(1)} %get-tuple-element.73), channel_id=1, source_target_pairs={{0,16},{16,0},{32,48},{48,32},{64,80},{80,64},{96,112},{112,96},{1... | collective-permute-start | bytes 98312 | tf_op jit(solution)/shard_map/ppermute | solution.py:206
  130.0 2.8 %collective-permute-start.13 = (f32[32,256]{1,0:T(8,128)S(1)}, f32[32,256]{1,0:T(8,128)S(1)}, u32[]{:S(2)}, u32[]{:S(2)}) collective-permute-start(f32[32,256]{1,0:T(8,128)S(1)} %get-tuple-element.79), channel_id=1, source_target_pairs={{0,16},{16,0},{32,48},{48,32},{64,80},{80,64},{96,112},{112,96},{1... | collective-permute-start | bytes 98312 | tf_op jit(solution)/shard_map/ppermute | solution.py:206
  131.9 1.2 collective-permute-start.12
  133.2 2.2 collective-permute-start.14
  133.4 2.0 collective-permute-start.15
  146.4 2.6 collective-permute-start.16
  149.0 0.7 collective-permute-start.17
  162.0 2.8 %collective-permute-start.18 = (bf16[32,256]{1,0:T(8,128)(2,1)S(1)}, bf16[32,256]{1,0:T(8,128)(2,1)S(1)}, u32[]{:S(2)}, u32[]{:S(2)}) collective-permute-start(bf16[32,256]{1,0:T(8,128)(2,1)S(1)} %add_convert_fusion.4), channel_id=1, source_target_pairs={{0,16},{16,0},{32,48},{48,32},{64,80},{80,64},{96,112},{112,96},{1... | collective-permute-start | bytes 49160 | tf_op jit(solution)/shard_map/ppermute | solution.py:206
  177.1 2.8 %collective-permute-start.19 = (bf16[32,256]{1,0:T(8,128)(2,1)S(1)}, bf16[32,256]{1,0:T(8,128)(2,1)S(1)}, u32[]{:S(2)}, u32[]{:S(2)}) collective-permute-start(bf16[32,256]{1,0:T(8,128)(2,1)S(1)} %add_convert_fusion.3), channel_id=1, source_target_pairs={{0,16},{16,0},{32,48},{48,32},{64,80},{80,64},{96,112},{112,96},{1... | collective-permute-start | bytes 49160 | tf_op jit(solution)/shard_map/ppermute | solution.py:206
  193.0 2.8 %collective-permute-start.21 = (bf16[32,256]{1,0:T(8,128)(2,1)S(1)}, bf16[32,256]{1,0:T(8,128)(2,1)S(1)}, u32[]{:S(2)}, u32[]{:S(2)}) collective-permute-start(bf16[32,256]{1,0:T(8,128)(2,1)S(1)} %add_convert_fusion.2), channel_id=1, source_target_pairs={{0,16},{16,0},{32,48},{48,32},{64,80},{80,64},{96,112},{112,96},{1... | collective-permute-start | bytes 49160 | tf_op jit(solution)/shard_map/ppermute | solution.py:206
  208.1 2.8 %collective-permute-start.22 = (bf16[32,256]{1,0:T(8,128)(2,1)S(1)}, bf16[32,256]{1,0:T(8,128)(2,1)S(1)}, u32[]{:S(2)}, u32[]{:S(2)}) collective-permute-start(bf16[32,256]{1,0:T(8,128)(2,1)S(1)} %add_convert_fusion.1), channel_id=1, source_target_pairs={{0,16},{16,0},{32,48},{48,32},{64,80},{80,64},{96,112},{112,96},{1... | collective-permute-start | bytes 49160 | tf_op jit(solution)/shard_map/ppermute | solution.py:206
  210.9 21.7 %collective-permute-start.23 = (bf16[32,512]{1,0:T(8,128)(2,1)S(1)}, bf16[32,512]{1,0:T(8,128)(2,1)S(1)}, u32[]{:S(2)}, u32[]{:S(2)}) collective-permute-start(bf16[32,512]{1,0:T(8,128)(2,1)S(1)} %pad_maximum_fusion.6), channel_id=1, source_target_pairs={{32,0},{0,32},{48,16},{16,48},{33,1},{1,33},{49,17},{17,49},{34,2}... | collective-permute-start | bytes 98312 | tf_op jit(solution)/shard_map/ppermute | solution.py:210
  244.7 3.6 %collective-permute-start.24 = (bf16[32,256]{1,0:T(8,128)(2,1)S(1)}, bf16[32,256]{1,0:T(8,128)(2,1)S(1)}, u32[]{:S(2)}, u32[]{:S(2)}) collective-permute-start(bf16[32,256]{1,0:T(8,128)(2,1)S(1)} %add_convert_fusion), channel_id=1, source_target_pairs={{0,16},{16,0},{32,48},{48,32},{64,80},{80,64},{96,112},{112,96},{1... | collective-permute-start | bytes 49160 | tf_op jit(solution)/shard_map/ppermute | solution.py:206
  260.7 2.8 %collective-permute-start.25 = (f32[32,256]{1,0:T(8,128)S(1)}, f32[32,256]{1,0:T(8,128)S(1)}, u32[]{:S(2)}, u32[]{:S(2)}) collective-permute-start(f32[32,256]{1,0:T(8,128)S(1)} %select_n.137), channel_id=1, source_target_pairs={{0,16},{16,0},{32,48},{48,32},{64,80},{80,64},{96,112},{112,96},{1... | collective-permute-start | bytes 98312 | tf_op jit(solution)/shard_map/ppermute | solution.py:206
  (4 other events, 21.0 us)

commit v7 on v6

--- a/solution.py
+++ b/solution.py
@@ -75,8 +75,12 @@
     chips, rhs, wide = blocks.shape
     parts, rows, cols = matrix.shape
 
-    def body(me_ref, matrix_ref, received_ref, x_ref, first_ref, base_ref, mine_ref, theirs_ref, out_ref, sems):
-        index = me_ref[0]
+    pieces = len(received)
+
+    def body(me_ref, matrix_ref, *refs):
+        received_refs = refs[:pieces]
+        x_ref, first_ref, base_ref, mine_ref, theirs_ref, out_ref, sems = refs[pieces:]
+        index, per = me_ref[0], chips // pieces
 
         def copy(source_ref, at, i):
             here = pl.ds(i * wide, wide)
@@ -90,7 +94,7 @@
         @pl.when(index % 2 != on_core)
         def _():
             for i in range(chips):
-                copy(received_ref, i * wide, i).start()
+                copy(received_refs[i // per], i % per * wide, i).start()
 
         @pl.when(index < late)
         def _():
@@ -115,7 +119,7 @@
     part = jax.ShapeDtypeStruct((rhs, wide), F32)
     return pl.pallas_call(
         body,
-        in_specs=[SMEM, HBM, HBM, VMEM, VMEM, VMEM],
+        in_specs=[SMEM, HBM, *[HBM] * pieces, VMEM, VMEM, VMEM],
         out_specs=[VMEM] * 3,
         out_shape=[part, part, pltpu.VMEM((2 * parts, rows, cols // 2), BF16)],
         scratch_shapes=[pltpu.SemaphoreType.DMA((chips,))],
@@ -124,7 +128,7 @@
             flops=4 * rhs * rows * cols, bytes_accessed=parts * rows * cols, transcendentals=0
         ),
         name="load_product",
-    )(me, matrix, received, blocks, keeps_first, base)
+    )(me, matrix, *received, blocks, keeps_first, base)
 
 
 def vmem_call(body, out_shape, name, flops):
@@ -206,7 +210,7 @@
         return lax.ppermute(x, "sweep", [(i, i ^ 1) for i in range(2 * planes)])
 
     def hop(x, a, b):
-        pairs = [p for c in range(2) for p in ((2 * a + c, 2 * b + c), (2 * b + c, 2 * a + c))]
+        pairs = [(2 * a + c, 2 * b + c) for c in range(2)]
         return lax.ppermute(x, "sweep", pairs)
 
     def exchange(blocks):
@@ -241,9 +245,11 @@
         return (x, base, *beside) if beside else x
 
     down_own, up_own = down_source.reshape(rhs, rows), up_source.reshape(rhs, rows)
-    down_got, up_other = swap(down_own[:, :wide]), swap(up_own)
-    sent, down_got, up_other = tie(second_halves(matrix, 0, chips, chips), down_got, up_other)
-    received = swap(sent)
+    half = chips // 2
+    sent_0, matrix, down_own, up_own = tie(second_halves(matrix, 0, half, chips), matrix, down_own, up_own)
+    down_got, up_other, received_0 = swap(down_own[:, :wide]), swap(up_own), swap(sent_0)
+    sent_1, down_got, up_other = tie(second_halves(matrix, half, chips - half, chips), down_got, up_other)
+    received = (received_0, swap(sent_1))
     up_a = jnp.where(on_0, up_own[:, :wide], up_other[:, wide:])
     up_b = jnp.where(on_0, up_other[:, wide:], up_own[:, :wide])
     up_b_rest = jnp.where(on_0, up_other[:, :wide], up_own[:, wide:])

time: 265 us -> 260 us (0.981)
  starting transfers between devices: 58.1 us -> 39.2 us
  waiting for transfers between devices: 14.6 us -> 29.1 us
    ppermute x6, starting transfers between devices: 26.6 us -> 7.45 us  [hop(): return lax.ppermute(x, 'sweep', pairs)]
    ppermute x6, waiting for transfers between devices: 2.41 us -> 16.9 us  [hop(): return lax.ppermute(x, 'sweep', pairs)]
    pallas_call x1 -> x2, Pallas kernels: 6.94 us -> 7.73 us  [second_halves(): pl.pallas_call(body, in_specs=[HBM], out_specs=HBM, out_shape=pltpu.HBM((...]
    ppermute x20 -> x21, starting transfers between devices: 31.5 us -> 31.8 us  [swap(): return lax.ppermute(x, 'sweep', [(i, i ^ 1) for i in range(2 * planes)])]
    ppermute x20 -> x21, waiting for transfers between devices: 12.2 us -> 12.2 us  [swap(): return lax.ppermute(x, 'sweep', [(i, i ^ 1) for i in range(2 * planes)])]
  transfers between devices with their start and end apart: 26 -> 27, of which waited for: 17 -> 17; matrix products, arithmetic and copies ran while one was open for 0% -> 0% of each run, Pallas kernels for 3% -> 2%
where the time goes in v7:
time: 260 us; the launch traced here: 259 us
  blocking collectives  153 us (59%)
  starting transfers between devices  39.2 us (15%)
  Pallas kernels  35.2 us (14%)
  waiting for transfers between devices  29.1 us (11%)
    all_to_all x14, blocking collectives, exchange(): return lax.all_to_all(blocks, 'layer', 0, 0, tiled=True)  153 us
    ppermute x21, starting transfers between devices, swap(): return lax.ppermute(x, 'sweep', [(i, i ^ 1) for i in range(2 * planes)])  31.8 us
    pallas_call x12, Pallas kernels, call(): pl.pallas_call(body, in_specs=[VMEM] * len(args), out_specs=jax.tree.map(...  19.3 us
    ppermute x6, waiting for transfers between devices, hop(): return lax.ppermute(x, 'sweep', pairs)  16.9 us
    ppermute x21, waiting for transfers between devices, swap(): return lax.ppermute(x, 'sweep', [(i, i ^ 1) for i in range(2 * planes)])  12.2 us
    pallas_call x2, Pallas kernels, load_product(): pl.pallas_call(body, in_specs=[SMEM, HBM, *[HBM] * pieces, VMEM, VMEM, VM...  8.11 us
    pallas_call x2, Pallas kernels, second_halves(): pl.pallas_call(body, in_specs=[HBM], out_specs=HBM, out_shape=pltpu.HBM((...  7.73 us
    ppermute x6, starting transfers between devices, hop(): return lax.ppermute(x, 'sweep', pairs)  7.45 us
  transfers between devices with their start and end apart: 27, of which 17 were waited for; matrix products, arithmetic and copies ran while one was open for 0% of the time, Pallas kernels for 2%

profile of v7, /device:TPU:1, one launch (start us, length us, event | category | flops | bytes accessed | tf_op | source)
XLA Modules:
  0.0 258.9 jit_solution(258232065281974729)
XLA Ops:
  0.0 3.9 %second_halves.2 = bf16[2,512,2048]{2,1,0:T(8,128)(2,1)} custom-call(bf16[2,512,8192]{2,1,0:T(8,128)(2,1)} %bitcast.20), custom_call_target="tpu_custom_call" | custom-call | tf_op jit(solution)/shard_map/second_halves/pallas_call | solution.py:59
  5.9 3.8 %second_halves.3 = bf16[2,512,2048]{2,1,0:T(8,128)(2,1)} custom-call(bf16[2,512,8192]{2,1,0:T(8,128)(2,1)} %bitcast.21), custom_call_target="tpu_custom_call" | custom-call | tf_op jit(solution)/shard_map/second_halves/pallas_call | solution.py:59
  10.1 14.2 %all_to_all.70.refs_2_ = bf16[16,32,256]{2,1,0:T(8,128)(2,1)S(1)} all-to-all(bf16[16,32,256]{2,1,0:T(8,128)(2,1)S(1)} %broadcast_in_dim.21), channel_id=1, replica_groups=mesh['sweep'=8,'layer'=16] {'layer'}, dimensions={0} | all-to-all | bytes 524288 | tf_op jit(solution)/shard_map/all_to_all | solution.py:217
  24.3 4.1 %load_product.2 = (f32[32,256]{1,0:T(8,128)S(1)}, f32[32,256]{1,0:T(8,128)S(1)}, bf16[4,512,4096]{2,1,0:T(8,128)(2,1)S(1)}) custom-call(s32[1]{0:T(128)} %bitcast.me_ref, bf16[2,512,8192]{2,1,0:T(8,128)(2,1)} %bitcast.22, bf16[2,512,2048]{2,1,0:T(8,128)(2,1)} %collective-permute-done.2.refs_0_, bf16[2,512,2048]{2,1,0:T(8,128)(2,1)} %collective-permute-done.3.refs_1_, ...), custom_call_target="tpu_custom_call" | custom-call | flops 536870912 | bytes 8388608 | tf_op jit(solution)/shard_map/load_product/pallas_call | solution.py:120
  28.4 2.0 collective-permute-start.4
  31.3 3.5 %collective-permute-start.5 = (bf16[32,256]{1,0:T(8,128)(2,1)S(1)}, bf16[32,256]{1,0:T(8,128)(2,1)S(1)}, u32[]{:S(2)}, u32[]{:S(2)}) collective-permute-start(bf16[32,256]{1,0:T(8,128)(2,1)S(1)} %add_convert_fusion.10), channel_id=1, source_target_pairs={{0,32},{16,48},{1,33},{17,49},{2,34},{18,50},{3,35},{19,51},{4,36}... | collective-permute-start | bytes 49160 | tf_op jit(solution)/shard_map/ppermute | solution.py:214
  35.7 10.5 %all_to_all.71.refs_2_ = bf16[16,32,256]{2,1,0:T(8,128)(2,1)S(1)} all-to-all(bf16[16,32,256]{2,1,0:T(8,128)(2,1)S(1)} %broadcast_in_dim.22), channel_id=1, replica_groups=mesh['sweep'=8,'layer'=16] {'layer'}, dimensions={0} | all-to-all | bytes 524288 | tf_op jit(solution)/shard_map/all_to_all | solution.py:217
  46.1 4.1 %load_product.3 = (f32[32,256]{1,0:T(8,128)S(1)}, f32[32,256]{1,0:T(8,128)S(1)}, bf16[4,512,4096]{2,1,0:T(8,128)(2,1)S(1)}) custom-call(s32[1]{0:T(128)} %bitcast.me_ref, bf16[2,512,8192]{2,1,0:T(8,128)(2,1)} %bitcast.23, bf16[2,512,2048]{2,1,0:T(8,128)(2,1)} %collective-permute-done.2.refs_0_, bf16[2,512,2048]{2,1,0:T(8,128)(2,1)} %collective-permute-done.3.refs_1_, ...), custom_call_target="tpu_custom_call" | custom-call | flops 536870912 | bytes 8388608 | tf_op jit(solution)/shard_map/load_product/pallas_call | solution.py:120
  50.2 2.8 %collective-permute-start.6 = (f32[32,256]{1,0:T(8,128)S(1)}, f32[32,256]{1,0:T(8,128)S(1)}, u32[]{:S(2)}, u32[]{:S(2)}) collective-permute-start(f32[32,256]{1,0:T(8,128)S(1)} %get-tuple-element.71), channel_id=1, source_target_pairs={{0,16},{16,0},{32,48},{48,32},{64,80},{80,64},{96,112},{112,96},{1... | collective-permute-start | bytes 98312 | tf_op jit(solution)/shard_map/ppermute | solution.py:210
  53.8 10.7 %all_to_all.72.x_ref = bf16[16,32,256]{2,1,0:T(8,128)(2,1)S(1)} all-to-all(bf16[16,32,256]{2,1,0:T(8,128)(2,1)S(1)} %broadcast_in_dim.23), channel_id=1, replica_groups=mesh['sweep'=8,'layer'=16] {'layer'}, dimensions={0} | all-to-all | bytes 524288 | tf_op jit(solution)/shard_map/all_to_all | solution.py:217
  64.6 2.5 down_product.1
  70.7 10.7 %all_to_all.73.x_ref = bf16[16,32,256]{2,1,0:T(8,128)(2,1)S(1)} all-to-all(bf16[16,32,256]{2,1,0:T(8,128)(2,1)S(1)} %broadcast_in_dim.24), channel_id=1, replica_groups=mesh['sweep'=8,'layer'=16] {'layer'}, dimensions={0} | all-to-all | bytes 524288 | tf_op jit(solution)/shard_map/all_to_all | solution.py:217
  85.8 10.7 %all_to_all.74.x_ref = bf16[16,32,256]{2,1,0:T(8,128)(2,1)S(1)} all-to-all(bf16[16,32,256]{2,1,0:T(8,128)(2,1)S(1)} %broadcast_in_dim.25), channel_id=1, replica_groups=mesh['sweep'=8,'layer'=16] {'layer'}, dimensions={0} | all-to-all | bytes 524288 | tf_op jit(solution)/shard_map/all_to_all | solution.py:217
  101.7 10.7 %all_to_all.75.x_ref = bf16[16,32,256]{2,1,0:T(8,128)(2,1)S(1)} all-to-all(bf16[16,32,256]{2,1,0:T(8,128)(2,1)S(1)} %broadcast_in_dim.26), channel_id=1, replica_groups=mesh['sweep'=8,'layer'=16] {'layer'}, dimensions={0} | all-to-all | bytes 524288 | tf_op jit(solution)/shard_map/all_to_all | solution.py:217
  116.8 10.7 %all_to_all.76.x_ref = bf16[16,32,256]{2,1,0:T(8,128)(2,1)S(1)} all-to-all(bf16[16,32,256]{2,1,0:T(8,128)(2,1)S(1)} %broadcast_in_dim.27), channel_id=1, replica_groups=mesh['sweep'=8,'layer'=16] {'layer'}, dimensions={0} | all-to-all | bytes 524288 | tf_op jit(solution)/shard_map/all_to_all | solution.py:217
  134.5 10.9 %all_to_all.77 = bf16[16,32,256]{2,1,0:T(8,128)(2,1)S(1)} all-to-all(bf16[16,32,256]{2,1,0:T(8,128)(2,1)S(1)} %up_product.7), channel_id=1, replica_groups=mesh['sweep'=8,'layer'=16] {'layer'}, dimensions={0} | all-to-all | bytes 524288 | tf_op jit(solution)/shard_map/all_to_all | solution.py:217
  150.3 10.7 %all_to_all.78 = bf16[16,32,256]{2,1,0:T(8,128)(2,1)S(1)} all-to-all(bf16[16,32,256]{2,1,0:T(8,128)(2,1)S(1)} %up_product.8), channel_id=1, replica_groups=mesh['sweep'=8,'layer'=16] {'layer'}, dimensions={0} | all-to-all | bytes 524288 | tf_op jit(solution)/shard_map/all_to_all | solution.py:217
  165.5 10.7 %all_to_all.79 = bf16[16,32,256]{2,1,0:T(8,128)(2,1)S(1)} all-to-all(bf16[16,32,256]{2,1,0:T(8,128)(2,1)S(1)} %up_product.9), channel_id=1, replica_groups=mesh['sweep'=8,'layer'=16] {'layer'}, dimensions={0} | all-to-all | bytes 524288 | tf_op jit(solution)/shard_map/all_to_all | solution.py:217
  181.3 10.7 %all_to_all.80 = bf16[16,32,256]{2,1,0:T(8,128)(2,1)S(1)} all-to-all(bf16[16,32,256]{2,1,0:T(8,128)(2,1)S(1)} %up_product.10), channel_id=1, replica_groups=mesh['sweep'=8,'layer'=16] {'layer'}, dimensions={0} | all-to-all | bytes 524288 | tf_op jit(solution)/shard_map/all_to_all | solution.py:217
  196.4 10.7 %all_to_all.81 = bf16[16,32,256]{2,1,0:T(8,128)(2,1)S(1)} all-to-all(bf16[16,32,256]{2,1,0:T(8,128)(2,1)S(1)} %up_product.11), channel_id=1, replica_groups=mesh['sweep'=8,'layer'=16] {'layer'}, dimensions={0} | all-to-all | bytes 524288 | tf_op jit(solution)/shard_map/all_to_all | solution.py:217
  211.3 16.0 %collective-permute-done.24.x_ref = bf16[32,512]{1,0:T(8,128)(2,1)S(1)} collective-permute-done((bf16[32,512]{1,0:T(8,128)(2,1)S(1)}, bf16[32,512]{1,0:T(8,128)(2,1)S(1)}, u32[]{:S(2)}, u32[]{:S(2)}) %collective-permute-start.24) | collective-permute-done | bytes 32800 | tf_op jit(solution)/shard_map/ppermute | solution.py:214
  228.9 10.5 %all_to_all.82 = bf16[16,32,256]{2,1,0:T(8,128)(2,1)S(1)} all-to-all(bf16[16,32,256]{2,1,0:T(8,128)(2,1)S(1)} %up_product.12), channel_id=1, replica_groups=mesh['sweep'=8,'layer'=16] {'layer'}, dimensions={0} | all-to-all | bytes 524288 | tf_op jit(solution)/shard_map/all_to_all | solution.py:217
  239.4 2.8 %collective-permute-start.25 = (bf16[32,256]{1,0:T(8,128)(2,1)S(1)}, bf16[32,256]{1,0:T(8,128)(2,1)S(1)}, u32[]{:S(2)}, u32[]{:S(2)}) collective-permute-start(bf16[32,256]{1,0:T(8,128)(2,1)S(1)} %add_convert_fusion), channel_id=1, source_target_pairs={{0,16},{16,0},{32,48},{48,32},{64,80},{80,64},{96,112},{112,96},{1... | collective-permute-start | bytes 49160 | tf_op jit(solution)/shard_map/ppermute | solution.py:210
  244.6 10.7 %all_to_all.83 = bf16[16,32,256]{2,1,0:T(8,128)(2,1)S(1)} all-to-all(bf16[16,32,256]{2,1,0:T(8,128)(2,1)S(1)} %up_product.13), channel_id=1, replica_groups=mesh['sweep'=8,'layer'=16] {'layer'}, dimensions={0} | all-to-all | bytes 524288 | tf_op jit(solution)/shard_map/all_to_all | solution.py:217
  (119 shorter events, 59.5 us)
Async XLA Ops:
  3.9 5.9 %collective-permute-start.1 = (f32[32,512]{1,0:T(8,128)S(1)}, f32[32,512]{1,0:T(8,128)S(1)}, u32[]{:S(2)}, u32[]{:S(2)}) collective-permute-start(f32[32,512]{1,0:T(8,128)S(1)} %bitcast.24), channel_id=1, source_target_pairs={{0,16},{16,0},{32,48},{48,32},{64,80},{80,64},{96,112},{112,96},{1... | collective-permute-start | bytes 196616 | tf_op jit(solution)/shard_map/ppermute | solution.py:210
  5.4 4.4 %collective-permute-start = (f32[32,256]{1,0:T(8,128)S(1)}, f32[32,256]{1,0:T(8,128)S(1)}, u32[]{:S(2)}, u32[]{:S(2)}) collective-permute-start(f32[32,256]{1,0:T(8,128)S(1)} %slice.41), channel_id=1, source_target_pairs={{0,16},{16,0},{32,48},{48,32},{64,80},{80,64},{96,112},{112,96},{1... | collective-permute-start | bytes 98312 | tf_op jit(solution)/shard_map/ppermute | solution.py:210
  5.5 18.8 %collective-permute-start.2 = (bf16[2,512,2048]{2,1,0:T(8,128)(2,1)}, bf16[2,512,2048]{2,1,0:T(8,128)(2,1)}, u32[]{:S(2)}, u32[]{:S(2)}) collective-permute-start(bf16[2,512,2048]{2,1,0:T(8,128)(2,1)} %second_halves.2), channel_id=1, source_target_pairs={{0,16},{16,0},{32,48},{48,32},{64,80},{80,64},{96,112},{112,96},{1... | collective-permute-start | bytes 12582920 | tf_op jit(solution)/shard_map/ppermute | solution.py:210
  9.8 14.5 %collective-permute-start.3 = (bf16[2,512,2048]{2,1,0:T(8,128)(2,1)}, bf16[2,512,2048]{2,1,0:T(8,128)(2,1)}, u32[]{:S(2)}, u32[]{:S(2)}) collective-permute-start(bf16[2,512,2048]{2,1,0:T(8,128)(2,1)} %second_halves.3), channel_id=1, source_target_pairs={{0,16},{16,0},{32,48},{48,32},{64,80},{80,64},{96,112},{112,96},{1... | collective-permute-start | bytes 12582920 | tf_op jit(solution)/shard_map/ppermute | solution.py:210
  28.4 2.9 %collective-permute-start.4 = (f32[32,256]{1,0:T(8,128)S(1)}, f32[32,256]{1,0:T(8,128)S(1)}, u32[]{:S(2)}, u32[]{:S(2)}) collective-permute-start(f32[32,256]{1,0:T(8,128)S(1)} %get-tuple-element.68), channel_id=1, source_target_pairs={{0,16},{16,0},{32,48},{48,32},{64,80},{80,64},{96,112},{112,96},{1... | collective-permute-start | bytes 98312 | tf_op jit(solution)/shard_map/ppermute | solution.py:210
  31.3 4.4 %collective-permute-start.5 = (bf16[32,256]{1,0:T(8,128)(2,1)S(1)}, bf16[32,256]{1,0:T(8,128)(2,1)S(1)}, u32[]{:S(2)}, u32[]{:S(2)}) collective-permute-start(bf16[32,256]{1,0:T(8,128)(2,1)S(1)} %add_convert_fusion.10), channel_id=1, source_target_pairs={{0,32},{16,48},{1,33},{17,49},{2,34},{18,50},{3,35},{19,51},{4,36}... | collective-permute-start | bytes 49160 | tf_op jit(solution)/shard_map/ppermute | solution.py:214
  50.2 3.6 %collective-permute-start.6 = (f32[32,256]{1,0:T(8,128)S(1)}, f32[32,256]{1,0:T(8,128)S(1)}, u32[]{:S(2)}, u32[]{:S(2)}) collective-permute-start(f32[32,256]{1,0:T(8,128)S(1)} %get-tuple-element.71), channel_id=1, source_target_pairs={{0,16},{16,0},{32,48},{48,32},{64,80},{80,64},{96,112},{112,96},{1... | collective-permute-start | bytes 98312 | tf_op jit(solution)/shard_map/ppermute | solution.py:210
  67.1 2.8 %collective-permute-start.7 = (f32[32,256]{1,0:T(8,128)S(1)}, f32[32,256]{1,0:T(8,128)S(1)}, u32[]{:S(2)}, u32[]{:S(2)}) collective-permute-start(f32[32,256]{1,0:T(8,128)S(1)} %get-tuple-element.74), channel_id=1, source_target_pairs={{0,16},{16,0},{32,48},{48,32},{64,80},{80,64},{96,112},{112,96},{1... | collective-permute-start | bytes 98312 | tf_op jit(solution)/shard_map/ppermute | solution.py:210
  82.9 2.8 %collective-permute-start.9 = (f32[32,256]{1,0:T(8,128)S(1)}, f32[32,256]{1,0:T(8,128)S(1)}, u32[]{:S(2)}, u32[]{:S(2)}) collective-permute-start(f32[32,256]{1,0:T(8,128)S(1)} %get-tuple-element.77), channel_id=1, source_target_pairs={{0,16},{16,0},{32,48},{48,32},{64,80},{80,64},{96,112},{112,96},{1... | collective-permute-start | bytes 98312 | tf_op jit(solution)/shard_map/ppermute | solution.py:210
  98.1 2.8 %collective-permute-start.10 = (f32[32,256]{1,0:T(8,128)S(1)}, f32[32,256]{1,0:T(8,128)S(1)}, u32[]{:S(2)}, u32[]{:S(2)}) collective-permute-start(f32[32,256]{1,0:T(8,128)S(1)} %get-tuple-element.79), channel_id=1, source_target_pairs={{0,16},{16,0},{32,48},{48,32},{64,80},{80,64},{96,112},{112,96},{1... | collective-permute-start | bytes 98312 | tf_op jit(solution)/shard_map/ppermute | solution.py:210
  100.9 0.7 collective-permute-start.11
  113.9 2.8 %collective-permute-start.12 = (f32[32,256]{1,0:T(8,128)S(1)}, f32[32,256]{1,0:T(8,128)S(1)}, u32[]{:S(2)}, u32[]{:S(2)}) collective-permute-start(f32[32,256]{1,0:T(8,128)S(1)} %get-tuple-element.81), channel_id=1, source_target_pairs={{0,16},{16,0},{32,48},{48,32},{64,80},{80,64},{96,112},{112,96},{1... | collective-permute-start | bytes 98312 | tf_op jit(solution)/shard_map/ppermute | solution.py:210
  129.1 2.8 %collective-permute-start.14 = (f32[32,256]{1,0:T(8,128)S(1)}, f32[32,256]{1,0:T(8,128)S(1)}, u32[]{:S(2)}, u32[]{:S(2)}) collective-permute-start(f32[32,256]{1,0:T(8,128)S(1)} %get-tuple-element.87), channel_id=1, source_target_pairs={{0,16},{16,0},{32,48},{48,32},{64,80},{80,64},{96,112},{112,96},{1... | collective-permute-start | bytes 98312 | tf_op jit(solution)/shard_map/ppermute | solution.py:210
  131.1 1.2 collective-permute-start.13
  132.3 2.2 collective-permute-start.15
  132.5 2.0 collective-permute-start.16
  145.5 2.6 %collective-permute-start.17 = (bf16[32,256]{1,0:T(8,128)(2,1)S(1)}, bf16[32,256]{1,0:T(8,128)(2,1)S(1)}, u32[]{:S(2)}, u32[]{:S(2)}) collective-permute-start(bf16[32,256]{1,0:T(8,128)(2,1)S(1)} %get-tuple-element.104), channel_id=1, source_target_pairs={{0,16},{16,0},{32,48},{48,32},{64,80},{80,64},{96,112},{112,96},{1... | collective-permute-start | bytes 49160 | tf_op jit(solution)/shard_map/ppermute | solution.py:210
  161.1 2.8 %collective-permute-start.19 = (bf16[32,256]{1,0:T(8,128)(2,1)S(1)}, bf16[32,256]{1,0:T(8,128)(2,1)S(1)}, u32[]{:S(2)}, u32[]{:S(2)}) collective-permute-start(bf16[32,256]{1,0:T(8,128)(2,1)S(1)} %add_convert_fusion.4), channel_id=1, source_target_pairs={{0,16},{16,0},{32,48},{48,32},{64,80},{80,64},{96,112},{112,96},{1... | collective-permute-start | bytes 49160 | tf_op jit(solution)/shard_map/ppermute | solution.py:210
  176.3 2.8 %collective-permute-start.20 = (bf16[32,256]{1,0:T(8,128)(2,1)S(1)}, bf16[32,256]{1,0:T(8,128)(2,1)S(1)}, u32[]{:S(2)}, u32[]{:S(2)}) collective-permute-start(bf16[32,256]{1,0:T(8,128)(2,1)S(1)} %add_convert_fusion.3), channel_id=1, source_target_pairs={{0,16},{16,0},{32,48},{48,32},{64,80},{80,64},{96,112},{112,96},{1... | collective-permute-start | bytes 49160 | tf_op jit(solution)/shard_map/ppermute | solution.py:210
  192.1 2.8 %collective-permute-start.22 = (bf16[32,256]{1,0:T(8,128)(2,1)S(1)}, bf16[32,256]{1,0:T(8,128)(2,1)S(1)}, u32[]{:S(2)}, u32[]{:S(2)}) collective-permute-start(bf16[32,256]{1,0:T(8,128)(2,1)S(1)} %add_convert_fusion.2), channel_id=1, source_target_pairs={{0,16},{16,0},{32,48},{48,32},{64,80},{80,64},{96,112},{112,96},{1... | collective-permute-start | bytes 49160 | tf_op jit(solution)/shard_map/ppermute | solution.py:210
  207.2 2.8 %collective-permute-start.23 = (bf16[32,256]{1,0:T(8,128)(2,1)S(1)}, bf16[32,256]{1,0:T(8,128)(2,1)S(1)}, u32[]{:S(2)}, u32[]{:S(2)}) collective-permute-start(bf16[32,256]{1,0:T(8,128)(2,1)S(1)} %add_convert_fusion.1), channel_id=1, source_target_pairs={{0,16},{16,0},{32,48},{48,32},{64,80},{80,64},{96,112},{112,96},{1... | collective-permute-start | bytes 49160 | tf_op jit(solution)/shard_map/ppermute | solution.py:210
  210.0 17.3 %collective-permute-start.24 = (bf16[32,512]{1,0:T(8,128)(2,1)S(1)}, bf16[32,512]{1,0:T(8,128)(2,1)S(1)}, u32[]{:S(2)}, u32[]{:S(2)}) collective-permute-start(bf16[32,512]{1,0:T(8,128)(2,1)S(1)} %pad_maximum_fusion.6), channel_id=1, source_target_pairs={{32,0},{48,16},{33,1},{49,17},{34,2},{50,18},{35,3},{51,19},{36,4}... | collective-permute-start | bytes 98312 | tf_op jit(solution)/shard_map/ppermute | solution.py:214
  239.4 3.6 %collective-permute-start.25 = (bf16[32,256]{1,0:T(8,128)(2,1)S(1)}, bf16[32,256]{1,0:T(8,128)(2,1)S(1)}, u32[]{:S(2)}, u32[]{:S(2)}) collective-permute-start(bf16[32,256]{1,0:T(8,128)(2,1)S(1)} %add_convert_fusion), channel_id=1, source_target_pairs={{0,16},{16,0},{32,48},{48,32},{64,80},{80,64},{96,112},{112,96},{1... | collective-permute-start | bytes 49160 | tf_op jit(solution)/shard_map/ppermute | solution.py:210
  255.4 2.8 %collective-permute-start.26 = (f32[32,256]{1,0:T(8,128)S(1)}, f32[32,256]{1,0:T(8,128)S(1)}, u32[]{:S(2)}, u32[]{:S(2)}) collective-permute-start(f32[32,256]{1,0:T(8,128)S(1)} %select_n.137), channel_id=1, source_target_pairs={{0,16},{16,0},{32,48},{48,32},{64,80},{80,64},{96,112},{112,96},{1... | collective-permute-start | bytes 98312 | tf_op jit(solution)/shard_map/ppermute | solution.py:210
  (5 other events, 11.3 us)

commit v8 on v7

v8 whole, which is shorter than its diff:
```python
import jax
import jax.numpy as jnp
from jax import lax
from jax.experimental import pallas as pl
from jax.experimental.pallas import tpu as pltpu
from jax.sharding import PartitionSpec as P

F32, BF16 = jnp.float32, jnp.bfloat16
MIB = 1 << 20
VMEM = pl.BlockSpec(memory_space=pltpu.VMEM)
HBM = pl.BlockSpec(memory_space=pltpu.HBM)
SMEM = pl.BlockSpec(memory_space=pltpu.SMEM)


def down_sums(x, g, sums):
    contract = (((1,), (1,)), ((), ()))
    r = lax.dot_general(x, g[0], contract, preferred_element_type=F32)
    m = lax.dot_general(x, g[1], contract, preferred_element_type=F32)
    return (r, m) if sums is None else (sums[0] + r, sums[1] + m)


def complex_of(sums, n):
    with_real, with_imag = sums
    return with_real[:n] - with_imag[n:], with_imag[:n] + with_real[n:]


def write_down(sums, base_ref, mine_ref, theirs_ref):
    n, wide = base_ref.shape[0] // 2, base_ref.shape[1]
    real, imag = complex_of(sums, n)
    mine_ref[...] = jnp.concatenate([real[:, :wide], imag[:, :wide]], axis=0) + base_ref[...]
    theirs_ref[...] = jnp.concatenate([real[:, wide:], imag[:, wide:]], axis=0)


def second_halves(matrix, first, count, chips):
    parts, rows, cols = matrix.shape
    wide = cols // (2 * chips)

    def body(matrix_ref, out_ref, held, in_sems, out_sems):
        taken, put = [], []
        for i in range(count):
            at = (2 * (first + i) + 1) * wide
            taken.append(
                pltpu.make_async_copy(matrix_ref.at[:, :, pl.ds(at, wide)], held.at[i], in_sems.at[i])
            )
            put.append(
                pltpu.make_async_copy(held.at[i], out_ref.at[:, :, pl.ds(i * wide, wide)], out_sems.at[i])
            )
        for copy in taken:
            copy.start()
        for i in range(count):
            taken[i].wait()
            put[i].start()
        for copy in put:
            copy.wait()

    return pl.pallas_call(
        body,
        in_specs=[HBM],
        out_specs=HBM,
        out_shape=pltpu.HBM((parts, rows, count * wide), BF16),
        scratch_shapes=[
            pltpu.VMEM((count, parts, rows, wide), BF16),
            pltpu.SemaphoreType.DMA((count,)),
            pltpu.SemaphoreType.DMA((count,)),
        ],
        compiler_params=pltpu.CompilerParams(vmem_limit_bytes=56 * MIB),
        name="second_halves",
    )(matrix)


def load_product(me, on_core, late, matrix, received, blocks, base):
    chips, rhs, wide = blocks.shape
    parts, rows, cols = matrix.shape
    pieces = len(received)

    def body(me_ref, matrix_ref, *refs):
        received_refs = refs[:pieces]
        x_ref, base_ref, mine_ref, theirs_ref, out_ref, sems = refs[pieces:]
        index, per = me_ref[0], chips // pieces

        def copy(source_ref, row, at, i, slot):
            return pltpu.make_async_copy(
                source_ref.at[:, pl.ds(row, wide), pl.ds(at, wide)],
                out_ref.at[pl.ds(0, parts), pl.ds(slot * wide, wide), pl.ds(i * wide, wide)],
                sems.at[slot, i],
            )

        @pl.when(index % 2 == on_core)
        def _():
            for i in range(chips):
                copy(matrix_ref, wide, 2 * i * wide, i, 0).start()
                copy(matrix_ref, 0, 2 * i * wide, i, 1).start()

        @pl.when(index % 2 != on_core)
        def _():
            for i in range(chips):
                copy(received_refs[i // per], 0, i % per * wide, i, 0).start()
                copy(received_refs[i // per], wide, i % per * wide, i, 1).start()

        def wait(i):
            for slot in range(2):
                copy(matrix_ref, 0, 0, i, slot).wait()

        @pl.when(index < late)
        def _():
            sums = None
            for i in range(chips):
                wait(i)
                sums = down_sums(x_ref[i], out_ref.at[:, :, pl.ds(i * wide, wide)], sums)
            write_down(sums, base_ref, mine_ref, theirs_ref)

        @pl.when(index >= late)
        def _():
            for i in range(chips):
                wait(i)
                at = slice(i * wide, (i + 1) * wide)
                for part in range(parts):
                    turned = out_ref[part, :, at].T
                    out_ref[parts + part, :wide, at] = turned[:, :wide]
                    out_ref[parts + part, wide:, at] = turned[:, wide:]
            mine_ref[...] = base_ref[...]
            theirs_ref[...] = base_ref[...]

    part = jax.ShapeDtypeStruct((rhs, wide), F32)
    return pl.pallas_call(
        body,
        in_specs=[SMEM, HBM, *[HBM] * pieces, VMEM, VMEM],
        out_specs=[VMEM] * 3,
        out_shape=[part, part, pltpu.VMEM((2 * parts, rows, cols // 2), BF16)],
        scratch_shapes=[pltpu.SemaphoreType.DMA((2, chips))],
        compiler_params=pltpu.CompilerParams(vmem_limit_bytes=(16 if on_core == 0 else 32) * MIB),
        cost_estimate=pl.CostEstimate(
            flops=4 * rhs * rows * cols, bytes_accessed=parts * rows * cols, transcendentals=0
        ),
        name="load_product",
    )(me, matrix, *received, blocks, base)


def vmem_call(body, out_shape, name, flops):
    def call(*args):
        return pl.pallas_call(
            body,
            in_specs=[VMEM] * len(args),
            out_specs=jax.tree.map(lambda _: VMEM, out_shape),
            out_shape=out_shape,
            compiler_params=pltpu.CompilerParams(vmem_limit_bytes=8 * MIB),
            cost_estimate=pl.CostEstimate(flops=flops, bytes_accessed=1 << 16, transcendentals=0),
            name=name,
        )(*args)

    return call


def down_body(x_ref, g_ref, base_ref, mine_ref, theirs_ref):
    chips, rhs, wide = x_ref.shape
    sums = None
    for i in range(chips):
        sums = down_sums(x_ref[i], g_ref.at[:, :, pl.ds(i * wide, wide)], sums)
    write_down(sums, base_ref, mine_ref, theirs_ref)


def turned_sums(x_ref, g_ref, slot):
    chips, rhs, wide = x_ref.shape
    sums = None
    for i in range(chips):
        terms = [
            jnp.dot(
                x_ref[i],
                g_ref[part, slot * wide : (slot + 1) * wide, i * wide : (i + 1) * wide],
                preferred_element_type=F32,
            )
            for part in (2, 3)
        ]
        sums = terms if sums is None else [total + more for total, more in zip(sums, terms)]
    return jnp.concatenate(complex_of(sums, rhs // 2), axis=0)


def turned_theirs_body(x_ref, g_ref, theirs_ref):
    theirs_ref[...] = turned_sums(x_ref, g_ref, 1)


def turned_mine_body(x_ref, g_ref, base_ref, mine_ref):
    mine_ref[...] = turned_sums(x_ref, g_ref, 0) + base_ref[...]


def up_term(x_ref, g_ref, slot, i):
    rhs, wide = x_ref.shape
    rows, at = slice(slot * wide, (slot + 1) * wide), slice(i * wide, (i + 1) * wide)
    terms = [jnp.dot(x_ref[...], g_ref[part, rows, at], preferred_element_type=F32) for part in range(2)]
    return jnp.concatenate(complex_of(terms, rhs // 2), axis=0)


def up_own_body(x_ref, g_ref, out_ref):
    for i in range(out_ref.shape[0]):
        out_ref[i] = up_term(x_ref, g_ref, 0, i)


def up_rest_body(x_ref, g_ref, own_ref, out_ref):
    for i in range(out_ref.shape[0]):
        out_ref[i] = (up_term(x_ref, g_ref, 1, i) + own_ref[i]).astype(BF16)


def make_masks(me, count, shape):
    def body(me_ref, out_ref):
        index = me_ref[0]
        for p in range(count):
            out_ref[p] = jnp.full(shape, jnp.where(index // 2 == p, 1, 0), jnp.int32)
        out_ref[count] = jnp.full(shape, jnp.where(index % 2 == 0, 1, 0), jnp.int32)

    return pl.pallas_call(
        body,
        in_specs=[SMEM],
        out_specs=VMEM,
        out_shape=pltpu.VMEM((count + 1, *shape), jnp.int32),
        name="make_masks",
    )(me)


def local(green, down_source, up_source):
    planes = lax.axis_size("sweep") // 2
    chips = lax.axis_size("layer")
    matrix = green[0]
    rows, cols = matrix.shape[1:]
    wide = rows // 2
    rhs = 2 * down_source.shape[2]

    def swap(x):
        return lax.ppermute(x, "sweep", [(i, i ^ 1) for i in range(2 * planes)])

    def hop(x, a, b):
        return lax.ppermute(x, "sweep", [(2 * a + c, 2 * b + c) for c in range(2)])

    def hop_across(x, a, b):
        return lax.ppermute(x, "sweep", [(2 * a + c, 2 * b + 1 - c) for c in range(2)])

    def exchange(blocks):
        return lax.all_to_all(blocks, "layer", 0, 0, tiled=True)

    def spread(x):
        return exchange(jnp.broadcast_to(x.astype(BF16), (chips, *x.shape)))

    tie = lambda *values: lax.optimization_barrier(values)
    me = lax.axis_index("sweep").astype(jnp.int32).reshape(1)
    masks = make_masks(me, planes, (rhs, wide))
    masks = [masks[p] == 1 for p in range(planes + 1)]
    on_0 = masks.pop()

    flops = 4 * rhs * rows * cols
    part = jax.ShapeDtypeStruct((rhs, wide), F32)
    down_call = vmem_call(down_body, (part, part), "down_product", flops)
    theirs_call = vmem_call(turned_theirs_body, part, "turned_theirs", flops // 2)
    mine_call = vmem_call(turned_mine_body, part, "turned_mine", flops // 2)
    own_call = vmem_call(up_own_body, jax.ShapeDtypeStruct((chips, rhs, wide), F32), "up_own", flops // 2)
    rest_call = vmem_call(up_rest_body, jax.ShapeDtypeStruct((chips, rhs, wide), BF16), "up_rest", flops // 2)

    def turned_call(blocks, mat, base):
        theirs = theirs_call(blocks, mat)
        return mine_call(blocks, mat, base), theirs

    def up_product(own, other, mat, base, *beside):
        blocks = rest_call(other.astype(BF16), mat, own_call(own.astype(BF16), mat))
        if beside:
            blocks, base, *beside = tie(blocks, base, *beside)
        x = base + jnp.sum(exchange(blocks).astype(F32), axis=0)
        return (x, base, *beside) if beside else x

    down_own, up_own = down_source.reshape(rhs, rows), up_source.reshape(rhs, rows)
    half = chips // 2
    sent_0, matrix, down_own, up_own = tie(second_halves(matrix, 0, half, chips), matrix, down_own, up_own)
    down_got, up_other, received_0 = swap(down_own[:, :wide]), swap(up_own), swap(sent_0)
    sent_1, down_got, up_other = tie(second_halves(matrix, half, chips - half, chips), down_got, up_other)
    received = (received_0, swap(sent_1))
    up_a = jnp.where(on_0, up_own[:, :wide], up_other[:, wide:])
    up_b = jnp.where(on_0, up_other[:, wide:], up_own[:, :wide])
    up_b_rest = jnp.where(on_0, up_other[:, :wide], up_own[:, wide:])
    base_a = jnp.where(on_0, down_own[:, wide:], down_got)
    base_b = jnp.where(on_0, down_got, down_own[:, wide:])
    down_a, mine_b, theirs_b = base_a, base_b, base_b

    x, base_b, up_a, up_b, up_b_rest, me, on_0, masks = tie(
        base_a, base_b, up_a, up_b, up_b_rest, me, on_0, masks
    )
    late = 4
    for p in range(planes):
        if p > 0:
            blocks = spread(hop(mine, p - 1, p) + hop_across(theirs, p - 1, p))
            if p == 1:
                mine, theirs, matrix_a = load_product(
                    me, 0, late, matrix, received, blocks, base_a
                )
            else:
                mine, theirs = turned_call(blocks, matrix_a, base_a)
            x = mine + swap(theirs)
            down_a = jnp.where(masks[p], x, down_a)
        blocks = spread(x)
        if p == 0:
            mine, theirs, matrix_b = load_product(me, 1, late, matrix, received, blocks, base_b)
        elif p == 1:
            mine, theirs = down_call(blocks, matrix_b, base_b)
        else:
            mine, theirs = turned_call(blocks, matrix_b, base_b)
        mine_b = jnp.where(masks[p], mine, mine_b)
        theirs_b = jnp.where(masks[p], theirs, theirs_b)

    mine_b, theirs_b, down_a = tie(mine_b, theirs_b, down_a)
    rest = up_b_rest + (mine_b + swap(theirs_b))
    base_b = up_b + (theirs_b + swap(mine_b))
    base_b, rest, down_a = tie(base_b, rest, down_a)
    base_a = up_a + swap(down_a)
    for p in reversed(range(planes)):
        if p == planes - 1:
            x, base_a, total_b = up_product(base_b, rest, matrix_a, base_a, base_b)
            total_a = x
        else:
            x = x.astype(BF16)
            x = up_product(hop(x, p + 1, p), hop_across(x, p + 1, p), matrix_b, base_b)
            total_b = jnp.where(masks[p], x, total_b)
            x = x.astype(BF16)
            x = up_product(x, swap(x), matrix_a, base_a)
            total_a = jnp.where(masks[p], x, total_a)

    got = swap(jnp.where(on_0, total_b, total_a))
    out = jnp.concatenate([jnp.where(on_0, total_a, total_b), got], axis=1)
    return out.reshape(1, 2, rhs // 2, rows)


def solution(mesh):
    in_specs = (
        P("sweep", None, "layer", None),
        P("sweep", None, None, "layer"),
        P("sweep", None, None, "layer"),
    )
    out_specs = P("sweep", None, None, "layer")
    return jax.shard_map(local, mesh=mesh, in_specs=in_specs, out_specs=out_specs, check_vma=False)
```

time: 260 us -> 254 us (0.977)
  waiting for transfers between devices: 29.1 us -> 23.2 us
    ppermute x21 -> x14, waiting for transfers between devices: 12.2 us -> 3.04 us  [swap(): return lax.ppermute(x, 'sweep', [(i, i ^ 1) for i in range(2 * planes)])]
    ppermute x21 -> x14, starting transfers between devices: 31.8 us -> 22.9 us  [swap(): return lax.ppermute(x, 'sweep', [(i, i ^ 1) for i in range(2 * planes)])]
    ppermute x6 -> x12, starting transfers between devices: 7.45 us -> 14.6 us  [the longest x6 7.52 us: hop(): return lax.ppermute(x, 'sweep', [(2 * a + c, 2 * b + c) for c in range(2)])]
    ppermute x6 -> x12, waiting for transfers between devices: 16.9 us -> 20.1 us  [the longest x6 16.5 us: hop(): return lax.ppermute(x, 'sweep', [(2 * a + c, 2 * b + c) for c in range(2)])]
    pallas_call x12 -> x23, Pallas kernels: 19.3 us -> 20.5 us  [call(): pl.pallas_call(body, in_specs=[VMEM] * len(args), out_specs=jax.tree.map(...]
  transfers between devices with their start and end apart: 27 -> 26, of which waited for: 17 -> 10; matrix products, arithmetic and copies ran while one was open for 0% -> 0% of each run, Pallas kernels for 2% -> 5%
where the time goes in v8:
time: 254 us
  blocking collectives  154 us (61%)
  starting transfers between devices  37.4 us (15%)
  Pallas kernels  36.7 us (14%)
  waiting for transfers between devices  23.2 us (9%)
    all_to_all x14, blocking collectives, exchange(): return lax.all_to_all(blocks, 'layer', 0, 0, tiled=True)  154 us
    ppermute x14, starting transfers between devices, swap(): return lax.ppermute(x, 'sweep', [(i, i ^ 1) for i in range(2 * planes)])  22.9 us
    pallas_call x23, Pallas kernels, call(): pl.pallas_call(body, in_specs=[VMEM] * len(args), out_specs=jax.tree.map(...  20.5 us
    ppermute x6, waiting for transfers between devices, hop(): return lax.ppermute(x, 'sweep', [(2 * a + c, 2 * b + c) for c in range(2)])  16.5 us
    pallas_call x2, Pallas kernels, load_product(): pl.pallas_call(body, in_specs=[SMEM, HBM, *[HBM] * pieces, VMEM, VMEM], o...  8.42 us
    pallas_call x2, Pallas kernels, second_halves(): pl.pallas_call(body, in_specs=[HBM], out_specs=HBM, out_shape=pltpu.HBM((...  7.75 us
    ppermute x6, starting transfers between devices, hop(): return lax.ppermute(x, 'sweep', [(2 * a + c, 2 * b + c) for c in range(2)])  7.52 us
    ppermute x6, starting transfers between devices, hop_across(): lax.ppermute(x, 'sweep', [(2 * a + c, 2 * b + 1 - c) for c in range(2)])  7.06 us
  transfers between devices with their start and end apart: 26, of which 10 were waited for; matrix products, arithmetic and copies ran while one was open for 0% of the time, Pallas kernels for 5%

profile of v8, /device:TPU:1, one launch (start us, length us, event | category | flops | bytes accessed | tf_op | source)
XLA Modules:
  0.0 253.5 jit_solution(10959809719117420844)
XLA Ops:
  0.0 3.9 %second_halves.2 = bf16[2,512,2048]{2,1,0:T(8,128)(2,1)} custom-call(bf16[2,512,8192]{2,1,0:T(8,128)(2,1)} %bitcast.16), custom_call_target="tpu_custom_call" | custom-call | tf_op jit(solution)/shard_map/second_halves/pallas_call | solution.py:56
  5.9 3.8 %second_halves.3 = bf16[2,512,2048]{2,1,0:T(8,128)(2,1)} custom-call(bf16[2,512,8192]{2,1,0:T(8,128)(2,1)} %bitcast.17), custom_call_target="tpu_custom_call" | custom-call | tf_op jit(solution)/shard_map/second_halves/pallas_call | solution.py:56
  10.1 14.2 %all_to_all.70.refs_2_ = bf16[16,32,256]{2,1,0:T(8,128)(2,1)S(1)} all-to-all(bf16[16,32,256]{2,1,0:T(8,128)(2,1)S(1)} %broadcast_in_dim.21), channel_id=1, replica_groups=mesh['sweep'=8,'layer'=16] {'layer'}, dimensions={0} | all-to-all | bytes 524288 | tf_op jit(solution)/shard_map/all_to_all | solution.py:237
  24.3 4.2 %load_product.2 = (f32[32,256]{1,0:T(8,128)S(1)}, f32[32,256]{1,0:T(8,128)S(1)}, bf16[4,512,4096]{2,1,0:T(8,128)(2,1)S(1)}) custom-call(s32[1]{0:T(128)} %bitcast.me_ref, bf16[2,512,8192]{2,1,0:T(8,128)(2,1)} %bitcast.18, bf16[2,512,2048]{2,1,0:T(8,128)(2,1)} %collective-permute-done.2.refs_0_, bf16[2,512,2048]{2,1,0:T(8,128)(2,1)} %collective-permute-done.3.refs_1_, ...), custom_call_target="tpu_custom_call" | custom-call | flops 536870912 | bytes 8388608 | tf_op jit(solution)/shard_map/load_product/pallas_call | solution.py:125
  28.5 3.5 %collective-permute-start.4 = (f32[32,256]{1,0:T(8,128)S(1)}, f32[32,256]{1,0:T(8,128)S(1)}, u32[]{:S(2)}, u32[]{:S(2)}) collective-permute-start(f32[32,256]{1,0:T(8,128)S(1)} %get-tuple-element.54), channel_id=1, source_target_pairs={{0,32},{16,48},{1,33},{17,49},{2,34},{18,50},{3,35},{19,51},{4,36}... | collective-permute-start | bytes 98312 | tf_op jit(solution)/shard_map/ppermute | solution.py:231
  32.1 3.1 %collective-permute-start.5 = (f32[32,256]{1,0:T(8,128)S(1)}, f32[32,256]{1,0:T(8,128)S(1)}, u32[]{:S(2)}, u32[]{:S(2)}) collective-permute-start(f32[32,256]{1,0:T(8,128)S(1)} %get-tuple-element.55), channel_id=1, source_target_pairs={{0,48},{16,32},{1,49},{17,33},{2,50},{18,34},{3,51},{19,35},{4,52}... | collective-permute-start | bytes 98312 | tf_op jit(solution)/shard_map/ppermute | solution.py:234
  36.2 10.6 %all_to_all.71.refs_2_ = bf16[16,32,256]{2,1,0:T(8,128)(2,1)S(1)} all-to-all(bf16[16,32,256]{2,1,0:T(8,128)(2,1)S(1)} %broadcast_in_dim.22), channel_id=1, replica_groups=mesh['sweep'=8,'layer'=16] {'layer'}, dimensions={0} | all-to-all | bytes 524288 | tf_op jit(solution)/shard_map/all_to_all | solution.py:237
  46.8 4.2 %load_product.3 = (f32[32,256]{1,0:T(8,128)S(1)}, f32[32,256]{1,0:T(8,128)S(1)}, bf16[4,512,4096]{2,1,0:T(8,128)(2,1)S(1)}) custom-call(s32[1]{0:T(128)} %bitcast.me_ref, bf16[2,512,8192]{2,1,0:T(8,128)(2,1)} %bitcast.19, bf16[2,512,2048]{2,1,0:T(8,128)(2,1)} %collective-permute-done.2.refs_0_, bf16[2,512,2048]{2,1,0:T(8,128)(2,1)} %collective-permute-done.3.refs_1_, ...), custom_call_target="tpu_custom_call" | custom-call | flops 536870912 | bytes 8388608 | tf_op jit(solution)/shard_map/load_product/pallas_call | solution.py:125
  54.3 10.7 %all_to_all.72.x_ref = bf16[16,32,256]{2,1,0:T(8,128)(2,1)S(1)} all-to-all(bf16[16,32,256]{2,1,0:T(8,128)(2,1)S(1)} %broadcast_in_dim.23), channel_id=1, replica_groups=mesh['sweep'=8,'layer'=16] {'layer'}, dimensions={0} | all-to-all | bytes 524288 | tf_op jit(solution)/shard_map/all_to_all | solution.py:237
  69.0 10.9 %all_to_all.73.x_ref = bf16[16,32,256]{2,1,0:T(8,128)(2,1)S(1)} all-to-all(bf16[16,32,256]{2,1,0:T(8,128)(2,1)S(1)} %broadcast_in_dim.24), channel_id=1, replica_groups=mesh['sweep'=8,'layer'=16] {'layer'}, dimensions={0} | all-to-all | bytes 524288 | tf_op jit(solution)/shard_map/all_to_all | solution.py:237
  80.7 3.0 %collective-permute-start.9 = (f32[32,256]{1,0:T(8,128)S(1)}, f32[32,256]{1,0:T(8,128)S(1)}, u32[]{:S(2)}, u32[]{:S(2)}) collective-permute-start(f32[32,256]{1,0:T(8,128)S(1)} %turned_theirs.4), channel_id=1, source_target_pairs={{0,16},{16,0},{32,48},{48,32},{64,80},{80,64},{96,112},{112,96},{1... | collective-permute-start | bytes 98312 | tf_op jit(solution)/shard_map/ppermute | solution.py:228
  84.6 10.8 %all_to_all.74.x_ref = bf16[16,32,256]{2,1,0:T(8,128)(2,1)S(1)} all-to-all(bf16[16,32,256]{2,1,0:T(8,128)(2,1)S(1)} %broadcast_in_dim.25), channel_id=1, replica_groups=mesh['sweep'=8,'layer'=16] {'layer'}, dimensions={0} | all-to-all | bytes 524288 | tf_op jit(solution)/shard_map/all_to_all | solution.py:237
  98.4 10.9 %all_to_all.75.x_ref = bf16[16,32,256]{2,1,0:T(8,128)(2,1)S(1)} all-to-all(bf16[16,32,256]{2,1,0:T(8,128)(2,1)S(1)} %broadcast_in_dim.26), channel_id=1, replica_groups=mesh['sweep'=8,'layer'=16] {'layer'}, dimensions={0} | all-to-all | bytes 524288 | tf_op jit(solution)/shard_map/all_to_all | solution.py:237
  114.0 10.8 %all_to_all.76.x_ref = bf16[16,32,256]{2,1,0:T(8,128)(2,1)S(1)} all-to-all(bf16[16,32,256]{2,1,0:T(8,128)(2,1)S(1)} %broadcast_in_dim.27), channel_id=1, replica_groups=mesh['sweep'=8,'layer'=16] {'layer'}, dimensions={0} | all-to-all | bytes 524288 | tf_op jit(solution)/shard_map/all_to_all | solution.py:237
  131.6 10.7 %all_to_all.77 = bf16[16,32,256]{2,1,0:T(8,128)(2,1)S(1)} all-to-all(bf16[16,32,256]{2,1,0:T(8,128)(2,1)S(1)} %up_rest.7), channel_id=1, replica_groups=mesh['sweep'=8,'layer'=16] {'layer'}, dimensions={0} | all-to-all | bytes 524288 | tf_op jit(solution)/shard_map/all_to_all | solution.py:237
  145.4 10.9 %all_to_all.78 = bf16[16,32,256]{2,1,0:T(8,128)(2,1)S(1)} all-to-all(bf16[16,32,256]{2,1,0:T(8,128)(2,1)S(1)} %up_rest.8), channel_id=1, replica_groups=mesh['sweep'=8,'layer'=16] {'layer'}, dimensions={0} | all-to-all | bytes 524288 | tf_op jit(solution)/shard_map/all_to_all | solution.py:237
  156.3 3.2 %collective-permute-start.18 = (bf16[32,256]{1,0:T(8,128)(2,1)S(1)}, bf16[32,256]{1,0:T(8,128)(2,1)S(1)}, u32[]{:S(2)}, u32[]{:S(2)}) collective-permute-start(bf16[32,256]{1,0:T(8,128)(2,1)S(1)} %add_convert_fusion.7.x_ref), channel_id=1, source_target_pairs={{0,16},{16,0},{32,48},{48,32},{64,80},{80,64},{96,112},{112,96},{1... | collective-permute-start | bytes 49160 | tf_op jit(solution)/shard_map/ppermute | solution.py:228
  161.2 10.8 %all_to_all.79 = bf16[16,32,256]{2,1,0:T(8,128)(2,1)S(1)} all-to-all(bf16[16,32,256]{2,1,0:T(8,128)(2,1)S(1)} %up_rest.9), channel_id=1, replica_groups=mesh['sweep'=8,'layer'=16] {'layer'}, dimensions={0} | all-to-all | bytes 524288 | tf_op jit(solution)/shard_map/all_to_all | solution.py:237
  175.1 10.9 %all_to_all.80 = bf16[16,32,256]{2,1,0:T(8,128)(2,1)S(1)} all-to-all(bf16[16,32,256]{2,1,0:T(8,128)(2,1)S(1)} %up_rest.10), channel_id=1, replica_groups=mesh['sweep'=8,'layer'=16] {'layer'}, dimensions={0} | all-to-all | bytes 524288 | tf_op jit(solution)/shard_map/all_to_all | solution.py:237
  186.0 3.0 %collective-permute-start.21 = (bf16[32,256]{1,0:T(8,128)(2,1)S(1)}, bf16[32,256]{1,0:T(8,128)(2,1)S(1)}, u32[]{:S(2)}, u32[]{:S(2)}) collective-permute-start(bf16[32,256]{1,0:T(8,128)(2,1)S(1)} %add_convert_fusion.5.x_ref), channel_id=1, source_target_pairs={{0,16},{16,0},{32,48},{48,32},{64,80},{80,64},{96,112},{112,96},{1... | collective-permute-start | bytes 49160 | tf_op jit(solution)/shard_map/ppermute | solution.py:228
  190.7 10.8 %all_to_all.81 = bf16[16,32,256]{2,1,0:T(8,128)(2,1)S(1)} all-to-all(bf16[16,32,256]{2,1,0:T(8,128)(2,1)S(1)} %up_rest.11), channel_id=1, replica_groups=mesh['sweep'=8,'layer'=16] {'layer'}, dimensions={0} | all-to-all | bytes 524288 | tf_op jit(solution)/shard_map/all_to_all | solution.py:237
  204.1 16.5 %collective-permute-done.23.x_ref = bf16[32,256]{1,0:T(8,128)(2,1)S(1)} collective-permute-done((bf16[32,256]{1,0:T(8,128)(2,1)S(1)}, bf16[32,256]{1,0:T(8,128)(2,1)S(1)}, u32[]{:S(2)}, u32[]{:S(2)}) %collective-permute-start.23) | collective-permute-done | bytes 16416 | tf_op jit(solution)/shard_map/ppermute | solution.py:231
  224.8 10.9 %all_to_all.82 = bf16[16,32,256]{2,1,0:T(8,128)(2,1)S(1)} all-to-all(bf16[16,32,256]{2,1,0:T(8,128)(2,1)S(1)} %up_rest.12), channel_id=1, replica_groups=mesh['sweep'=8,'layer'=16] {'layer'}, dimensions={0} | all-to-all | bytes 524288 | tf_op jit(solution)/shard_map/all_to_all | solution.py:237
  239.2 10.7 %all_to_all.83 = bf16[16,32,256]{2,1,0:T(8,128)(2,1)S(1)} all-to-all(bf16[16,32,256]{2,1,0:T(8,128)(2,1)S(1)} %up_rest.13), channel_id=1, replica_groups=mesh['sweep'=8,'layer'=16] {'layer'}, dimensions={0} | all-to-all | bytes 524288 | tf_op jit(solution)/shard_map/all_to_all | solution.py:237
  (113 shorter events, 50.1 us)
Async XLA Ops:
  3.9 5.9 %collective-permute-start.1 = (f32[32,512]{1,0:T(8,128)S(1)}, f32[32,512]{1,0:T(8,128)S(1)}, u32[]{:S(2)}, u32[]{:S(2)}) collective-permute-start(f32[32,512]{1,0:T(8,128)S(1)} %bitcast.20), channel_id=1, source_target_pairs={{0,16},{16,0},{32,48},{48,32},{64,80},{80,64},{96,112},{112,96},{1... | collective-permute-start | bytes 196616 | tf_op jit(solution)/shard_map/ppermute | solution.py:228
  5.4 4.4 %collective-permute-start = (f32[32,256]{1,0:T(8,128)S(1)}, f32[32,256]{1,0:T(8,128)S(1)}, u32[]{:S(2)}, u32[]{:S(2)}) collective-permute-start(f32[32,256]{1,0:T(8,128)S(1)} %slice.38), channel_id=1, source_target_pairs={{0,16},{16,0},{32,48},{48,32},{64,80},{80,64},{96,112},{112,96},{1... | collective-permute-start | bytes 98312 | tf_op jit(solution)/shard_map/ppermute | solution.py:228
  5.5 18.8 %collective-permute-start.2 = (bf16[2,512,2048]{2,1,0:T(8,128)(2,1)}, bf16[2,512,2048]{2,1,0:T(8,128)(2,1)}, u32[]{:S(2)}, u32[]{:S(2)}) collective-permute-start(bf16[2,512,2048]{2,1,0:T(8,128)(2,1)} %second_halves.2), channel_id=1, source_target_pairs={{0,16},{16,0},{32,48},{48,32},{64,80},{80,64},{96,112},{112,96},{1... | collective-permute-start | bytes 12582920 | tf_op jit(solution)/shard_map/ppermute | solution.py:228
  9.8 14.5 %collective-permute-start.3 = (bf16[2,512,2048]{2,1,0:T(8,128)(2,1)}, bf16[2,512,2048]{2,1,0:T(8,128)(2,1)}, u32[]{:S(2)}, u32[]{:S(2)}) collective-permute-start(bf16[2,512,2048]{2,1,0:T(8,128)(2,1)} %second_halves.3), channel_id=1, source_target_pairs={{0,16},{16,0},{32,48},{48,32},{64,80},{80,64},{96,112},{112,96},{1... | collective-permute-start | bytes 12582920 | tf_op jit(solution)/shard_map/ppermute | solution.py:228
  28.5 6.7 %collective-permute-start.4 = (f32[32,256]{1,0:T(8,128)S(1)}, f32[32,256]{1,0:T(8,128)S(1)}, u32[]{:S(2)}, u32[]{:S(2)}) collective-permute-start(f32[32,256]{1,0:T(8,128)S(1)} %get-tuple-element.54), channel_id=1, source_target_pairs={{0,32},{16,48},{1,33},{17,49},{2,34},{18,50},{3,35},{19,51},{4,36}... | collective-permute-start | bytes 98312 | tf_op jit(solution)/shard_map/ppermute | solution.py:231
  32.1 4.1 %collective-permute-start.5 = (f32[32,256]{1,0:T(8,128)S(1)}, f32[32,256]{1,0:T(8,128)S(1)}, u32[]{:S(2)}, u32[]{:S(2)}) collective-permute-start(f32[32,256]{1,0:T(8,128)S(1)} %get-tuple-element.55), channel_id=1, source_target_pairs={{0,48},{16,32},{1,49},{17,33},{2,50},{18,34},{3,51},{19,35},{4,52}... | collective-permute-start | bytes 98312 | tf_op jit(solution)/shard_map/ppermute | solution.py:234
  51.1 3.2 %collective-permute-start.6 = (f32[32,256]{1,0:T(8,128)S(1)}, f32[32,256]{1,0:T(8,128)S(1)}, u32[]{:S(2)}, u32[]{:S(2)}) collective-permute-start(f32[32,256]{1,0:T(8,128)S(1)} %get-tuple-element.57), channel_id=1, source_target_pairs={{0,16},{16,0},{32,48},{48,32},{64,80},{80,64},{96,112},{112,96},{1... | collective-permute-start | bytes 98312 | tf_op jit(solution)/shard_map/ppermute | solution.py:228
  67.6 1.4 collective-permute-start.7
  80.7 3.9 %collective-permute-start.9 = (f32[32,256]{1,0:T(8,128)S(1)}, f32[32,256]{1,0:T(8,128)S(1)}, u32[]{:S(2)}, u32[]{:S(2)}) collective-permute-start(f32[32,256]{1,0:T(8,128)S(1)} %turned_theirs.4), channel_id=1, source_target_pairs={{0,16},{16,0},{32,48},{48,32},{64,80},{80,64},{96,112},{112,96},{1... | collective-permute-start | bytes 98312 | tf_op jit(solution)/shard_map/ppermute | solution.py:228
  96.2 2.2 collective-permute-start.10
  110.1 3.9 %collective-permute-start.12 = (f32[32,256]{1,0:T(8,128)S(1)}, f32[32,256]{1,0:T(8,128)S(1)}, u32[]{:S(2)}, u32[]{:S(2)}) collective-permute-start(f32[32,256]{1,0:T(8,128)S(1)} %turned_theirs.6), channel_id=1, source_target_pairs={{0,16},{16,0},{32,48},{48,32},{64,80},{80,64},{96,112},{112,96},{1... | collective-permute-start | bytes 98312 | tf_op jit(solution)/shard_map/ppermute | solution.py:228
  126.5 2.8 %collective-permute-start.14 = (f32[32,256]{1,0:T(8,128)S(1)}, f32[32,256]{1,0:T(8,128)S(1)}, u32[]{:S(2)}, u32[]{:S(2)}) collective-permute-start(f32[32,256]{1,0:T(8,128)S(1)} %get-tuple-element.64), channel_id=1, source_target_pairs={{0,16},{16,0},{32,48},{48,32},{64,80},{80,64},{96,112},{112,96},{1... | collective-permute-start | bytes 98312 | tf_op jit(solution)/shard_map/ppermute | solution.py:228
  128.4 1.2 collective-permute-start.13
  129.7 1.9 collective-permute-start.15
  142.4 1.3 collective-permute-start.17
  143.1 1.5 collective-permute-start.16
  156.3 4.1 %collective-permute-start.18 = (bf16[32,256]{1,0:T(8,128)(2,1)S(1)}, bf16[32,256]{1,0:T(8,128)(2,1)S(1)}, u32[]{:S(2)}, u32[]{:S(2)}) collective-permute-start(bf16[32,256]{1,0:T(8,128)(2,1)S(1)} %add_convert_fusion.7.x_ref), channel_id=1, source_target_pairs={{0,16},{16,0},{32,48},{48,32},{64,80},{80,64},{96,112},{112,96},{1... | collective-permute-start | bytes 49160 | tf_op jit(solution)/shard_map/ppermute | solution.py:228
  172.1 1.3 collective-permute-start.20
  172.7 1.5 collective-permute-start.19
  186.0 3.8 %collective-permute-start.21 = (bf16[32,256]{1,0:T(8,128)(2,1)S(1)}, bf16[32,256]{1,0:T(8,128)(2,1)S(1)}, u32[]{:S(2)}, u32[]{:S(2)}) collective-permute-start(bf16[32,256]{1,0:T(8,128)(2,1)S(1)} %add_convert_fusion.5.x_ref), channel_id=1, source_target_pairs={{0,16},{16,0},{32,48},{48,32},{64,80},{80,64},{96,112},{112,96},{1... | collective-permute-start | bytes 49160 | tf_op jit(solution)/shard_map/ppermute | solution.py:228
  201.5 19.1 %collective-permute-start.23 = (bf16[32,256]{1,0:T(8,128)(2,1)S(1)}, bf16[32,256]{1,0:T(8,128)(2,1)S(1)}, u32[]{:S(2)}, u32[]{:S(2)}) collective-permute-start(bf16[32,256]{1,0:T(8,128)(2,1)S(1)} %add_convert_fusion.4), channel_id=1, source_target_pairs={{32,0},{48,16},{33,1},{49,17},{34,2},{50,18},{35,3},{51,19},{36,4}... | collective-permute-start | bytes 49160 | tf_op jit(solution)/shard_map/ppermute | solution.py:231
  202.8 21.2 %collective-permute-start.22 = (bf16[32,256]{1,0:T(8,128)(2,1)S(1)}, bf16[32,256]{1,0:T(8,128)(2,1)S(1)}, u32[]{:S(2)}, u32[]{:S(2)}) collective-permute-start(bf16[32,256]{1,0:T(8,128)(2,1)S(1)} %add_convert_fusion.4), channel_id=1, source_target_pairs={{32,16},{48,0},{33,17},{49,1},{34,18},{50,2},{35,19},{51,3},{36,20... | collective-permute-start | bytes 49160 | tf_op jit(solution)/shard_map/ppermute | solution.py:234
  235.7 2.7 %collective-permute-start.24 = (bf16[32,256]{1,0:T(8,128)(2,1)S(1)}, bf16[32,256]{1,0:T(8,128)(2,1)S(1)}, u32[]{:S(2)}, u32[]{:S(2)}) collective-permute-start(bf16[32,256]{1,0:T(8,128)(2,1)S(1)} %add_convert_fusion.3.x_ref), channel_id=1, source_target_pairs={{0,16},{16,0},{32,48},{48,32},{64,80},{80,64},{96,112},{112,96},{1... | collective-permute-start | bytes 49160 | tf_op jit(solution)/shard_map/ppermute | solution.py:228
  250.1 2.8 %collective-permute-start.25 = (f32[32,256]{1,0:T(8,128)S(1)}, f32[32,256]{1,0:T(8,128)S(1)}, u32[]{:S(2)}, u32[]{:S(2)}) collective-permute-start(f32[32,256]{1,0:T(8,128)S(1)} %select_n.96), channel_id=1, source_target_pairs={{0,16},{16,0},{32,48},{48,32},{64,80},{80,64},{96,112},{112,96},{1... | collective-permute-start | bytes 98312 | tf_op jit(solution)/shard_map/ppermute | solution.py:228
  (4 other events, 10.7 us)

commit v9 on v8

--- a/solution.py
+++ b/solution.py
@@ -151,12 +151,21 @@
     return call
 
 
-def down_body(x_ref, g_ref, base_ref, mine_ref, theirs_ref):
+def rows_sums(x_ref, g_ref, slot):
     chips, rhs, wide = x_ref.shape
     sums = None
     for i in range(chips):
-        sums = down_sums(x_ref[i], g_ref.at[:, :, pl.ds(i * wide, wide)], sums)
-    write_down(sums, base_ref, mine_ref, theirs_ref)
+        part_ref = g_ref.at[:, pl.ds(slot * wide, wide), pl.ds(i * wide, wide)]
+        sums = down_sums(x_ref[i], part_ref, sums)
+    return jnp.concatenate(complex_of(sums, rhs // 2), axis=0)
+
+
+def rows_theirs_body(x_ref, g_ref, theirs_ref):
+    theirs_ref[...] = rows_sums(x_ref, g_ref, 1)
+
+
+def rows_mine_body(x_ref, g_ref, base_ref, mine_ref):
+    mine_ref[...] = rows_sums(x_ref, g_ref, 0) + base_ref[...]
 
 
 def turned_sums(x_ref, g_ref, slot):
@@ -247,7 +256,8 @@
 
     flops = 4 * rhs * rows * cols
     part = jax.ShapeDtypeStruct((rhs, wide), F32)
-    down_call = vmem_call(down_body, (part, part), "down_product", flops)
+    rows_theirs = vmem_call(rows_theirs_body, part, "rows_theirs", flops // 2)
+    rows_mine = vmem_call(rows_mine_body, part, "rows_mine", flops // 2)
     theirs_call = vmem_call(turned_theirs_body, part, "turned_theirs", flops // 2)
     mine_call = vmem_call(turned_mine_body, part, "turned_mine", flops // 2)
     own_call = vmem_call(up_own_body, jax.ShapeDtypeStruct((chips, rhs, wide), F32), "up_own", flops // 2)
@@ -296,7 +306,7 @@
         if p == 0:
             mine, theirs, matrix_b = load_product(me, 1, late, matrix, received, blocks, base_b)
         elif p == 1:
-            mine, theirs = down_call(blocks, matrix_b, base_b)
+            theirs, mine = rows_theirs(blocks, matrix_b), rows_mine(blocks, matrix_b, base_b)
         else:
             mine, theirs = turned_call(blocks, matrix_b, base_b)
         mine_b = jnp.where(masks[p], mine, mine_b)

time: 254 us -> 277 us (1.091)
  local copies, waits for them, and re-layouts: 0.15 us -> 23.2 us
    unnamed x4 -> x14, local copies, waits for them, and re-layouts: 0.01 us -> 23.1 us
    pallas_call x23 -> x24, Pallas kernels: 20.5 us -> 20.7 us  [call(): pl.pallas_call(body, in_specs=[VMEM] * len(args), out_specs=jax.tree.map(...]
  transfers between devices with their start and end apart: 26 -> 26, of which waited for: 10 -> 7; matrix products, arithmetic and copies ran while one was open for 0% -> 0% of each run, Pallas kernels for 5% -> 5%
where the time goes in v9:
time: 277 us; the launch traced here: 276 us
  blocking collectives  155 us (56%)
  starting transfers between devices  37 us (13%)
  Pallas kernels  36.9 us (13%)
  local copies, waits for them, and re-layouts  23.2 us (8%)
  waiting for transfers between devices  22.2 us (8%)
    all_to_all x14, blocking collectives, exchange(): return lax.all_to_all(blocks, 'layer', 0, 0, tiled=True)  155 us
    unnamed x14, local copies, waits for them, and re-layouts  23.1 us
    ppermute x14, starting transfers between devices, swap(): return lax.ppermute(x, 'sweep', [(i, i ^ 1) for i in range(2 * planes)])  22.4 us
    pallas_call x24, Pallas kernels, call(): pl.pallas_call(body, in_specs=[VMEM] * len(args), out_specs=jax.tree.map(...  20.7 us
    ppermute x6, waiting for transfers between devices, hop(): return lax.ppermute(x, 'sweep', [(2 * a + c, 2 * b + c) for c in range(2)])  16 us
    pallas_call x2, Pallas kernels, load_product(): pl.pallas_call(body, in_specs=[SMEM, HBM, *[HBM] * pieces, VMEM, VMEM], o...  8.4 us
    pallas_call x2, Pallas kernels, second_halves(): pl.pallas_call(body, in_specs=[HBM], out_specs=HBM, out_shape=pltpu.HBM((...  7.74 us
    ppermute x6, starting transfers between devices, hop(): return lax.ppermute(x, 'sweep', [(2 * a + c, 2 * b + c) for c in range(2)])  7.49 us
  transfers between devices with their start and end apart: 26, of which 7 were waited for; matrix products, arithmetic and copies ran while one was open for 0% of the time, Pallas kernels for 5%

profile of v9, /device:TPU:1, one launch (start us, length us, event | category | flops | bytes accessed | tf_op | source)
XLA Modules:
  0.0 276.3 jit_solution(2015308326838924779)
XLA Ops:
  0.0 3.9 %second_halves.2 = bf16[2,512,2048]{2,1,0:T(8,128)(2,1)} custom-call(bf16[2,512,8192]{2,1,0:T(8,128)(2,1)} %bitcast.16), custom_call_target="tpu_custom_call" | custom-call | tf_op jit(solution)/shard_map/second_halves/pallas_call | solution.py:56
  5.9 3.8 %second_halves.3 = bf16[2,512,2048]{2,1,0:T(8,128)(2,1)} custom-call(bf16[2,512,8192]{2,1,0:T(8,128)(2,1)} %bitcast.17), custom_call_target="tpu_custom_call" | custom-call | tf_op jit(solution)/shard_map/second_halves/pallas_call | solution.py:56
  10.1 14.2 %all_to_all.70.refs_2_ = bf16[16,32,256]{2,1,0:T(8,128)(2,1)S(1)} all-to-all(bf16[16,32,256]{2,1,0:T(8,128)(2,1)S(1)} %broadcast_in_dim.21), channel_id=1, replica_groups=mesh['sweep'=8,'layer'=16] {'layer'}, dimensions={0} | all-to-all | bytes 524288 | tf_op jit(solution)/shard_map/all_to_all | solution.py:246
  24.3 4.2 %load_product.2 = (f32[32,256]{1,0:T(8,128)S(1)}, f32[32,256]{1,0:T(8,128)S(1)}, bf16[4,512,4096]{2,1,0:T(8,128)(2,1)S(1)}) custom-call(s32[1]{0:T(128)} %bitcast.me_ref, bf16[2,512,8192]{2,1,0:T(8,128)(2,1)} %bitcast.18, bf16[2,512,2048]{2,1,0:T(8,128)(2,1)} %collective-permute-done.2.refs_0_, bf16[2,512,2048]{2,1,0:T(8,128)(2,1)} %collective-permute-done.3.refs_1_, ...), custom_call_target="tpu_custom_call" | custom-call | flops 536870912 | bytes 8388608 | tf_op jit(solution)/shard_map/load_product/pallas_call | solution.py:125
  28.5 3.5 %collective-permute-start.4 = (f32[32,256]{1,0:T(8,128)S(1)}, f32[32,256]{1,0:T(8,128)S(1)}, u32[]{:S(2)}, u32[]{:S(2)}) collective-permute-start(f32[32,256]{1,0:T(8,128)S(1)} %get-tuple-element.52), channel_id=1, source_target_pairs={{0,32},{16,48},{1,33},{17,49},{2,34},{18,50},{3,35},{19,51},{4,36}... | collective-permute-start | bytes 98312 | tf_op jit(solution)/shard_map/ppermute | solution.py:240
  36.2 10.6 %all_to_all.71.refs_2_ = bf16[16,32,256]{2,1,0:T(8,128)(2,1)S(1)} all-to-all(bf16[16,32,256]{2,1,0:T(8,128)(2,1)S(1)} %broadcast_in_dim.22), channel_id=1, replica_groups=mesh['sweep'=8,'layer'=16] {'layer'}, dimensions={0} | all-to-all | bytes 524288 | tf_op jit(solution)/shard_map/all_to_all | solution.py:246
  46.8 4.2 %load_product.3 = (f32[32,256]{1,0:T(8,128)S(1)}, f32[32,256]{1,0:T(8,128)S(1)}, bf16[4,512,4096]{2,1,0:T(8,128)(2,1)S(1)}) custom-call(s32[1]{0:T(128)} %bitcast.me_ref, bf16[2,512,8192]{2,1,0:T(8,128)(2,1)} %bitcast.19, bf16[2,512,2048]{2,1,0:T(8,128)(2,1)} %collective-permute-done.2.refs_0_, bf16[2,512,2048]{2,1,0:T(8,128)(2,1)} %collective-permute-done.3.refs_1_, ...), custom_call_target="tpu_custom_call" | custom-call | flops 536870912 | bytes 8388608 | tf_op jit(solution)/shard_map/load_product/pallas_call | solution.py:125
  54.3 10.7 %all_to_all.72.x_ref = bf16[16,32,256]{2,1,0:T(8,128)(2,1)S(1)} all-to-all(bf16[16,32,256]{2,1,0:T(8,128)(2,1)S(1)} %broadcast_in_dim.23), channel_id=1, replica_groups=mesh['sweep'=8,'layer'=16] {'layer'}, dimensions={0} | all-to-all | bytes 524288 | tf_op jit(solution)/shard_map/all_to_all | solution.py:246
  69.1 10.9 %all_to_all.73.x_ref = bf16[16,32,256]{2,1,0:T(8,128)(2,1)S(1)} all-to-all(bf16[16,32,256]{2,1,0:T(8,128)(2,1)S(1)} %broadcast_in_dim.24), channel_id=1, replica_groups=mesh['sweep'=8,'layer'=16] {'layer'}, dimensions={0} | all-to-all | bytes 524288 | tf_op jit(solution)/shard_map/all_to_all | solution.py:246
  84.7 10.8 %all_to_all.74.x_ref = bf16[16,32,256]{2,1,0:T(8,128)(2,1)S(1)} all-to-all(bf16[16,32,256]{2,1,0:T(8,128)(2,1)S(1)} %broadcast_in_dim.25), channel_id=1, replica_groups=mesh['sweep'=8,'layer'=16] {'layer'}, dimensions={0} | all-to-all | bytes 524288 | tf_op jit(solution)/shard_map/all_to_all | solution.py:246
  98.6 10.9 %all_to_all.75.x_ref = bf16[16,32,256]{2,1,0:T(8,128)(2,1)S(1)} all-to-all(bf16[16,32,256]{2,1,0:T(8,128)(2,1)S(1)} %broadcast_in_dim.26), channel_id=1, replica_groups=mesh['sweep'=8,'layer'=16] {'layer'}, dimensions={0} | all-to-all | bytes 524288 | tf_op jit(solution)/shard_map/all_to_all | solution.py:246
  114.2 10.8 %all_to_all.76.x_ref = bf16[16,32,256]{2,1,0:T(8,128)(2,1)S(1)} all-to-all(bf16[16,32,256]{2,1,0:T(8,128)(2,1)S(1)} %broadcast_in_dim.27), channel_id=1, replica_groups=mesh['sweep'=8,'layer'=16] {'layer'}, dimensions={0} | all-to-all | bytes 524288 | tf_op jit(solution)/shard_map/all_to_all | solution.py:246
  130.1 5.8 %copy-done.1 = bf16[4,512,4096]{2,1,0:T(8,128)(2,1)S(1)} copy-done((bf16[4,512,4096]{2,1,0:T(8,128)(2,1)S(1)}, bf16[4,512,4096]{2,1,0:T(8,128)(2,1)}, u32[]{:S(2)}) %copy-start.1) | copy-done | bytes 16777240
  137.5 10.7 %all_to_all.77 = bf16[16,32,256]{2,1,0:T(8,128)(2,1)S(1)} all-to-all(bf16[16,32,256]{2,1,0:T(8,128)(2,1)S(1)} %up_rest.7), channel_id=1, replica_groups=mesh['sweep'=8,'layer'=16] {'layer'}, dimensions={0} | all-to-all | bytes 524288 | tf_op jit(solution)/shard_map/all_to_all | solution.py:246
  151.4 10.9 %all_to_all.78 = bf16[16,32,256]{2,1,0:T(8,128)(2,1)S(1)} all-to-all(bf16[16,32,256]{2,1,0:T(8,128)(2,1)S(1)} %up_rest.8), channel_id=1, replica_groups=mesh['sweep'=8,'layer'=16] {'layer'}, dimensions={0} | all-to-all | bytes 524288 | tf_op jit(solution)/shard_map/all_to_all | solution.py:246
  165.5 5.8 %copy-done.2 = bf16[4,512,4096]{2,1,0:T(8,128)(2,1)S(1)} copy-done((bf16[4,512,4096]{2,1,0:T(8,128)(2,1)S(1)}, bf16[4,512,4096]{2,1,0:T(8,128)(2,1)}, u32[]{:S(2)}) %copy-start.2) | copy-done | bytes 16777240
  172.9 11.0 %all_to_all.79 = bf16[16,32,256]{2,1,0:T(8,128)(2,1)S(1)} all-to-all(bf16[16,32,256]{2,1,0:T(8,128)(2,1)S(1)} %up_rest.9), channel_id=1, replica_groups=mesh['sweep'=8,'layer'=16] {'layer'}, dimensions={0} | all-to-all | bytes 524288 | tf_op jit(solution)/shard_map/all_to_all | solution.py:246
  187.1 11.1 %all_to_all.80 = bf16[16,32,256]{2,1,0:T(8,128)(2,1)S(1)} all-to-all(bf16[16,32,256]{2,1,0:T(8,128)(2,1)S(1)} %up_rest.10), channel_id=1, replica_groups=mesh['sweep'=8,'layer'=16] {'layer'}, dimensions={0} | all-to-all | bytes 524288 | tf_op jit(solution)/shard_map/all_to_all | solution.py:246
  200.8 5.8 %copy-done.3 = bf16[4,512,4096]{2,1,0:T(8,128)(2,1)S(1)} copy-done((bf16[4,512,4096]{2,1,0:T(8,128)(2,1)S(1)}, bf16[4,512,4096]{2,1,0:T(8,128)(2,1)}, u32[]{:S(2)}) %copy-start.3) | copy-done | bytes 16777240
  208.2 11.0 %all_to_all.81 = bf16[16,32,256]{2,1,0:T(8,128)(2,1)S(1)} all-to-all(bf16[16,32,256]{2,1,0:T(8,128)(2,1)S(1)} %up_rest.11), channel_id=1, replica_groups=mesh['sweep'=8,'layer'=16] {'layer'}, dimensions={0} | all-to-all | bytes 524288 | tf_op jit(solution)/shard_map/all_to_all | solution.py:246
  221.8 16.0 %collective-permute-done.23.x_ref = bf16[32,256]{1,0:T(8,128)(2,1)S(1)} collective-permute-done((bf16[32,256]{1,0:T(8,128)(2,1)S(1)}, bf16[32,256]{1,0:T(8,128)(2,1)S(1)}, u32[]{:S(2)}, u32[]{:S(2)}) %collective-permute-start.23) | collective-permute-done | bytes 16416 | tf_op jit(solution)/shard_map/ppermute | solution.py:240
  241.8 10.7 %all_to_all.82 = bf16[16,32,256]{2,1,0:T(8,128)(2,1)S(1)} all-to-all(bf16[16,32,256]{2,1,0:T(8,128)(2,1)S(1)} %up_rest.12), channel_id=1, replica_groups=mesh['sweep'=8,'layer'=16] {'layer'}, dimensions={0} | all-to-all | bytes 524288 | tf_op jit(solution)/shard_map/all_to_all | solution.py:246
  254.6 5.8 %copy-done.4 = bf16[4,512,4096]{2,1,0:T(8,128)(2,1)S(1)} copy-done((bf16[4,512,4096]{2,1,0:T(8,128)(2,1)S(1)}, bf16[4,512,4096]{2,1,0:T(8,128)(2,1)}, u32[]{:S(2)}) %copy-start.4) | copy-done | bytes 16777240
  262.0 11.0 %all_to_all.83 = bf16[16,32,256]{2,1,0:T(8,128)(2,1)S(1)} all-to-all(bf16[16,32,256]{2,1,0:T(8,128)(2,1)S(1)} %up_rest.13), channel_id=1, replica_groups=mesh['sweep'=8,'layer'=16] {'layer'}, dimensions={0} | all-to-all | bytes 524288 | tf_op jit(solution)/shard_map/all_to_all | solution.py:246
  (124 shorter events, 61.8 us)
Async XLA Ops:
  3.9 5.9 %collective-permute-start.1 = (f32[32,512]{1,0:T(8,128)S(1)}, f32[32,512]{1,0:T(8,128)S(1)}, u32[]{:S(2)}, u32[]{:S(2)}) collective-permute-start(f32[32,512]{1,0:T(8,128)S(1)} %bitcast.20), channel_id=1, source_target_pairs={{0,16},{16,0},{32,48},{48,32},{64,80},{80,64},{96,112},{112,96},{1... | collective-permute-start | bytes 196616 | tf_op jit(solution)/shard_map/ppermute | solution.py:237
  5.4 4.4 %collective-permute-start = (f32[32,256]{1,0:T(8,128)S(1)}, f32[32,256]{1,0:T(8,128)S(1)}, u32[]{:S(2)}, u32[]{:S(2)}) collective-permute-start(f32[32,256]{1,0:T(8,128)S(1)} %slice.38), channel_id=1, source_target_pairs={{0,16},{16,0},{32,48},{48,32},{64,80},{80,64},{96,112},{112,96},{1... | collective-permute-start | bytes 98312 | tf_op jit(solution)/shard_map/ppermute | solution.py:237
  5.5 18.8 %collective-permute-start.2 = (bf16[2,512,2048]{2,1,0:T(8,128)(2,1)}, bf16[2,512,2048]{2,1,0:T(8,128)(2,1)}, u32[]{:S(2)}, u32[]{:S(2)}) collective-permute-start(bf16[2,512,2048]{2,1,0:T(8,128)(2,1)} %second_halves.2), channel_id=1, source_target_pairs={{0,16},{16,0},{32,48},{48,32},{64,80},{80,64},{96,112},{112,96},{1... | collective-permute-start | bytes 12582920 | tf_op jit(solution)/shard_map/ppermute | solution.py:237
  9.8 14.5 %collective-permute-start.3 = (bf16[2,512,2048]{2,1,0:T(8,128)(2,1)}, bf16[2,512,2048]{2,1,0:T(8,128)(2,1)}, u32[]{:S(2)}, u32[]{:S(2)}) collective-permute-start(bf16[2,512,2048]{2,1,0:T(8,128)(2,1)} %second_halves.3), channel_id=1, source_target_pairs={{0,16},{16,0},{32,48},{48,32},{64,80},{80,64},{96,112},{112,96},{1... | collective-permute-start | bytes 12582920 | tf_op jit(solution)/shard_map/ppermute | solution.py:237
  28.5 6.7 %collective-permute-start.4 = (f32[32,256]{1,0:T(8,128)S(1)}, f32[32,256]{1,0:T(8,128)S(1)}, u32[]{:S(2)}, u32[]{:S(2)}) collective-permute-start(f32[32,256]{1,0:T(8,128)S(1)} %get-tuple-element.52), channel_id=1, source_target_pairs={{0,32},{16,48},{1,33},{17,49},{2,34},{18,50},{3,35},{19,51},{4,36}... | collective-permute-start | bytes 98312 | tf_op jit(solution)/shard_map/ppermute | solution.py:240
  32.1 4.1 %collective-permute-start.5 = (f32[32,256]{1,0:T(8,128)S(1)}, f32[32,256]{1,0:T(8,128)S(1)}, u32[]{:S(2)}, u32[]{:S(2)}) collective-permute-start(f32[32,256]{1,0:T(8,128)S(1)} %get-tuple-element.53), channel_id=1, source_target_pairs={{0,48},{16,32},{1,49},{17,33},{2,50},{18,34},{3,51},{19,35},{4,52}... | collective-permute-start | bytes 98312 | tf_op jit(solution)/shard_map/ppermute | solution.py:243
  51.0 3.2 %collective-permute-start.6 = (f32[32,256]{1,0:T(8,128)S(1)}, f32[32,256]{1,0:T(8,128)S(1)}, u32[]{:S(2)}, u32[]{:S(2)}) collective-permute-start(f32[32,256]{1,0:T(8,128)S(1)} %get-tuple-element.55), channel_id=1, source_target_pairs={{0,16},{16,0},{32,48},{48,32},{64,80},{80,64},{96,112},{112,96},{1... | collective-permute-start | bytes 98312 | tf_op jit(solution)/shard_map/ppermute | solution.py:237
  66.4 2.7 collective-permute-start.7
  80.8 3.9 %collective-permute-start.9 = (f32[32,256]{1,0:T(8,128)S(1)}, f32[32,256]{1,0:T(8,128)S(1)}, u32[]{:S(2)}, u32[]{:S(2)}) collective-permute-start(f32[32,256]{1,0:T(8,128)S(1)} %turned_theirs.4), channel_id=1, source_target_pairs={{0,16},{16,0},{32,48},{48,32},{64,80},{80,64},{96,112},{112,96},{1... | collective-permute-start | bytes 98312 | tf_op jit(solution)/shard_map/ppermute | solution.py:237
  96.3 2.2 collective-permute-start.10
  110.2 3.9 %collective-permute-start.12 = (f32[32,256]{1,0:T(8,128)S(1)}, f32[32,256]{1,0:T(8,128)S(1)}, u32[]{:S(2)}, u32[]{:S(2)}) collective-permute-start(f32[32,256]{1,0:T(8,128)S(1)} %turned_theirs.6), channel_id=1, source_target_pairs={{0,16},{16,0},{32,48},{48,32},{64,80},{80,64},{96,112},{112,96},{1... | collective-permute-start | bytes 98312 | tf_op jit(solution)/shard_map/ppermute | solution.py:237
  126.7 2.8 %collective-permute-start.14 = (f32[32,256]{1,0:T(8,128)S(1)}, f32[32,256]{1,0:T(8,128)S(1)}, u32[]{:S(2)}, u32[]{:S(2)}) collective-permute-start(f32[32,256]{1,0:T(8,128)S(1)} %get-tuple-element.60), channel_id=1, source_target_pairs={{0,16},{16,0},{32,48},{48,32},{64,80},{80,64},{96,112},{112,96},{1... | collective-permute-start | bytes 98312 | tf_op jit(solution)/shard_map/ppermute | solution.py:237
  128.6 1.2 collective-permute-start.13
  129.8 7.7 %collective-permute-start.15 = (f32[32,256]{1,0:T(8,128)S(1)}, f32[32,256]{1,0:T(8,128)S(1)}, u32[]{:S(2)}, u32[]{:S(2)}) collective-permute-start(f32[32,256]{1,0:T(8,128)S(1)} %get-tuple-element.67), channel_id=1, source_target_pairs={{0,16},{16,0},{32,48},{48,32},{64,80},{80,64},{96,112},{112,96},{1... | collective-permute-start | bytes 98312 | tf_op jit(solution)/shard_map/ppermute | solution.py:237
  148.3 1.3 collective-permute-start.17
  149.0 1.5 collective-permute-start.16
  162.3 9.8 %collective-permute-start.18 = (bf16[32,256]{1,0:T(8,128)(2,1)S(1)}, bf16[32,256]{1,0:T(8,128)(2,1)S(1)}, u32[]{:S(2)}, u32[]{:S(2)}) collective-permute-start(bf16[32,256]{1,0:T(8,128)(2,1)S(1)} %add_convert_fusion.7.x_ref), channel_id=1, source_target_pairs={{0,16},{16,0},{32,48},{48,32},{64,80},{80,64},{96,112},{112,96},{1... | collective-permute-start | bytes 49160 | tf_op jit(solution)/shard_map/ppermute | solution.py:237
  184.0 1.3 collective-permute-start.20
  184.7 1.5 collective-permute-start.19
  198.2 9.2 %collective-permute-start.21 = (bf16[32,256]{1,0:T(8,128)(2,1)S(1)}, bf16[32,256]{1,0:T(8,128)(2,1)S(1)}, u32[]{:S(2)}, u32[]{:S(2)}) collective-permute-start(bf16[32,256]{1,0:T(8,128)(2,1)S(1)} %add_convert_fusion.5.x_ref), channel_id=1, source_target_pairs={{0,16},{16,0},{32,48},{48,32},{64,80},{80,64},{96,112},{112,96},{1... | collective-permute-start | bytes 49160 | tf_op jit(solution)/shard_map/ppermute | solution.py:237
  219.2 18.6 %collective-permute-start.23 = (bf16[32,256]{1,0:T(8,128)(2,1)S(1)}, bf16[32,256]{1,0:T(8,128)(2,1)S(1)}, u32[]{:S(2)}, u32[]{:S(2)}) collective-permute-start(bf16[32,256]{1,0:T(8,128)(2,1)S(1)} %add_convert_fusion.4), channel_id=1, source_target_pairs={{32,0},{48,16},{33,1},{49,17},{34,2},{50,18},{35,3},{51,19},{36,4}... | collective-permute-start | bytes 49160 | tf_op jit(solution)/shard_map/ppermute | solution.py:240
  220.6 20.4 %collective-permute-start.22 = (bf16[32,256]{1,0:T(8,128)(2,1)S(1)}, bf16[32,256]{1,0:T(8,128)(2,1)S(1)}, u32[]{:S(2)}, u32[]{:S(2)}) collective-permute-start(bf16[32,256]{1,0:T(8,128)(2,1)S(1)} %add_convert_fusion.4), channel_id=1, source_target_pairs={{32,16},{48,0},{33,17},{49,1},{34,18},{50,2},{35,19},{51,3},{36,20... | collective-permute-start | bytes 49160 | tf_op jit(solution)/shard_map/ppermute | solution.py:243
  252.6 8.6 %collective-permute-start.24 = (bf16[32,256]{1,0:T(8,128)(2,1)S(1)}, bf16[32,256]{1,0:T(8,128)(2,1)S(1)}, u32[]{:S(2)}, u32[]{:S(2)}) collective-permute-start(bf16[32,256]{1,0:T(8,128)(2,1)S(1)} %add_convert_fusion.3.x_ref), channel_id=1, source_target_pairs={{0,16},{16,0},{32,48},{48,32},{64,80},{80,64},{96,112},{112,96},{1... | collective-permute-start | bytes 49160 | tf_op jit(solution)/shard_map/ppermute | solution.py:237
  273.1 2.6 collective-permute-start.25
  (9 other events, 96.0 us)

commit v10 on v8

--- a/solution.py
+++ b/solution.py
@@ -283,7 +283,7 @@
     late = 4
     for p in range(planes):
         if p > 0:
-            blocks = spread(hop(mine, p - 1, p) + hop_across(theirs, p - 1, p))
+            blocks = spread(hop((mine + swap(theirs)).astype(BF16), p - 1, p))
             if p == 1:
                 mine, theirs, matrix_a = load_product(
                     me, 0, late, matrix, received, blocks, base_a

time: 254 us -> 253 us (level)
    ppermute x6 -> x3, starting transfers between devices: 7.06 us -> 2.62 us  [hop_across(): lax.ppermute(x, 'sweep', [(2 * a + c, 2 * b + 1 - c) for c in range(2)])]
    ppermute x14 -> x17, starting transfers between devices: 22.9 us -> 27.1 us  [swap(): return lax.ppermute(x, 'sweep', [(i, i ^ 1) for i in range(2 * planes)])]
  transfers between devices with their start and end apart: 26 -> 26, of which waited for: 10 -> 12; matrix products, arithmetic and copies ran while one was open for 0% -> 0% of each run, Pallas kernels for 5% -> 5%
where the time goes in v10:
time: 253 us; the launch traced here: 252 us
  blocking collectives  154 us (61%)
  starting transfers between devices  37.2 us (15%)
  Pallas kernels  36.7 us (15%)
  waiting for transfers between devices  22.6 us (9%)
    all_to_all x14, blocking collectives, exchange(): return lax.all_to_all(blocks, 'layer', 0, 0, tiled=True)  154 us
    ppermute x17, starting transfers between devices, swap(): return lax.ppermute(x, 'sweep', [(i, i ^ 1) for i in range(2 * planes)])  27.1 us
    pallas_call x23, Pallas kernels, call(): pl.pallas_call(body, in_specs=[VMEM] * len(args), out_specs=jax.tree.map(...  20.5 us
    ppermute x6, waiting for transfers between devices, hop(): return lax.ppermute(x, 'sweep', [(2 * a + c, 2 * b + c) for c in range(2)])  15.2 us
    pallas_call x2, Pallas kernels, load_product(): pl.pallas_call(body, in_specs=[SMEM, HBM, *[HBM] * pieces, VMEM, VMEM], o...  8.43 us
    pallas_call x2, Pallas kernels, second_halves(): pl.pallas_call(body, in_specs=[HBM], out_specs=HBM, out_shape=pltpu.HBM((...  7.75 us
    ppermute x6, starting transfers between devices, hop(): return lax.ppermute(x, 'sweep', [(2 * a + c, 2 * b + c) for c in range(2)])  7.46 us
  transfers between devices with their start and end apart: 26, of which 12 were waited for; matrix products, arithmetic and copies ran while one was open for 0% of the time, Pallas kernels for 5%

profile of v10, /device:TPU:1, one launch (start us, length us, event | category | flops | bytes accessed | tf_op | source)
XLA Modules:
  0.0 252.1 jit_solution(6431401288849985016)
XLA Ops:
  0.0 3.9 %second_halves.2 = bf16[2,512,2048]{2,1,0:T(8,128)(2,1)} custom-call(bf16[2,512,8192]{2,1,0:T(8,128)(2,1)} %bitcast.16), custom_call_target="tpu_custom_call" | custom-call | tf_op jit(solution)/shard_map/second_halves/pallas_call | solution.py:56
  5.9 3.8 %second_halves.3 = bf16[2,512,2048]{2,1,0:T(8,128)(2,1)} custom-call(bf16[2,512,8192]{2,1,0:T(8,128)(2,1)} %bitcast.17), custom_call_target="tpu_custom_call" | custom-call | tf_op jit(solution)/shard_map/second_halves/pallas_call | solution.py:56
  10.1 14.2 %all_to_all.70.refs_2_ = bf16[16,32,256]{2,1,0:T(8,128)(2,1)S(1)} all-to-all(bf16[16,32,256]{2,1,0:T(8,128)(2,1)S(1)} %broadcast_in_dim.21), channel_id=1, replica_groups=mesh['sweep'=8,'layer'=16] {'layer'}, dimensions={0} | all-to-all | bytes 524288 | tf_op jit(solution)/shard_map/all_to_all | solution.py:237
  24.3 4.2 %load_product.2 = (f32[32,256]{1,0:T(8,128)S(1)}, f32[32,256]{1,0:T(8,128)S(1)}, bf16[4,512,4096]{2,1,0:T(8,128)(2,1)S(1)}) custom-call(s32[1]{0:T(128)} %bitcast.me_ref, bf16[2,512,8192]{2,1,0:T(8,128)(2,1)} %bitcast.18, bf16[2,512,2048]{2,1,0:T(8,128)(2,1)} %collective-permute-done.2.refs_0_, bf16[2,512,2048]{2,1,0:T(8,128)(2,1)} %collective-permute-done.3.refs_1_, ...), custom_call_target="tpu_custom_call" | custom-call | flops 536870912 | bytes 8388608 | tf_op jit(solution)/shard_map/load_product/pallas_call | solution.py:125
  31.4 3.5 %collective-permute-start.5 = (bf16[32,256]{1,0:T(8,128)(2,1)S(1)}, bf16[32,256]{1,0:T(8,128)(2,1)S(1)}, u32[]{:S(2)}, u32[]{:S(2)}) collective-permute-start(bf16[32,256]{1,0:T(8,128)(2,1)S(1)} %add_convert_fusion.2), channel_id=1, source_target_pairs={{0,32},{16,48},{1,33},{17,49},{2,34},{18,50},{3,35},{19,51},{4,36}... | collective-permute-start | bytes 49160 | tf_op jit(solution)/shard_map/ppermute | solution.py:231
  35.8 10.5 %all_to_all.71.refs_2_ = bf16[16,32,256]{2,1,0:T(8,128)(2,1)S(1)} all-to-all(bf16[16,32,256]{2,1,0:T(8,128)(2,1)S(1)} %broadcast_in_dim.22), channel_id=1, replica_groups=mesh['sweep'=8,'layer'=16] {'layer'}, dimensions={0} | all-to-all | bytes 524288 | tf_op jit(solution)/shard_map/all_to_all | solution.py:237
  46.3 4.2 %load_product.3 = (f32[32,256]{1,0:T(8,128)S(1)}, f32[32,256]{1,0:T(8,128)S(1)}, bf16[4,512,4096]{2,1,0:T(8,128)(2,1)S(1)}) custom-call(s32[1]{0:T(128)} %bitcast.me_ref, bf16[2,512,8192]{2,1,0:T(8,128)(2,1)} %bitcast.19, bf16[2,512,2048]{2,1,0:T(8,128)(2,1)} %collective-permute-done.2.refs_0_, bf16[2,512,2048]{2,1,0:T(8,128)(2,1)} %collective-permute-done.3.refs_1_, ...), custom_call_target="tpu_custom_call" | custom-call | flops 536870912 | bytes 8388608 | tf_op jit(solution)/shard_map/load_product/pallas_call | solution.py:125
  50.5 2.8 %collective-permute-start.6 = (f32[32,256]{1,0:T(8,128)S(1)}, f32[32,256]{1,0:T(8,128)S(1)}, u32[]{:S(2)}, u32[]{:S(2)}) collective-permute-start(f32[32,256]{1,0:T(8,128)S(1)} %get-tuple-element.57), channel_id=1, source_target_pairs={{0,16},{16,0},{32,48},{48,32},{64,80},{80,64},{96,112},{112,96},{1... | collective-permute-start | bytes 98312 | tf_op jit(solution)/shard_map/ppermute | solution.py:228
  54.2 10.7 %all_to_all.72.x_ref = bf16[16,32,256]{2,1,0:T(8,128)(2,1)S(1)} all-to-all(bf16[16,32,256]{2,1,0:T(8,128)(2,1)S(1)} %broadcast_in_dim.23), channel_id=1, replica_groups=mesh['sweep'=8,'layer'=16] {'layer'}, dimensions={0} | all-to-all | bytes 524288 | tf_op jit(solution)/shard_map/all_to_all | solution.py:237
  70.9 10.7 %all_to_all.73.x_ref = bf16[16,32,256]{2,1,0:T(8,128)(2,1)S(1)} all-to-all(bf16[16,32,256]{2,1,0:T(8,128)(2,1)S(1)} %broadcast_in_dim.24), channel_id=1, replica_groups=mesh['sweep'=8,'layer'=16] {'layer'}, dimensions={0} | all-to-all | bytes 524288 | tf_op jit(solution)/shard_map/all_to_all | solution.py:237
  85.3 10.7 %all_to_all.74.x_ref = bf16[16,32,256]{2,1,0:T(8,128)(2,1)S(1)} all-to-all(bf16[16,32,256]{2,1,0:T(8,128)(2,1)S(1)} %broadcast_in_dim.25), channel_id=1, replica_groups=mesh['sweep'=8,'layer'=16] {'layer'}, dimensions={0} | all-to-all | bytes 524288 | tf_op jit(solution)/shard_map/all_to_all | solution.py:237
  100.4 10.7 %all_to_all.75.x_ref = bf16[16,32,256]{2,1,0:T(8,128)(2,1)S(1)} all-to-all(bf16[16,32,256]{2,1,0:T(8,128)(2,1)S(1)} %broadcast_in_dim.26), channel_id=1, replica_groups=mesh['sweep'=8,'layer'=16] {'layer'}, dimensions={0} | all-to-all | bytes 524288 | tf_op jit(solution)/shard_map/all_to_all | solution.py:237
  114.8 10.7 %all_to_all.76.x_ref = bf16[16,32,256]{2,1,0:T(8,128)(2,1)S(1)} all-to-all(bf16[16,32,256]{2,1,0:T(8,128)(2,1)S(1)} %broadcast_in_dim.27), channel_id=1, replica_groups=mesh['sweep'=8,'layer'=16] {'layer'}, dimensions={0} | all-to-all | bytes 524288 | tf_op jit(solution)/shard_map/all_to_all | solution.py:237
  132.4 10.7 %all_to_all.77 = bf16[16,32,256]{2,1,0:T(8,128)(2,1)S(1)} all-to-all(bf16[16,32,256]{2,1,0:T(8,128)(2,1)S(1)} %up_rest.7), channel_id=1, replica_groups=mesh['sweep'=8,'layer'=16] {'layer'}, dimensions={0} | all-to-all | bytes 524288 | tf_op jit(solution)/shard_map/all_to_all | solution.py:237
  146.2 10.9 %all_to_all.78 = bf16[16,32,256]{2,1,0:T(8,128)(2,1)S(1)} all-to-all(bf16[16,32,256]{2,1,0:T(8,128)(2,1)S(1)} %up_rest.8), channel_id=1, replica_groups=mesh['sweep'=8,'layer'=16] {'layer'}, dimensions={0} | all-to-all | bytes 524288 | tf_op jit(solution)/shard_map/all_to_all | solution.py:237
  157.1 3.2 %collective-permute-start.18 = (bf16[32,256]{1,0:T(8,128)(2,1)S(1)}, bf16[32,256]{1,0:T(8,128)(2,1)S(1)}, u32[]{:S(2)}, u32[]{:S(2)}) collective-permute-start(bf16[32,256]{1,0:T(8,128)(2,1)S(1)} %add_convert_fusion.7.x_ref), channel_id=1, source_target_pairs={{0,16},{16,0},{32,48},{48,32},{64,80},{80,64},{96,112},{112,96},{1... | collective-permute-start | bytes 49160 | tf_op jit(solution)/shard_map/ppermute | solution.py:228
  162.0 10.8 %all_to_all.79 = bf16[16,32,256]{2,1,0:T(8,128)(2,1)S(1)} all-to-all(bf16[16,32,256]{2,1,0:T(8,128)(2,1)S(1)} %up_rest.9), channel_id=1, replica_groups=mesh['sweep'=8,'layer'=16] {'layer'}, dimensions={0} | all-to-all | bytes 524288 | tf_op jit(solution)/shard_map/all_to_all | solution.py:237
  175.8 10.9 %all_to_all.80 = bf16[16,32,256]{2,1,0:T(8,128)(2,1)S(1)} all-to-all(bf16[16,32,256]{2,1,0:T(8,128)(2,1)S(1)} %up_rest.10), channel_id=1, replica_groups=mesh['sweep'=8,'layer'=16] {'layer'}, dimensions={0} | all-to-all | bytes 524288 | tf_op jit(solution)/shard_map/all_to_all | solution.py:237
  186.8 3.0 %collective-permute-start.21 = (bf16[32,256]{1,0:T(8,128)(2,1)S(1)}, bf16[32,256]{1,0:T(8,128)(2,1)S(1)}, u32[]{:S(2)}, u32[]{:S(2)}) collective-permute-start(bf16[32,256]{1,0:T(8,128)(2,1)S(1)} %add_convert_fusion.5.x_ref), channel_id=1, source_target_pairs={{0,16},{16,0},{32,48},{48,32},{64,80},{80,64},{96,112},{112,96},{1... | collective-permute-start | bytes 49160 | tf_op jit(solution)/shard_map/ppermute | solution.py:228
  191.4 10.8 %all_to_all.81 = bf16[16,32,256]{2,1,0:T(8,128)(2,1)S(1)} all-to-all(bf16[16,32,256]{2,1,0:T(8,128)(2,1)S(1)} %up_rest.11), channel_id=1, replica_groups=mesh['sweep'=8,'layer'=16] {'layer'}, dimensions={0} | all-to-all | bytes 524288 | tf_op jit(solution)/shard_map/all_to_all | solution.py:237
  204.9 14.3 %collective-permute-done.23.x_ref = bf16[32,256]{1,0:T(8,128)(2,1)S(1)} collective-permute-done((bf16[32,256]{1,0:T(8,128)(2,1)S(1)}, bf16[32,256]{1,0:T(8,128)(2,1)S(1)}, u32[]{:S(2)}, u32[]{:S(2)}) %collective-permute-start.23) | collective-permute-done | bytes 16416 | tf_op jit(solution)/shard_map/ppermute | solution.py:231
  220.0 2.6 %collective-permute-done.22.x_ref = bf16[32,256]{1,0:T(8,128)(2,1)S(1)} collective-permute-done((bf16[32,256]{1,0:T(8,128)(2,1)S(1)}, bf16[32,256]{1,0:T(8,128)(2,1)S(1)}, u32[]{:S(2)}, u32[]{:S(2)}) %collective-permute-start.22) | collective-permute-done | bytes 16416 | tf_op jit(solution)/shard_map/ppermute | solution.py:234
  223.4 10.9 %all_to_all.82 = bf16[16,32,256]{2,1,0:T(8,128)(2,1)S(1)} all-to-all(bf16[16,32,256]{2,1,0:T(8,128)(2,1)S(1)} %up_rest.12), channel_id=1, replica_groups=mesh['sweep'=8,'layer'=16] {'layer'}, dimensions={0} | all-to-all | bytes 524288 | tf_op jit(solution)/shard_map/all_to_all | solution.py:237
  237.8 10.7 %all_to_all.83 = bf16[16,32,256]{2,1,0:T(8,128)(2,1)S(1)} all-to-all(bf16[16,32,256]{2,1,0:T(8,128)(2,1)S(1)} %up_rest.13), channel_id=1, replica_groups=mesh['sweep'=8,'layer'=16] {'layer'}, dimensions={0} | all-to-all | bytes 524288 | tf_op jit(solution)/shard_map/all_to_all | solution.py:237
  (113 shorter events, 52.1 us)
Async XLA Ops:
  3.9 5.9 %collective-permute-start.1 = (f32[32,512]{1,0:T(8,128)S(1)}, f32[32,512]{1,0:T(8,128)S(1)}, u32[]{:S(2)}, u32[]{:S(2)}) collective-permute-start(f32[32,512]{1,0:T(8,128)S(1)} %bitcast.20), channel_id=1, source_target_pairs={{0,16},{16,0},{32,48},{48,32},{64,80},{80,64},{96,112},{112,96},{1... | collective-permute-start | bytes 196616 | tf_op jit(solution)/shard_map/ppermute | solution.py:228
  5.4 4.4 %collective-permute-start = (f32[32,256]{1,0:T(8,128)S(1)}, f32[32,256]{1,0:T(8,128)S(1)}, u32[]{:S(2)}, u32[]{:S(2)}) collective-permute-start(f32[32,256]{1,0:T(8,128)S(1)} %slice.38), channel_id=1, source_target_pairs={{0,16},{16,0},{32,48},{48,32},{64,80},{80,64},{96,112},{112,96},{1... | collective-permute-start | bytes 98312 | tf_op jit(solution)/shard_map/ppermute | solution.py:228
  5.5 18.8 %collective-permute-start.2 = (bf16[2,512,2048]{2,1,0:T(8,128)(2,1)}, bf16[2,512,2048]{2,1,0:T(8,128)(2,1)}, u32[]{:S(2)}, u32[]{:S(2)}) collective-permute-start(bf16[2,512,2048]{2,1,0:T(8,128)(2,1)} %second_halves.2), channel_id=1, source_target_pairs={{0,16},{16,0},{32,48},{48,32},{64,80},{80,64},{96,112},{112,96},{1... | collective-permute-start | bytes 12582920 | tf_op jit(solution)/shard_map/ppermute | solution.py:228
  9.8 14.5 %collective-permute-start.3 = (bf16[2,512,2048]{2,1,0:T(8,128)(2,1)}, bf16[2,512,2048]{2,1,0:T(8,128)(2,1)}, u32[]{:S(2)}, u32[]{:S(2)}) collective-permute-start(bf16[2,512,2048]{2,1,0:T(8,128)(2,1)} %second_halves.3), channel_id=1, source_target_pairs={{0,16},{16,0},{32,48},{48,32},{64,80},{80,64},{96,112},{112,96},{1... | collective-permute-start | bytes 12582920 | tf_op jit(solution)/shard_map/ppermute | solution.py:228
  28.5 2.9 %collective-permute-start.4 = (f32[32,256]{1,0:T(8,128)S(1)}, f32[32,256]{1,0:T(8,128)S(1)}, u32[]{:S(2)}, u32[]{:S(2)}) collective-permute-start(f32[32,256]{1,0:T(8,128)S(1)} %get-tuple-element.55), channel_id=1, source_target_pairs={{0,16},{16,0},{32,48},{48,32},{64,80},{80,64},{96,112},{112,96},{1... | collective-permute-start | bytes 98312 | tf_op jit(solution)/shard_map/ppermute | solution.py:228
  31.4 4.4 %collective-permute-start.5 = (bf16[32,256]{1,0:T(8,128)(2,1)S(1)}, bf16[32,256]{1,0:T(8,128)(2,1)S(1)}, u32[]{:S(2)}, u32[]{:S(2)}) collective-permute-start(bf16[32,256]{1,0:T(8,128)(2,1)S(1)} %add_convert_fusion.2), channel_id=1, source_target_pairs={{0,32},{16,48},{1,33},{17,49},{2,34},{18,50},{3,35},{19,51},{4,36}... | collective-permute-start | bytes 49160 | tf_op jit(solution)/shard_map/ppermute | solution.py:231
  50.5 3.6 %collective-permute-start.6 = (f32[32,256]{1,0:T(8,128)S(1)}, f32[32,256]{1,0:T(8,128)S(1)}, u32[]{:S(2)}, u32[]{:S(2)}) collective-permute-start(f32[32,256]{1,0:T(8,128)S(1)} %get-tuple-element.57), channel_id=1, source_target_pairs={{0,16},{16,0},{32,48},{48,32},{64,80},{80,64},{96,112},{112,96},{1... | collective-permute-start | bytes 98312 | tf_op jit(solution)/shard_map/ppermute | solution.py:228
  67.4 2.8 %collective-permute-start.7 = (f32[32,256]{1,0:T(8,128)S(1)}, f32[32,256]{1,0:T(8,128)S(1)}, u32[]{:S(2)}, u32[]{:S(2)}) collective-permute-start(f32[32,256]{1,0:T(8,128)S(1)} %get-tuple-element.60), channel_id=1, source_target_pairs={{0,16},{16,0},{32,48},{48,32},{64,80},{80,64},{96,112},{112,96},{1... | collective-permute-start | bytes 98312 | tf_op jit(solution)/shard_map/ppermute | solution.py:228
  82.5 2.8 %collective-permute-start.9 = (f32[32,256]{1,0:T(8,128)S(1)}, f32[32,256]{1,0:T(8,128)S(1)}, u32[]{:S(2)}, u32[]{:S(2)}) collective-permute-start(f32[32,256]{1,0:T(8,128)S(1)} %turned_theirs.4), channel_id=1, source_target_pairs={{0,16},{16,0},{32,48},{48,32},{64,80},{80,64},{96,112},{112,96},{1... | collective-permute-start | bytes 98312 | tf_op jit(solution)/shard_map/ppermute | solution.py:228
  96.9 2.8 %collective-permute-start.10 = (f32[32,256]{1,0:T(8,128)S(1)}, f32[32,256]{1,0:T(8,128)S(1)}, u32[]{:S(2)}, u32[]{:S(2)}) collective-permute-start(f32[32,256]{1,0:T(8,128)S(1)} %turned_theirs.5), channel_id=1, source_target_pairs={{0,16},{16,0},{32,48},{48,32},{64,80},{80,64},{96,112},{112,96},{1... | collective-permute-start | bytes 98312 | tf_op jit(solution)/shard_map/ppermute | solution.py:228
  111.9 2.8 %collective-permute-start.12 = (f32[32,256]{1,0:T(8,128)S(1)}, f32[32,256]{1,0:T(8,128)S(1)}, u32[]{:S(2)}, u32[]{:S(2)}) collective-permute-start(f32[32,256]{1,0:T(8,128)S(1)} %turned_theirs.6), channel_id=1, source_target_pairs={{0,16},{16,0},{32,48},{48,32},{64,80},{80,64},{96,112},{112,96},{1... | collective-permute-start | bytes 98312 | tf_op jit(solution)/shard_map/ppermute | solution.py:228
  127.2 2.8 %collective-permute-start.14 = (f32[32,256]{1,0:T(8,128)S(1)}, f32[32,256]{1,0:T(8,128)S(1)}, u32[]{:S(2)}, u32[]{:S(2)}) collective-permute-start(f32[32,256]{1,0:T(8,128)S(1)} %get-tuple-element.64), channel_id=1, source_target_pairs={{0,16},{16,0},{32,48},{48,32},{64,80},{80,64},{96,112},{112,96},{1... | collective-permute-start | bytes 98312 | tf_op jit(solution)/shard_map/ppermute | solution.py:228
  129.2 1.2 collective-permute-start.13
  130.4 1.9 collective-permute-start.15
  143.1 1.3 collective-permute-start.17
  143.8 1.5 collective-permute-start.16
  157.1 4.1 %collective-permute-start.18 = (bf16[32,256]{1,0:T(8,128)(2,1)S(1)}, bf16[32,256]{1,0:T(8,128)(2,1)S(1)}, u32[]{:S(2)}, u32[]{:S(2)}) collective-permute-start(bf16[32,256]{1,0:T(8,128)(2,1)S(1)} %add_convert_fusion.7.x_ref), channel_id=1, source_target_pairs={{0,16},{16,0},{32,48},{48,32},{64,80},{80,64},{96,112},{112,96},{1... | collective-permute-start | bytes 49160 | tf_op jit(solution)/shard_map/ppermute | solution.py:228
  172.8 1.3 collective-permute-start.20
  173.5 1.5 collective-permute-start.19
  186.8 3.8 %collective-permute-start.21 = (bf16[32,256]{1,0:T(8,128)(2,1)S(1)}, bf16[32,256]{1,0:T(8,128)(2,1)S(1)}, u32[]{:S(2)}, u32[]{:S(2)}) collective-permute-start(bf16[32,256]{1,0:T(8,128)(2,1)S(1)} %add_convert_fusion.5.x_ref), channel_id=1, source_target_pairs={{0,16},{16,0},{32,48},{48,32},{64,80},{80,64},{96,112},{112,96},{1... | collective-permute-start | bytes 49160 | tf_op jit(solution)/shard_map/ppermute | solution.py:228
  202.3 16.9 %collective-permute-start.23 = (bf16[32,256]{1,0:T(8,128)(2,1)S(1)}, bf16[32,256]{1,0:T(8,128)(2,1)S(1)}, u32[]{:S(2)}, u32[]{:S(2)}) collective-permute-start(bf16[32,256]{1,0:T(8,128)(2,1)S(1)} %add_convert_fusion.4), channel_id=1, source_target_pairs={{32,0},{48,16},{33,1},{49,17},{34,2},{50,18},{35,3},{51,19},{36,4}... | collective-permute-start | bytes 49160 | tf_op jit(solution)/shard_map/ppermute | solution.py:231
  203.6 19.0 %collective-permute-start.22 = (bf16[32,256]{1,0:T(8,128)(2,1)S(1)}, bf16[32,256]{1,0:T(8,128)(2,1)S(1)}, u32[]{:S(2)}, u32[]{:S(2)}) collective-permute-start(bf16[32,256]{1,0:T(8,128)(2,1)S(1)} %add_convert_fusion.4), channel_id=1, source_target_pairs={{32,16},{48,0},{33,17},{49,1},{34,18},{50,2},{35,19},{51,3},{36,20... | collective-permute-start | bytes 49160 | tf_op jit(solution)/shard_map/ppermute | solution.py:234
  234.3 2.7 %collective-permute-start.24 = (bf16[32,256]{1,0:T(8,128)(2,1)S(1)}, bf16[32,256]{1,0:T(8,128)(2,1)S(1)}, u32[]{:S(2)}, u32[]{:S(2)}) collective-permute-start(bf16[32,256]{1,0:T(8,128)(2,1)S(1)} %add_convert_fusion.3.x_ref), channel_id=1, source_target_pairs={{0,16},{16,0},{32,48},{48,32},{64,80},{80,64},{96,112},{112,96},{1... | collective-permute-start | bytes 49160 | tf_op jit(solution)/shard_map/ppermute | solution.py:228
  248.6 2.8 %collective-permute-start.25 = (f32[32,256]{1,0:T(8,128)S(1)}, f32[32,256]{1,0:T(8,128)S(1)}, u32[]{:S(2)}, u32[]{:S(2)}) collective-permute-start(f32[32,256]{1,0:T(8,128)S(1)} %select_n.96), channel_id=1, source_target_pairs={{0,16},{16,0},{32,48},{48,32},{64,80},{80,64},{96,112},{112,96},{1... | collective-permute-start | bytes 98312 | tf_op jit(solution)/shard_map/ppermute | solution.py:228
  (4 other events, 10.7 us)
